TPU v7x, 128 devices: a whole 4x4x4 slice. The times are simulated.
128 devices in a mesh: row: 8 (over x, y_lo), col: 16 (over z, y_hi, core).
Axes of the slice: x: 4, y: 4 (y_hi: 2, y_lo: 2; y = y_hi * 2 + y_lo), z: 4, core: 2. Of those that a mesh axis runs over, the one named last changes fastest.
Arguments:
- density: bfloat16 [8192, 8192], P('row', 'col'), may hold values from -1.75 to 1.75
- pattern: int32 [64, 64], P('row', 'col'), may hold values from 0 to 1, as said below
- square_filter: int32 [64, 64], P('row', 'col'), may hold values from 0 to 1
- step_filter: int32 [64, 64], P('row', 'col'), may hold values from 0 to 1
Outputs:
- square: bfloat16 [8192, 8192], P('row', 'col')
- stepped: bfloat16 [8192, 8192], P('row', 'col')
Inputs may be any that keep to these rules, and one draw needn't show every extreme that they name: Atom blocks sit at positions on a cycle of length 256, block i at 4 p(i) plus 0 to 3, where p is a permutation of the 64 blocks; pattern keeps block pairs whose cycle distance is at most 32, square_filter those within 48, step_filter those within 40, all from the same positions.
All inputs are finite; a program needn't handle non-finite values.
Results may differ from a plain program's by a relative error of at most 0.0049.
Values may be sent and summed in bfloat16 or wider, within the bound.
No kernel may reach another device: no remote copies, remote signals or barrier semaphores. Data moves between devices by JAX's collectives and lax.ppermute only.
A program may use at most 128 MiB of HBM per device.

v0:
```python
import jax
import jax.numpy as jnp
from jax import lax
from jax.sharding import PartitionSpec as P

BLOCK = 128


def expand(values, mask):
    rows, cols = values.shape
    shaped = values.reshape(rows // BLOCK, BLOCK, cols // BLOCK, BLOCK)
    return (shaped * mask[:, None, :, None].astype(values.dtype)).reshape(rows, cols)


def right_folder(columns, piece):
    return jnp.dot(piece, columns, preferred_element_type=jnp.float32)


def on_device(density, pattern, square_filter, step_filter):
    masked = expand(density, pattern)
    columns = lax.all_gather(masked, "row", axis=0, tiled=True)
    product = right_folder(columns, lax.all_gather(masked, "col", axis=1, tiled=True))
    square = expand(product, square_filter).astype(jnp.bfloat16)
    square_cols = lax.all_gather(square, "row", axis=0, tiled=True)
    second = right_folder(square_cols, lax.all_gather(masked, "col", axis=1, tiled=True))
    stepped = 1.5 * masked.astype(jnp.float32) - 0.5 * second
    stepped = expand(stepped, step_filter).astype(jnp.bfloat16)
    return (square, stepped)


def solution(mesh):
    placed = (P("row", "col"), P("row", "col"), P("row", "col"), P("row", "col"))
    return jax.shard_map(
        on_device,
        mesh=mesh,
        in_specs=placed,
        out_specs=(P("row", "col"), P("row", "col")),
        check_vma=False,
    )
```

profile of v0, /device:TPU:0, one launch (start us, length us, event | category | flops | bytes accessed | tf_op | source)
XLA Modules:
  0.0 513.1 jit_solution(10281734568358968585)
XLA Ops:
  7.2 0.0 all-gather.6.cloned.1.call-start
  7.2 0.7 convert_element_type.21
  7.9 0.1 copy.6
  8.0 0.3 mul.45
  8.3 0.0 copy-start.1
  8.4 2.3 bitcast_multiply_fusion.2
  10.7 0.0 all-gather.6.cloned.1.call-update
  10.7 0.0 all-gather.4.cloned.1.call-start
  10.8 0.7 all-gather.4.cloned.1.call-update
  11.5 0.0 all-gather.8.cloned.1.call-start
  11.5 0.0 copy-done.1
  11.5 0.1 copy.7
  11.6 170.1 %all-gather.6.cloned.1.call-done = bf16[8192,512]{1,0:T(8,128)(2,1)} async-done(((bf16[1024,512]{1,0:T(8,128)(2,1)}), bf16[8192,512]{1,0:T(8,128)(2,1)}) %all-gather.6.cloned.1.call-update) | async-done | bytes 8388624 | tf_op jit(solution)/shard_map/all_gather | solution.py:21
  181.7 127.4 %all-gather.4.cloned.1.call-done = bf16[1024,8192]{1,0:T(8,128)(2,1)} async-done(((bf16[1024,512]{1,0:T(8,128)(2,1)}), bf16[1024,8192]{1,0:T(8,128)(2,1)}) %all-gather.4.cloned.1.call-update) | async-done | bytes 16777232 | tf_op jit(solution)/shard_map/all_gather | solution.py:22
  309.2 0.3 mul.48
  309.5 0.0 copy-start.2
  309.5 15.6 %fusion.1 = bf16[1024,512]{1,0:T(8,128)(2,1)} fusion(f32[128,8,4,128]{3,2,1,0:T(4,128)S(1)} %bitcast.22, bf16[1024,8192]{1,0:T(8,128)(2,1)} %all-gather.4.cloned.1.call-done, bf16[8192,512]{1,0:T(8,128)(2,1)} %all-gather.6.cloned.1.call-done), kind=kOutput, calls=%fused_computation.3 | convolution fusion | flops 8590983168 | bytes 28311552 | tf_op jit(solution)/shard_map/dot_general | solution.py:16
  325.1 0.0 copy-start
  325.1 0.0 all-gather.8.cloned.1.call-update
  325.1 0.0 copy-done.2
  325.1 0.1 copy.8
  325.2 165.4 %all-gather.8.cloned.1.call-done = bf16[8192,512]{1,0:T(8,128)(2,1)} async-done(((bf16[1024,512]{1,0:T(8,128)(2,1)}), bf16[8192,512]{1,0:T(8,128)(2,1)}) %all-gather.8.cloned.1.call-update) | async-done | bytes 8388624 | tf_op jit(solution)/shard_map/all_gather | solution.py:24
  490.6 0.3 mul.55
  491.0 0.0 copy-done
  491.0 15.6 %fusion = bf16[1024,512]{1,0:T(8,128)(2,1)} fusion(f32[128,8,4,128]{3,2,1,0:T(4,128)S(1)} %bitcast.21, bf16[1024,512]{1,0:T(8,128)(2,1)S(1)} %copy-done, bf16[1024,8192]{1,0:T(8,128)(2,1)} %all-gather.4.cloned.1.call-done, bf16[8192,512]{1,0:T(8,128)(2,1)} %all-gather.8.cloned.1.call-done), kind=kOutput, calls=%fused_computation.1 | convolution fusion | flops 8593080320 | bytes 29360128 | tf_op jit(solution)/shard_map/dot_general | solution.py:16
  (2 shorter events, 0.0 us)
Async XLA Ops:
  7.2 174.6 %all-gather.6.cloned.1.call-start = ((), (), s32[]{:S(2)}) async-start(), calls=%async_computation.1 | async-start | bytes 9437184 | tf_op jit(solution)/shard_map/all_gather | solution.py:21
  8.3 3.2 copy-start.1
  10.7 298.5 %all-gather.4.cloned.1.call-start = ((), (), s32[]{:S(2)}) async-start(), calls=%async_computation | async-start | bytes 17825792 | tf_op jit(solution)/shard_map/all_gather | solution.py:22
  11.5 479.2 %all-gather.8.cloned.1.call-start = ((), (), s32[]{:S(2)}) async-start(), calls=%async_computation.2 | async-start | bytes 9437184 | tf_op jit(solution)/shard_map/all_gather | solution.py:24
  309.5 15.6 %copy-start.2 = (s32[8,4]{0,1:T(4,128)S(1)}, s32[8,4]{0,1:T(4,128)}, u32[]{:S(2)}) copy-start(s32[8,4]{0,1:T(4,128)} %param.7) | copy-start | bytes 388
  325.1 165.9 %copy-start = (bf16[1024,512]{1,0:T(8,128)(2,1)S(1)}, bf16[1024,512]{1,0:T(8,128)(2,1)}, u32[]{:S(2)}) copy-start(bf16[1024,512]{1,0:T(8,128)(2,1)} %bitcast_multiply_fusion.2) | copy-start | bytes 3145732
Sparse Core Ops, SparseCore 0:
  10.8 170.8 all-gather.5
  184.7 124.4 all-gather.3
  325.2 165.3 all-gather.7
where the time goes:
time: 518 us; the launch traced here: 513 us
  waiting for transfers between devices  464 us (90%)
  matrix products  31.2 us (6%)
  between operations  13.8 us (3%)
    all_gather x1, waiting for transfers between devices, on_device(): columns = lax.all_gather(masked, 'row', axis=0, tiled=True)  170 us
    all_gather x1, waiting for transfers between devices, on_device(): square_cols = lax.all_gather(square, 'row', axis=0, tiled=True)  165 us
    all_gather x1, waiting for transfers between devices, on_device(): lax.all_gather(masked, 'col', axis=1, tiled=True)  127 us
    dot_general x2, matrix products, right_folder(): return jnp.dot(piece, columns, preferred_element_type=jnp.float32)  31.2 us
  transfers between devices with their start and end apart: 3, of which 3 were waited for; matrix products, arithmetic and copies ran while one was open for 0% of the time, Pallas kernels for 0%

commit v1 on v0

v1 whole, which is shorter than its diff:
```python
import functools

import jax
import jax.numpy as jnp
from jax import lax
from jax.experimental import pallas as pl
from jax.experimental.pallas import tpu as pltpu
from jax.sharding import PartitionSpec as P

BLOCK = 128
NB = 64
TR = 8
TC = 16
SL = 16
KP, KS, KT = 17, 25, 21
SLOTS = KP + 1
PACK = 4 * SLOTS
ZERO = PACK - 1
NONE = NB
VMEM_LIMIT = 40 * 1024 * 1024
BF = jnp.bfloat16


def row_index(x, y):
    return (x % 4) * 2 + (y % 2)


def col_index(z, y, core):
    return (z % 4) * 4 + (y % 2) * 2 + (core % 2)


def row_shift(value, dx, dy):
    pairs = [(row_index(x, y), row_index(x + dx, y + dy)) for x in range(4) for y in range(2)]
    return lax.ppermute(value, "row", pairs)


def col_shift(value, dz, dy, dc):
    pairs = [
        (col_index(z, y, c), col_index(z + dz, y + dy, c + dc))
        for z in range(4)
        for y in range(2)
        for c in range(2)
    ]
    return lax.ppermute(value, "col", pairs)


def pack_kernel(place, sliced, packed, lists, flags, flags_s, sem):
    lane = lax.broadcasted_iota(jnp.int32, (8, BLOCK), 1)
    for s in range(TR):
        flags[8 * s : 8 * s + 8, :] = sliced[s, 8, :, 0:BLOCK].astype(jnp.float32)[0:8].astype(jnp.int32)
    copy = pltpu.make_async_copy(flags, flags_s, sem)
    copy.start()
    packed[...] = jnp.zeros_like(packed)
    for n in range(12):
        for t in range(32):
            lists[n, t] = NONE
    copy.wait()

    def kept(i, counts):
        out = []
        for n in range(4):
            lists[n, counts[n]] = i
            packed[n * SLOTS + counts[n]] = sliced[i // 8, i % 8, :, n * BLOCK : (n + 1) * BLOCK]
            out.append(counts[n] + flags_s[i, n])
        for n in range(4, 12):
            lists[n, counts[n]] = i
            out.append(counts[n] + flags_s[i, n])
        return tuple(out)

    counts = lax.fori_loop(0, NB, kept, (jnp.int32(0),) * 12, unroll=4)
    for n in range(12):
        lists[n, counts[n]] = NONE
    lane = lax.broadcasted_iota(jnp.int32, (SL, BLOCK), 1)
    heads = []
    for g in range(4):
        part = jnp.where(lane < 4, flags[SL * g : SL * (g + 1), :].astype(jnp.float32), 0.0)
        heads.append(pltpu.roll(part, place[1] * 4 + (g % 2) * NB, 1))
    packed[KP] = (heads[0] + heads[1]).astype(BF)
    packed[SLOTS + KP] = (heads[2] + heads[3]).astype(BF)
    packed[2 * SLOTS + KP] = jnp.zeros((SL, BLOCK), BF)
    packed[ZERO] = jnp.zeros((SL, BLOCK), BF)


def fetch_rows(place, parts, rows, sems):
    x, y = place[0] // 2, place[0] % 2
    copies = []
    for dx in range(4):
        for h in range(2):
            d = lax.rem(x - dx + 4, 4) * 2 + (y + h) % 2
            copies.append(pltpu.make_async_copy(parts[dx].at[h], rows.at[:, d], sems.at[2 * dx + h]))
    return copies


def fetch_cols(place, parts, cols, sems):
    z, y, core = place[1] // 4, (place[1] // 2) % 2, place[1] % 2
    copies = []
    for dc in range(2):
        for dz in range(4):
            for h in range(2):
                c = lax.rem(z - dz + 4, 4) * 4 + ((y + h) % 2) * 2 + (core + dc) % 2
                n = len(copies)
                copies.append(
                    pltpu.make_async_copy(parts[4 * dc + dz].at[h], cols.at[pl.ds(c * PACK, PACK)], sems.at[n])
                )
    return copies


def gather_left(table, outer, inner, cols, left, n_outer, n_inner):
    ks = [inner(t) for t in range(n_inner)]

    def one(s, carry):
        i = outer(s)
        at = pl.multiple_of(s * SL, SL)
        for t in range(n_inner):
            left[pl.ds(at, SL), t * BLOCK : (t + 1) * BLOCK] = cols[table[i, ks[t]]]
        return carry

    lax.fori_loop(0, n_outer, one, 0)


def square_kernel(place, lists, *refs):
    row_parts, col_parts = refs[:4], refs[4:12]
    square, table = refs[12:14]
    rows, cols, left, index, sems, sem = refs[14:]
    from_cols = fetch_cols(place, col_parts, cols, sems)
    from_rows = fetch_rows(place, row_parts, rows, sems.at[pl.ds(16, 8)])
    for copy in from_cols + from_rows:
        copy.start()
    for copy in from_cols:
        copy.wait()
    lane = lax.broadcasted_iota(jnp.int32, (SL, BLOCK), 1)
    heads = []
    for slot in (KP, SLOTS + KP):
        head = jnp.zeros((SL, BLOCK), jnp.float32)
        for c in range(TC):
            head = head + cols[c * PACK + slot].astype(jnp.float32)
        heads += [head, pltpu.roll(head, NB, 1)]
    kept = jnp.concatenate([jnp.where(lane < NB, head, 0.0) for head in heads], axis=0)
    before = lax.broadcasted_iota(jnp.int32, (NB, NB), 1) < lax.broadcasted_iota(jnp.int32, (NB, NB), 0)
    rank = jnp.dot(before.astype(jnp.float32).astype(BF), kept.astype(BF), preferred_element_type=jnp.float32)
    slot = lax.broadcasted_iota(jnp.int32, (NB, BLOCK), 1) * SLOTS + rank.astype(jnp.int32)
    index[0:NB, :] = jnp.where(kept > 0.5, slot, ZERO)
    index[NB : NB + 8, :] = jnp.full((8, BLOCK), ZERO, jnp.int32)
    copy = pltpu.make_async_copy(index, table, sem)
    copy.start()
    copy.wait()
    for copy in from_rows:
        copy.wait()
    for j in range(4):
        gather_left(table, lambda s: lists[4 + j, s], lambda t: lists[j, t], cols, left, KS, KP)
        right = rows[j * SLOTS : j * SLOTS + KP].reshape(KP * BLOCK, BLOCK)
        product = jnp.dot(left[...], right, preferred_element_type=jnp.float32)
        square[j * KS : (j + 1) * KS] = product.astype(BF).reshape(KS, SL, BLOCK)


def step_kernel(place, lists, table, *refs):
    row_parts, col_parts = refs[:4], refs[4:12]
    stepped = refs[12]
    rows, cols, left, own, sems = refs[13:]
    copies = fetch_cols(place, col_parts, cols, sems)
    copies += fetch_rows(place, row_parts, rows, sems.at[pl.ds(16, 8)])
    for copy in copies:
        copy.start()
    stepped[...] = jnp.zeros_like(stepped)
    for copy in copies:
        copy.wait()
    for j in range(4):
        gather_left(table, lambda s: lists[8 + j, s], lambda t: lists[4 + j, t], cols, left, KT, KS)
        for s in range(KT):
            own[s] = cols[table[lists[8 + j, s], place[1] * 4 + j]]
        right = rows[j * KS : (j + 1) * KS].reshape(KS * BLOCK, BLOCK)
        product = jnp.dot(left[...], right, preferred_element_type=jnp.float32)
        result = 1.5 * own[...].astype(jnp.float32) - 0.5 * product.reshape(KT, SL, BLOCK)
        own[...] = result.astype(BF)
        for s in range(KT):
            i = lists[8 + j, s]

            @pl.when(i < NB)
            def _():
                stepped[i, :, j * BLOCK : (j + 1) * BLOCK] = own[s]


def square_rows_kernel(place, lists, *refs):
    row_parts = refs[:4]
    out = refs[4]
    rows, sems = refs[5:]
    copies = fetch_rows(place, row_parts, rows, sems)
    for copy in copies:
        copy.start()
    out[...] = jnp.zeros_like(out)
    for copy in copies:
        copy.wait()
    for j in range(4):

        def one(s, carry):
            i = lists[4 + j, s]

            @pl.when(i // 8 == place[0])
            def _():
                out[i % 8, :, :, j * BLOCK : (j + 1) * BLOCK] = rows[j * KS + s]

            return carry

        lax.fori_loop(0, KS, one, 0)


SMEM = pl.BlockSpec(memory_space=pltpu.SMEM)
VMEM = pl.BlockSpec(memory_space=pltpu.VMEM)
ANY = pl.BlockSpec(memory_space=pl.ANY)


def call(kernel, outs, in_specs, out_specs, scratch, flops, moved):
    return pl.pallas_call(
        kernel,
        out_shape=outs,
        in_specs=in_specs,
        out_specs=out_specs,
        scratch_shapes=scratch,
        compiler_params=pltpu.CompilerParams(vmem_limit_bytes=VMEM_LIMIT),
        cost_estimate=pl.CostEstimate(flops=flops, bytes_accessed=moved, transcendentals=0),
    )


def gather_rows(packed):
    both = jnp.stack([packed, row_shift(packed, 0, 1)])
    return [both] + [row_shift(both, dx, 0) for dx in (1, 2, 3)]


def gather_cols(packed):
    both = jnp.stack([packed, col_shift(packed, 0, 1, 0)])
    mine = [both] + [col_shift(both, dz, 0, 0) for dz in (1, 2, 3)]
    return mine + [col_shift(part, 0, 0, 1) for part in mine]


def on_device(density, pattern, square_filter, step_filter):
    place = jnp.stack([lax.axis_index("row"), lax.axis_index("col")]).astype(jnp.int32)
    masks = jnp.concatenate([pattern, square_filter, step_filter], axis=1).astype(BF)
    head = jnp.pad(masks, ((0, SL - 8), (0, 4 * BLOCK - 12)))
    blocks = density.reshape(8, TR, SL, 4 * BLOCK).transpose(1, 0, 2, 3)
    sent = jnp.concatenate([blocks, jnp.broadcast_to(head, (TR, 1, SL, 4 * BLOCK))], axis=1)
    sliced = lax.all_to_all(sent, "row", 0, 0, tiled=True)

    packed, lists = call(
        pack_kernel,
        (jax.ShapeDtypeStruct((PACK, SL, BLOCK), BF), jax.ShapeDtypeStruct((12, 32), jnp.int32)),
        [SMEM, VMEM],
        (VMEM, SMEM),
        [pltpu.VMEM((NB, BLOCK), jnp.int32), pltpu.SMEM((NB, BLOCK), jnp.int32), pltpu.SemaphoreType.DMA],
        0,
        2 << 20,
    )(place, sliced)

    row_parts = gather_rows(packed)
    col_parts = gather_cols(packed)
    square_packed, table = call(
        square_kernel,
        (
            jax.ShapeDtypeStruct((4 * KS, SL, BLOCK), BF),
            jax.ShapeDtypeStruct((NB + 8, BLOCK), jnp.int32),
        ),
        [SMEM, SMEM] + [ANY] * 12,
        (VMEM, SMEM),
        [
            pltpu.VMEM((PACK, TR, SL, BLOCK), BF),
            pltpu.VMEM((TC * PACK, SL, BLOCK), BF),
            pltpu.VMEM((KS * SL, KP * BLOCK), BF),
            pltpu.VMEM((NB + 8, BLOCK), jnp.int32),
            pltpu.SemaphoreType.DMA((24,)),
            pltpu.SemaphoreType.DMA,
        ],
        2 * 4 * KS * SL * KP * BLOCK * BLOCK,
        8 << 20,
    )(place, lists, *row_parts, *col_parts)

    square_parts = gather_rows(square_packed)
    stepped = call(
        step_kernel,
        jax.ShapeDtypeStruct((NB, SL, 4 * BLOCK), BF),
        [SMEM, SMEM, SMEM] + [ANY] * 12,
        VMEM,
        [
            pltpu.VMEM((4 * KS, TR, SL, BLOCK), BF),
            pltpu.VMEM((TC * PACK, SL, BLOCK), BF),
            pltpu.VMEM((KT * SL, KS * BLOCK), BF),
            pltpu.VMEM((KT, SL, BLOCK), BF),
            pltpu.SemaphoreType.DMA((24,)),
        ],
        2 * 4 * KT * SL * KS * BLOCK * BLOCK,
        9 << 20,
    )(place, lists, table, *square_parts, *col_parts)
    back = lax.all_to_all(stepped, "row", 0, 0, tiled=True)
    square = call(
        square_rows_kernel,
        jax.ShapeDtypeStruct((8, TR, SL, 4 * BLOCK), BF),
        [SMEM, SMEM] + [ANY] * 4,
        VMEM,
        [pltpu.VMEM((4 * KS, TR, SL, BLOCK), BF), pltpu.SemaphoreType.DMA((8,))],
        0,
        4 << 20,
    )(place, lists, *square_parts)
    square = square.reshape(8 * BLOCK, 4 * BLOCK)
    stepped = back.reshape(TR, 8, SL, 4 * BLOCK).transpose(1, 0, 2, 3).reshape(8 * BLOCK, 4 * BLOCK)
    return square, stepped


def solution(mesh):
    placed = (P("row", "col"),) * 4
    return jax.shard_map(
        on_device,
        mesh=mesh,
        in_specs=placed,
        out_specs=(P("row", "col"), P("row", "col")),
        check_vma=False,
    )
```

time: 518 us -> 190 us (0.37)
  waiting for transfers between devices: 464 us -> 116 us
  Pallas kernels: 0 us -> 39.6 us
  matrix products: 31.2 us -> 0 us
  starting transfers between devices: 0.12 us -> 26.6 us
  between operations: 13.8 us -> 0.74 us
    all_gather x3 -> x0, waiting for transfers between devices: 463 us -> none  [the longest x1 170 us: on_device(): columns = lax.all_gather(masked, 'row', axis=0, tiled=True)]
    ppermute x0 -> x16, waiting for transfers between devices: none -> 85.6 us  [the longest x8 58.6 us: row_shift(): return lax.ppermute(value, 'row', pairs)]
    pallas_call x0 -> x4, Pallas kernels: none -> 39.6 us  [the longest x1 16 us: on_device(): call(step_kernel, jax.ShapeDtypeStruct((NB, SL, 4 * BLOCK), BF), [SMEM, S...]
    dot_general x2 -> x0, matrix products: 31.2 us -> none  [right_folder(): return jnp.dot(piece, columns, preferred_element_type=jnp.float32)]
    all_to_all x0 -> x2, waiting for transfers between devices: none -> 30.1 us  [the longest x1 17.8 us: on_device(): sliced = lax.all_to_all(sent, 'row', 0, 0, tiled=True)]
    ppermute x0 -> x16, starting transfers between devices: none -> 17 us  [the longest x8 8.79 us: col_shift(): return lax.ppermute(value, 'col', pairs)]
    all_to_all x0 -> x2, starting transfers between devices: none -> 9.65 us  [the longest x1 5.4 us: on_device(): sliced = lax.all_to_all(sent, 'row', 0, 0, tiled=True)]
  transfers between devices with their start and end apart: 3 -> 18, of which waited for: 3 -> 12; matrix products, arithmetic and copies ran while one was open for 0% -> 0% of each run, Pallas kernels for 0% -> 2%
where the time goes in v1:
time: 190 us
  waiting for transfers between devices  116 us (61%)
  Pallas kernels  39.6 us (21%)
  starting transfers between devices  26.6 us (14%)
  local copies, waits for them, and re-layouts  3.69 us (2%)
  other arithmetic  3.45 us (2%)
    ppermute x8, waiting for transfers between devices, row_shift(): return lax.ppermute(value, 'row', pairs)  58.6 us
    ppermute x8, waiting for transfers between devices, col_shift(): return lax.ppermute(value, 'col', pairs)  27 us
    all_to_all x1, waiting for transfers between devices, on_device(): sliced = lax.all_to_all(sent, 'row', 0, 0, tiled=True)  17.8 us
    pallas_call x1, Pallas kernels, on_device(): call(step_kernel, jax.ShapeDtypeStruct((NB, SL, 4 * BLOCK), BF), [SMEM, S...  16 us
    pallas_call x1, Pallas kernels, on_device(): call(square_kernel, (jax.ShapeDtypeStruct((4 * KS, SL, BLOCK), BF), jax.S...  13.5 us
    all_to_all x1, waiting for transfers between devices, on_device(): back = lax.all_to_all(stepped, 'row', 0, 0, tiled=True)  12.3 us
    ppermute x8, starting transfers between devices, col_shift(): return lax.ppermute(value, 'col', pairs)  8.79 us
    ppermute x8, starting transfers between devices, row_shift(): return lax.ppermute(value, 'row', pairs)  8.18 us
  transfers between devices with their start and end apart: 18, of which 12 were waited for; matrix products, arithmetic and copies ran while one was open for 0% of the time, Pallas kernels for 2%

profile of v1, /device:TPU:0, one launch (start us, length us, event | category | flops | bytes accessed | tf_op | source)
XLA Modules:
  0.0 189.8 jit_solution(15969647161951770334)
XLA Ops:
  0.6 0.7 convert.9
  1.3 0.7 convert.10
  2.0 0.7 convert.11
  2.7 0.1 copy.11
  2.8 1.3 copy.13
  4.1 1.1 pad_maximum_fusion
  5.3 5.4 %all-to-all-start = ((bf16[8,9,16,512]{3,2,1,0:T(8,128)(2,1)}), bf16[8,9,16,512]{3,2,1,0:T(8,128)(2,1)S(1)}, u32[]{:S(2)}, u32[]{:S(2)}) async-start(bf16[8,9,16,512]{3,2,1,0:T(8,128)(2,1)} %pad_maximum_fusion), calls=%async_computation | async-start | bytes 2359296 | tf_op jit(solution)/shard_map/all_to_all | solution.py:241
  10.7 0.1 pad_add_fusion.place
  10.7 17.8 %all-to-all-done.sliced = bf16[8,9,16,512]{3,2,1,0:T(8,128)(2,1)S(1)} async-done(((bf16[8,9,16,512]{3,2,1,0:T(8,128)(2,1)}), bf16[8,9,16,512]{3,2,1,0:T(8,128)(2,1)S(1)}, u32[]{:S(2)}, u32[]{:S(2)}) %all-to-all-start) | async-done | bytes 1179680 | tf_op jit(solution)/shard_map/all_to_all | solution.py:241
  28.6 5.6 %shard_map.59 = (bf16[72,16,128]{2,1,0:T(8,128)(2,1)S(1)}, s32[12,32]{1,0:T(8,128)S(1)}) custom-call(s32[2]{0:T(128)S(1)} %pad_add_fusion.place, bf16[8,9,16,512]{3,2,1,0:T(8,128)(2,1)S(1)} %all-to-all-done.sliced), custom_call_target="tpu_custom_call" | custom-call | bytes 2097152 | tf_op jit(solution)/shard_map/pallas_call | solution.py:243
  34.1 3.0 %collective-permute-start.4 = (bf16[72,16,128]{2,1,0:T(8,128)(2,1)S(1)}, bf16[72,16,128]{2,1,0:T(8,128)(2,1)S(1)}, u32[]{:S(2)}, u32[]{:S(2)}) collective-permute-start(bf16[72,16,128]{2,1,0:T(8,128)(2,1)S(1)} %get-tuple-element.7), channel_id=1, source_target_pairs={{0,2},{1,3},{2,0},{3,1},{4,6},{5,7},{6,4},{7,5},{8,10},{9,11},{10,... | collective-permute-start | bytes 884744 | tf_op jit(solution)/shard_map/ppermute | solution.py:44
  37.1 0.0 collective-permute-start
  37.1 8.5 %collective-permute-done.4 = bf16[72,16,128]{2,1,0:T(8,128)(2,1)S(1)} collective-permute-done((bf16[72,16,128]{2,1,0:T(8,128)(2,1)S(1)}, bf16[72,16,128]{2,1,0:T(8,128)(2,1)S(1)}, u32[]{:S(2)}, u32[]{:S(2)}) %collective-permute-start.4) | collective-permute-done | bytes 294944 | tf_op jit(solution)/shard_map/ppermute | solution.py:44
  45.7 3.1 %collective-permute-done = bf16[72,16,128]{2,1,0:T(8,128)(2,1)S(1)} collective-permute-done((bf16[72,16,128]{2,1,0:T(8,128)(2,1)S(1)}, bf16[72,16,128]{2,1,0:T(8,128)(2,1)S(1)}, u32[]{:S(2)}, u32[]{:S(2)}) %collective-permute-start) | collective-permute-done | bytes 294944 | tf_op jit(solution)/shard_map/ppermute | solution.py:34
  48.8 0.1 pad_maximum_fusion.2
  48.9 1.1 collective-permute-start.3
  50.0 1.4 collective-permute-start.2
  51.3 4.0 %collective-permute-start.7 = (bf16[2,72,16,128]{3,2,1,0:T(8,128)(2,1)S(1)}, bf16[2,72,16,128]{3,2,1,0:T(8,128)(2,1)S(1)}, u32[]{:S(2)}, u32[]{:S(2)}) collective-permute-start(bf16[2,72,16,128]{3,2,1,0:T(8,128)(2,1)S(1)} %get-tuple-element.10.refs_4_), channel_id=1, source_target_pairs={{0,12},{1,13},{2,14},{3,15},{4,0},{5,1},{6,2},{7,3},{8,4},{9,5},{1... | collective-permute-start | bytes 1769480 | tf_op jit(solution)/shard_map/ppermute | solution.py:44
  55.4 0.0 collective-permute-start.6
  55.4 1.3 collective-permute-start.5
  56.6 8.6 %collective-permute-done.3.refs_3_ = bf16[2,72,16,128]{3,2,1,0:T(8,128)(2,1)S(1)} collective-permute-done((bf16[2,72,16,128]{3,2,1,0:T(8,128)(2,1)S(1)}, bf16[2,72,16,128]{3,2,1,0:T(8,128)(2,1)S(1)}, u32[]{:S(2)}, u32[]{:S(2)}) %collective-permute-start.3) | collective-permute-done | bytes 589856 | tf_op jit(solution)/shard_map/ppermute | solution.py:34
  65.2 0.0 collective-permute-start.1
  65.2 0.0 collective-permute-done.2.refs_2_
  65.2 0.0 collective-permute-start.8
  65.2 13.6 %collective-permute-done.7.refs_7_ = bf16[2,72,16,128]{3,2,1,0:T(8,128)(2,1)S(1)} collective-permute-done((bf16[2,72,16,128]{3,2,1,0:T(8,128)(2,1)S(1)}, bf16[2,72,16,128]{3,2,1,0:T(8,128)(2,1)S(1)}, u32[]{:S(2)}, u32[]{:S(2)}) %collective-permute-start.7) | collective-permute-done | bytes 589856 | tf_op jit(solution)/shard_map/ppermute | solution.py:44
  78.8 0.0 collective-permute-start.11
  78.8 0.0 collective-permute-done.6.refs_6_
  78.8 0.5 collective-permute-start.10
  79.3 2.9 %collective-permute-done.5.refs_5_ = bf16[2,72,16,128]{3,2,1,0:T(8,128)(2,1)S(1)} collective-permute-done((bf16[2,72,16,128]{3,2,1,0:T(8,128)(2,1)S(1)}, bf16[2,72,16,128]{3,2,1,0:T(8,128)(2,1)S(1)}, u32[]{:S(2)}, u32[]{:S(2)}) %collective-permute-start.5) | collective-permute-done | bytes 589856 | tf_op jit(solution)/shard_map/ppermute | solution.py:44
  82.2 0.0 collective-permute-start.9
  82.2 0.0 collective-permute-done.1.refs_1_
  82.2 0.0 collective-permute-done.8.refs_8_
  82.2 0.0 collective-permute-done.11.refs_11_
  82.2 0.0 collective-permute-done.10.refs_10_
  82.3 2.0 %collective-permute-done.9.refs_9_ = bf16[2,72,16,128]{3,2,1,0:T(8,128)(2,1)S(1)} collective-permute-done((bf16[2,72,16,128]{3,2,1,0:T(8,128)(2,1)S(1)}, bf16[2,72,16,128]{3,2,1,0:T(8,128)(2,1)S(1)}, u32[]{:S(2)}, u32[]{:S(2)}) %collective-permute-start.9) | collective-permute-done | bytes 589856 | tf_op jit(solution)/shard_map/ppermute | solution.py:44
  84.2 13.5 %shard_map.60 = (bf16[100,16,128]{2,1,0:T(8,128)(2,1)S(1)}, s32[72,128]{1,0:T(8,128)S(1)}) custom-call(s32[2]{0:T(128)S(1)} %pad_add_fusion.place, s32[12,32]{1,0:T(8,128)S(1)} %get-tuple-element.6.lists, bf16[2,72,16,128]{3,2,1,0:T(8,128)(2,1)S(1)} %get-tuple-element.11.refs_0_, bf16[2,72,16,128]{3,2,1,0:T(8,128)(2,1)S(1)} %collective-permute-done.1.refs_1_, ...), custom_call_target="tpu_custom_call" | custom-call | flops 891289600 | bytes 8388608 | tf_op jit(solution)/shard_map/pallas_call | solution.py:255
  97.7 2.5 %collective-permute-start.12 = (bf16[100,16,128]{2,1,0:T(8,128)(2,1)S(1)}, bf16[100,16,128]{2,1,0:T(8,128)(2,1)S(1)}, u32[]{:S(2)}, u32[]{:S(2)}) collective-permute-start(bf16[100,16,128]{2,1,0:T(8,128)(2,1)S(1)} %get-tuple-element.8), channel_id=1, source_target_pairs={{0,16},{16,0},{32,48},{48,32},{64,80},{80,64},{96,112},{112,96},{1... | collective-permute-start | bytes 1228808 | tf_op jit(solution)/shard_map/ppermute | solution.py:34
  100.3 9.8 %collective-permute-done.12 = bf16[100,16,128]{2,1,0:T(8,128)(2,1)S(1)} collective-permute-done((bf16[100,16,128]{2,1,0:T(8,128)(2,1)S(1)}, bf16[100,16,128]{2,1,0:T(8,128)(2,1)S(1)}, u32[]{:S(2)}, u32[]{:S(2)}) %collective-permute-start.12) | collective-permute-done | bytes 409632 | tf_op jit(solution)/shard_map/ppermute | solution.py:34
  110.0 0.1 pad_maximum_fusion.1.refs_0_
  110.1 1.8 collective-permute-start.15
  111.9 1.4 collective-permute-start.14
  113.3 0.0 collective-permute-start.13
  113.3 18.0 %collective-permute-done.15.refs_3_ = bf16[2,100,16,128]{3,2,1,0:T(8,128)(2,1)S(1)} collective-permute-done((bf16[2,100,16,128]{3,2,1,0:T(8,128)(2,1)S(1)}, bf16[2,100,16,128]{3,2,1,0:T(8,128)(2,1)S(1)}, u32[]{:S(2)}, u32[]{:S(2)}) %collective-permute-start.15) | collective-permute-done | bytes 819232 | tf_op jit(solution)/shard_map/ppermute | solution.py:34
  131.3 3.3 %collective-permute-done.14.refs_2_ = bf16[2,100,16,128]{3,2,1,0:T(8,128)(2,1)S(1)} collective-permute-done((bf16[2,100,16,128]{3,2,1,0:T(8,128)(2,1)S(1)}, bf16[2,100,16,128]{3,2,1,0:T(8,128)(2,1)S(1)}, u32[]{:S(2)}, u32[]{:S(2)}) %collective-permute-start.14) | collective-permute-done | bytes 819232 | tf_op jit(solution)/shard_map/ppermute | solution.py:34
  134.6 15.8 %collective-permute-done.13.refs_1_ = bf16[2,100,16,128]{3,2,1,0:T(8,128)(2,1)S(1)} collective-permute-done((bf16[2,100,16,128]{3,2,1,0:T(8,128)(2,1)S(1)}, bf16[2,100,16,128]{3,2,1,0:T(8,128)(2,1)S(1)}, u32[]{:S(2)}, u32[]{:S(2)}) %collective-permute-start.13) | collective-permute-done | bytes 819232 | tf_op jit(solution)/shard_map/ppermute | solution.py:34
  150.4 16.0 %shard_map.62 = bf16[64,16,512]{2,1,0:T(8,128)(2,1)} custom-call(s32[2]{0:T(128)S(1)} %pad_add_fusion.place, s32[12,32]{1,0:T(8,128)S(1)} %get-tuple-element.6.lists, s32[72,128]{1,0:T(8,128)S(1)} %get-tuple-element.9.table, bf16[2,100,16,128]{3,2,1,0:T(8,128)(2,1)S(1)} %pad_maximum_fusion.1.refs_0_, ...), custom_call_target="tpu_custom_call" | custom-call | flops 1101004800 | bytes 9437184 | tf_op jit(solution)/shard_map/pallas_call | solution.py:276
  166.4 4.3 %all-to-all-start.1 = ((bf16[64,16,512]{2,1,0:T(8,128)(2,1)}), bf16[64,16,512]{2,1,0:T(8,128)(2,1)}, u32[]{:S(2)}, u32[]{:S(2)}) async-start(bf16[64,16,512]{2,1,0:T(8,128)(2,1)} %shard_map.62), calls=%async_computation.1 | async-start | bytes 2097152 | tf_op jit(solution)/shard_map/all_to_all | solution.py:291
  170.7 4.6 %shard_map.61 = bf16[8,8,16,512]{3,2,1,0:T(8,128)(2,1)} custom-call(s32[2]{0:T(128)S(1)} %pad_add_fusion.place, s32[12,32]{1,0:T(8,128)S(1)} %get-tuple-element.6.lists, bf16[2,100,16,128]{3,2,1,0:T(8,128)(2,1)S(1)} %pad_maximum_fusion.1.refs_0_, bf16[2,100,16,128]{3,2,1,0:T(8,128)(2,1)S(1)} %collective-permute-done.13.refs_1_, ...), custom_call_target="tpu_custom_call" | custom-call | bytes 4194304 | tf_op jit(solution)/shard_map/pallas_call | solution.py:292
  175.3 12.3 %all-to-all-done.1 = bf16[64,16,512]{2,1,0:T(8,128)(2,1)} async-done(((bf16[64,16,512]{2,1,0:T(8,128)(2,1)}), bf16[64,16,512]{2,1,0:T(8,128)(2,1)}, u32[]{:S(2)}, u32[]{:S(2)}) %all-to-all-start.1) | async-done | bytes 1048608 | tf_op jit(solution)/shard_map/all_to_all | solution.py:291
  187.5 2.3 %copy.10 = bf16[8,8,16,512]{3,2,1,0:T(8,128)(2,1)} copy(bf16[8,8,16,512]{3,2,0,1:T(8,128)(2,1)} %bitcast.11) | data formatting | bytes 2097152 | tf_op jit(solution)/shard_map/transpose | solution.py:302
  (3 shorter events, 0.0 us)
Async XLA Ops:
  5.3 23.3 %all-to-all-start = ((bf16[8,9,16,512]{3,2,1,0:T(8,128)(2,1)}), bf16[8,9,16,512]{3,2,1,0:T(8,128)(2,1)S(1)}, u32[]{:S(2)}, u32[]{:S(2)}) async-start(bf16[8,9,16,512]{3,2,1,0:T(8,128)(2,1)} %pad_maximum_fusion), calls=%async_computation | async-start | bytes 2359296 | tf_op jit(solution)/shard_map/all_to_all | solution.py:241
  34.1 11.5 %collective-permute-start.4 = (bf16[72,16,128]{2,1,0:T(8,128)(2,1)S(1)}, bf16[72,16,128]{2,1,0:T(8,128)(2,1)S(1)}, u32[]{:S(2)}, u32[]{:S(2)}) collective-permute-start(bf16[72,16,128]{2,1,0:T(8,128)(2,1)S(1)} %get-tuple-element.7), channel_id=1, source_target_pairs={{0,2},{1,3},{2,0},{3,1},{4,6},{5,7},{6,4},{7,5},{8,10},{9,11},{10,... | collective-permute-start | bytes 884744 | tf_op jit(solution)/shard_map/ppermute | solution.py:44
  37.1 11.6 %collective-permute-start = (bf16[72,16,128]{2,1,0:T(8,128)(2,1)S(1)}, bf16[72,16,128]{2,1,0:T(8,128)(2,1)S(1)}, u32[]{:S(2)}, u32[]{:S(2)}) collective-permute-start(bf16[72,16,128]{2,1,0:T(8,128)(2,1)S(1)} %get-tuple-element.7), channel_id=1, source_target_pairs={{0,16},{16,0},{32,48},{48,32},{64,80},{80,64},{96,112},{112,96},{1... | collective-permute-start | bytes 884744 | tf_op jit(solution)/shard_map/ppermute | solution.py:34
  48.9 16.3 %collective-permute-start.3 = (bf16[2,72,16,128]{3,2,1,0:T(8,128)(2,1)S(1)}, bf16[2,72,16,128]{3,2,1,0:T(8,128)(2,1)S(1)}, u32[]{:S(2)}, u32[]{:S(2)}) collective-permute-start(bf16[2,72,16,128]{3,2,1,0:T(8,128)(2,1)S(1)} %get-tuple-element.11.refs_0_), channel_id=1, source_target_pairs={{0,96},{16,112},{32,0},{48,16},{64,32},{80,48},{96,64},{112,80},{1... | collective-permute-start | bytes 1769480 | tf_op jit(solution)/shard_map/ppermute | solution.py:34
  50.0 15.2 %collective-permute-start.2 = (bf16[2,72,16,128]{3,2,1,0:T(8,128)(2,1)S(1)}, bf16[2,72,16,128]{3,2,1,0:T(8,128)(2,1)S(1)}, u32[]{:S(2)}, u32[]{:S(2)}) collective-permute-start(bf16[2,72,16,128]{3,2,1,0:T(8,128)(2,1)S(1)} %get-tuple-element.11.refs_0_), channel_id=1, source_target_pairs={{0,64},{16,80},{32,96},{48,112},{64,0},{80,16},{96,32},{112,48},{1... | collective-permute-start | bytes 1769480 | tf_op jit(solution)/shard_map/ppermute | solution.py:34
  51.3 27.5 %collective-permute-start.7 = (bf16[2,72,16,128]{3,2,1,0:T(8,128)(2,1)S(1)}, bf16[2,72,16,128]{3,2,1,0:T(8,128)(2,1)S(1)}, u32[]{:S(2)}, u32[]{:S(2)}) collective-permute-start(bf16[2,72,16,128]{3,2,1,0:T(8,128)(2,1)S(1)} %get-tuple-element.10.refs_4_), channel_id=1, source_target_pairs={{0,12},{1,13},{2,14},{3,15},{4,0},{5,1},{6,2},{7,3},{8,4},{9,5},{1... | collective-permute-start | bytes 1769480 | tf_op jit(solution)/shard_map/ppermute | solution.py:44
  55.4 23.5 %collective-permute-start.6 = (bf16[2,72,16,128]{3,2,1,0:T(8,128)(2,1)S(1)}, bf16[2,72,16,128]{3,2,1,0:T(8,128)(2,1)S(1)}, u32[]{:S(2)}, u32[]{:S(2)}) collective-permute-start(bf16[2,72,16,128]{3,2,1,0:T(8,128)(2,1)S(1)} %get-tuple-element.10.refs_4_), channel_id=1, source_target_pairs={{0,8},{1,9},{2,10},{3,11},{4,12},{5,13},{6,14},{7,15},{8,0},{9,1},... | collective-permute-start | bytes 1769480 | tf_op jit(solution)/shard_map/ppermute | solution.py:44
  55.4 26.9 %collective-permute-start.5 = (bf16[2,72,16,128]{3,2,1,0:T(8,128)(2,1)S(1)}, bf16[2,72,16,128]{3,2,1,0:T(8,128)(2,1)S(1)}, u32[]{:S(2)}, u32[]{:S(2)}) collective-permute-start(bf16[2,72,16,128]{3,2,1,0:T(8,128)(2,1)S(1)} %get-tuple-element.10.refs_4_), channel_id=1, source_target_pairs={{0,4},{1,5},{2,6},{3,7},{4,8},{5,9},{6,10},{7,11},{8,12},{9,13},{1... | collective-permute-start | bytes 1769480 | tf_op jit(solution)/shard_map/ppermute | solution.py:44
  65.2 17.0 %collective-permute-start.1 = (bf16[2,72,16,128]{3,2,1,0:T(8,128)(2,1)S(1)}, bf16[2,72,16,128]{3,2,1,0:T(8,128)(2,1)S(1)}, u32[]{:S(2)}, u32[]{:S(2)}) collective-permute-start(bf16[2,72,16,128]{3,2,1,0:T(8,128)(2,1)S(1)} %get-tuple-element.11.refs_0_), channel_id=1, source_target_pairs={{0,32},{16,48},{32,64},{48,80},{64,96},{80,112},{96,0},{112,16},{1... | collective-permute-start | bytes 1769480 | tf_op jit(solution)/shard_map/ppermute | solution.py:34
  65.2 17.0 %collective-permute-start.8 = (bf16[2,72,16,128]{3,2,1,0:T(8,128)(2,1)S(1)}, bf16[2,72,16,128]{3,2,1,0:T(8,128)(2,1)S(1)}, u32[]{:S(2)}, u32[]{:S(2)}) collective-permute-start(bf16[2,72,16,128]{3,2,1,0:T(8,128)(2,1)S(1)} %get-tuple-element.10.refs_4_), channel_id=1, source_target_pairs={{0,1},{1,0},{2,3},{3,2},{4,5},{5,4},{6,7},{7,6},{8,9},{9,8},{10,11... | collective-permute-start | bytes 1769480 | tf_op jit(solution)/shard_map/ppermute | solution.py:44
  78.8 3.4 %collective-permute-start.11 = (bf16[2,72,16,128]{3,2,1,0:T(8,128)(2,1)S(1)}, bf16[2,72,16,128]{3,2,1,0:T(8,128)(2,1)S(1)}, u32[]{:S(2)}, u32[]{:S(2)}) collective-permute-start(bf16[2,72,16,128]{3,2,1,0:T(8,128)(2,1)S(1)} %collective-permute-done.7.refs_7_), channel_id=1, source_target_pairs={{0,1},{1,0},{2,3},{3,2},{4,5},{5,4},{6,7},{7,6},{8,9},{9,8},{10,11... | collective-permute-start | bytes 1769480 | tf_op jit(solution)/shard_map/ppermute | solution.py:44
  78.8 3.4 %collective-permute-start.10 = (bf16[2,72,16,128]{3,2,1,0:T(8,128)(2,1)S(1)}, bf16[2,72,16,128]{3,2,1,0:T(8,128)(2,1)S(1)}, u32[]{:S(2)}, u32[]{:S(2)}) collective-permute-start(bf16[2,72,16,128]{3,2,1,0:T(8,128)(2,1)S(1)} %collective-permute-done.6.refs_6_), channel_id=1, source_target_pairs={{0,1},{1,0},{2,3},{3,2},{4,5},{5,4},{6,7},{7,6},{8,9},{9,8},{10,11... | collective-permute-start | bytes 1769480 | tf_op jit(solution)/shard_map/ppermute | solution.py:44
  82.2 2.0 %collective-permute-start.9 = (bf16[2,72,16,128]{3,2,1,0:T(8,128)(2,1)S(1)}, bf16[2,72,16,128]{3,2,1,0:T(8,128)(2,1)S(1)}, u32[]{:S(2)}, u32[]{:S(2)}) collective-permute-start(bf16[2,72,16,128]{3,2,1,0:T(8,128)(2,1)S(1)} %collective-permute-done.5.refs_5_), channel_id=1, source_target_pairs={{0,1},{1,0},{2,3},{3,2},{4,5},{5,4},{6,7},{7,6},{8,9},{9,8},{10,11... | collective-permute-start | bytes 1769480 | tf_op jit(solution)/shard_map/ppermute | solution.py:44
  97.7 12.3 %collective-permute-start.12 = (bf16[100,16,128]{2,1,0:T(8,128)(2,1)S(1)}, bf16[100,16,128]{2,1,0:T(8,128)(2,1)S(1)}, u32[]{:S(2)}, u32[]{:S(2)}) collective-permute-start(bf16[100,16,128]{2,1,0:T(8,128)(2,1)S(1)} %get-tuple-element.8), channel_id=1, source_target_pairs={{0,16},{16,0},{32,48},{48,32},{64,80},{80,64},{96,112},{112,96},{1... | collective-permute-start | bytes 1228808 | tf_op jit(solution)/shard_map/ppermute | solution.py:34
  110.1 21.2 %collective-permute-start.15 = (bf16[2,100,16,128]{3,2,1,0:T(8,128)(2,1)S(1)}, bf16[2,100,16,128]{3,2,1,0:T(8,128)(2,1)S(1)}, u32[]{:S(2)}, u32[]{:S(2)}) collective-permute-start(bf16[2,100,16,128]{3,2,1,0:T(8,128)(2,1)S(1)} %pad_maximum_fusion.1.refs_0_), channel_id=1, source_target_pairs={{0,96},{16,112},{32,0},{48,16},{64,32},{80,48},{96,64},{112,80},{1... | collective-permute-start | bytes 2457608 | tf_op jit(solution)/shard_map/ppermute | solution.py:34
  111.9 22.7 %collective-permute-start.14 = (bf16[2,100,16,128]{3,2,1,0:T(8,128)(2,1)S(1)}, bf16[2,100,16,128]{3,2,1,0:T(8,128)(2,1)S(1)}, u32[]{:S(2)}, u32[]{:S(2)}) collective-permute-start(bf16[2,100,16,128]{3,2,1,0:T(8,128)(2,1)S(1)} %pad_maximum_fusion.1.refs_0_), channel_id=1, source_target_pairs={{0,64},{16,80},{32,96},{48,112},{64,0},{80,16},{96,32},{112,48},{1... | collective-permute-start | bytes 2457608 | tf_op jit(solution)/shard_map/ppermute | solution.py:34
  113.3 37.1 %collective-permute-start.13 = (bf16[2,100,16,128]{3,2,1,0:T(8,128)(2,1)S(1)}, bf16[2,100,16,128]{3,2,1,0:T(8,128)(2,1)S(1)}, u32[]{:S(2)}, u32[]{:S(2)}) collective-permute-start(bf16[2,100,16,128]{3,2,1,0:T(8,128)(2,1)S(1)} %pad_maximum_fusion.1.refs_0_), channel_id=1, source_target_pairs={{0,32},{16,48},{32,64},{48,80},{64,96},{80,112},{96,0},{112,16},{1... | collective-permute-start | bytes 2457608 | tf_op jit(solution)/shard_map/ppermute | solution.py:34
  166.4 21.1 %all-to-all-start.1 = ((bf16[64,16,512]{2,1,0:T(8,128)(2,1)}), bf16[64,16,512]{2,1,0:T(8,128)(2,1)}, u32[]{:S(2)}, u32[]{:S(2)}) async-start(bf16[64,16,512]{2,1,0:T(8,128)(2,1)} %shard_map.62), calls=%async_computation.1 | async-start | bytes 2097152 | tf_op jit(solution)/shard_map/all_to_all | solution.py:291

commit v2 on v1

v2 whole, which is shorter than its diff:
```python
import functools

import jax
import jax.numpy as jnp
from jax import lax
from jax.experimental import pallas as pl
from jax.experimental.pallas import tpu as pltpu
from jax.sharding import PartitionSpec as P

BLOCK = 128
NB = 64
TR = 8
TC = 16
SL = 16
KP, KS, KT = 17, 25, 21
SLOTS = KP + 1
PACK = 4 * SLOTS
ZERO = PACK - 1
NONE = NB
VMEM_LIMIT = 60 * 1024 * 1024
BF = jnp.bfloat16


def row_index(x, y):
    return (x % 4) * 2 + (y % 2)


def col_index(z, y, core):
    return (z % 4) * 4 + (y % 2) * 2 + (core % 2)


def row_shift(value, dx, dy):
    pairs = [(row_index(x, y), row_index(x + dx, y + dy)) for x in range(4) for y in range(2)]
    return lax.ppermute(value, "row", pairs)


def col_shift(value, dz, dy, dc):
    pairs = [
        (col_index(z, y, c), col_index(z + dz, y + dy, c + dc))
        for z in range(4)
        for y in range(2)
        for c in range(2)
    ]
    return lax.ppermute(value, "col", pairs)


def slice_kernel(density, pattern, square_filter, step_filter, sent, small, masks, sems):
    copies = [pltpu.make_async_copy(density.at[:, d], sent.at[d, pl.ds(0, 8)], sems.at[d]) for d in range(TR)]
    filters = [
        pltpu.make_async_copy(mask, masks.at[n], sems.at[TR + n])
        for n, mask in enumerate((pattern, square_filter, step_filter))
    ]
    for copy in filters + copies:
        copy.start()
    small[...] = jnp.zeros_like(small)
    for n, copy in enumerate(filters):
        copy.wait()
        small[4 * n : 4 * n + 4, 0:8] = masks[n].astype(jnp.float32)
    head = small[...].astype(BF)
    for d in range(TR):
        sent[d, 8, :, 0:BLOCK] = head
        sent[d, 8, :, BLOCK:] = jnp.zeros((SL, 3 * BLOCK), BF)
    for copy in copies:
        copy.wait()


def pack_kernel(sliced, packed, lists, flags, flags_s, sem):
    marks = jnp.zeros((SL, BLOCK), jnp.float32)
    for s in range(TR):
        mark = sliced[s, 8, :, 0:BLOCK].astype(jnp.float32)
        marks = marks + (pltpu.roll(mark, 8 * s, 1) if s else mark)
    flags[...] = marks.astype(jnp.int32)
    copy = pltpu.make_async_copy(flags, flags_s, sem)
    copy.start()
    packed[...] = jnp.zeros_like(packed)
    for n in range(4):
        for t in range(KP):
            lists[n, t] = NONE
    copy.wait()

    def kept(b, counts):
        for q in range(8):
            i = 8 * b + q
            out = []
            for n in range(4):
                lists[n, counts[n]] = i
                packed[n * SLOTS + counts[n]] = sliced[b, q, :, n * BLOCK : (n + 1) * BLOCK]
                out.append(counts[n] + flags_s[n, i])
            counts = tuple(out)
        return counts

    counts = lax.fori_loop(0, TR, kept, (jnp.int32(0),) * 4)
    for n in range(4):
        lists[n, counts[n]] = NONE
    packed[KP] = marks.astype(BF)
    packed[ZERO] = jnp.zeros((SL, BLOCK), BF)


def lists_kernel(flags, lists):
    for n in range(8):
        for t in range(KS):
            lists[n, t] = NONE

    def kept(b, counts):
        for q in range(8):
            i = 8 * b + q
            out = []
            for n in range(8):
                lists[n, counts[n]] = i
                out.append(counts[n] + flags[4 + n, i])
            counts = tuple(out)
        return counts

    counts = lax.fori_loop(0, TR, kept, (jnp.int32(0),) * 8)
    for n in range(8):
        lists[n, counts[n]] = NONE


def fetch(parts, layout, target, sems):
    copies = []
    for part, pieces in zip(parts, layout):
        for start, back, line, at, size in pieces:
            n = len(copies)
            copies.append(pltpu.make_async_copy(part.at[pl.ds(start, size)], target(back, line, at, size), sems.at[n]))
    return copies


def fetch_rows(place, parts, layout, rows, sems):
    x, y = place[0] // 2, place[0] % 2

    def target(back, line, at, size):
        return rows.at[pl.ds(at, size), lax.rem(x - back + 4, 4) * 2 + (y + line) % 2]

    return fetch(parts, layout, target, sems)


def fetch_cols(place, parts, layout, cols, sems):
    z, y, core = place[1] // 4, (place[1] // 2) % 2, place[1] % 2

    def target(back, line, at, size):
        line, other = line % 2, line // 2
        c = lax.rem(z - back + 4, 4) * 4 + ((y + line) % 2) * 2 + (core + other) % 2
        return cols.at[pl.ds(c * PACK + at, size)]

    return fetch(parts, layout, target, sems)


def product(table, outer, inner, cols, right):
    total = None
    for t in range(0, len(inner), 2):
        pair = inner[t : t + 2]
        left = jnp.concatenate(
            [jnp.concatenate([cols[table[k, i]] for k in pair], axis=1) for i in outer], axis=0
        )
        part = jnp.dot(left, right(t, len(pair)), preferred_element_type=jnp.float32)
        total = part if total is None else total + part
    return total


def square_kernel(place, inner, outer, *refs):
    row_parts, col_parts = refs[:NR], refs[NR : NR + NC]
    square, table, rows, cols, marks, index, col_sems, row_sems, sem = refs[NR + NC :]
    from_cols = fetch_cols(place, col_parts, COLS, cols, col_sems)
    from_rows = fetch_rows(place, row_parts, ROWS, rows, row_sems)
    for copy in from_cols + from_rows:
        copy.start()
    for copy in from_cols:
        copy.wait()
    for c in range(TC):
        marks[4 * c : 4 * c + 4, :] = cols[c * PACK + KP].astype(jnp.float32)[0:4]
    kept = marks[...]
    before = lax.broadcasted_iota(jnp.int32, (BLOCK, BLOCK), 0) < lax.broadcasted_iota(jnp.int32, (BLOCK, BLOCK), 1)
    rank = jnp.dot(kept.astype(BF), before.astype(jnp.float32).astype(BF), preferred_element_type=jnp.float32)
    slot = lax.broadcasted_iota(jnp.int32, (NB, BLOCK), 0) * SLOTS + rank.astype(jnp.int32)
    index[0:NB, :] = jnp.where(kept > 0.5, slot, ZERO)
    index[NB : NB + 8, :] = jnp.full((8, BLOCK), ZERO, jnp.int32)
    copy = pltpu.make_async_copy(index, table, sem)
    copy.start()
    copy.wait()
    for copy in from_rows:
        copy.wait()

    def column(j, carry):
        def right(t, n):
            return rows[pl.ds(j * SLOTS + t, n)].reshape(n * BLOCK, BLOCK)

        result = product(table, [outer[j, s] for s in range(KS)], [inner[j, t] for t in range(KP)], cols, right)
        square[pl.ds(j * KS, KS)] = result.astype(BF).reshape(KS, SL, BLOCK)
        return carry

    lax.fori_loop(0, 4, column, 0)


def step_kernel(place, inner, table, *refs):
    row_parts, col_parts = refs[:NS], refs[NS : NS + NC]
    stepped, rows, cols, col_sems, row_sems = refs[NS + NC :]
    copies = fetch_cols(place, col_parts, COLS, cols, col_sems)
    copies += fetch_rows(place, row_parts, SQUARES, rows, row_sems)
    for copy in copies:
        copy.start()
    stepped[...] = jnp.zeros_like(stepped)
    for copy in copies:
        copy.wait()
    for j in range(4):

        def right(t, n):
            return rows[j * KS + t : j * KS + t + n].reshape(n * BLOCK, BLOCK)

        outer = [inner[4 + j, s] for s in range(KT)]
        second = product(table, outer, [inner[j, t] for t in range(KS)], cols, right)
        for s, i in enumerate(outer):
            own = cols[table[place[1] * 4 + j, i]].astype(jnp.float32)
            result = 1.5 * own - 0.5 * second[s * SL : (s + 1) * SL]

            @pl.when(i < NB)
            def _():
                stepped[i, :, j * BLOCK : (j + 1) * BLOCK] = result.astype(BF)


def square_rows_kernel(place, lists, *refs):
    row_parts = refs[:NS]
    out, rows, sems = refs[NS:]
    copies = fetch_rows(place, row_parts, SQUARES, rows, sems)
    for copy in copies:
        copy.start()
    out[...] = jnp.zeros_like(out)
    for copy in copies:
        copy.wait()
    for j in range(4):

        def one(s, carry):
            i = lists[j, s]

            @pl.when(i // 8 == place[0])
            def _():
                out[i % 8, :, :, j * BLOCK : (j + 1) * BLOCK] = rows[j * KS + s]

            return carry

        lax.fori_loop(0, KS, one, 0)


SMEM = pl.BlockSpec(memory_space=pltpu.SMEM)
VMEM = pl.BlockSpec(memory_space=pltpu.VMEM)
ANY = pl.BlockSpec(memory_space=pl.ANY)


def call(kernel, outs, in_specs, out_specs, scratch, flops, moved):
    return pl.pallas_call(
        kernel,
        out_shape=outs,
        in_specs=in_specs,
        out_specs=out_specs,
        scratch_shapes=scratch,
        compiler_params=pltpu.CompilerParams(vmem_limit_bytes=VMEM_LIMIT),
        cost_estimate=pl.CostEstimate(flops=flops, bytes_accessed=moved, transcendentals=0),
    )


def apart(slots):
    half = slots // 2
    whole = [(0, 0), (0, 1), (1, 0), (3, 0), (1, 1), (3, 1)]
    layout = [[(0, back, line, 0, slots)] for back, line in whole]
    return layout + [[(0, 2, line, at, half)] for line in range(2) for at in (0, half)]


def merged(slots):
    half = slots // 2
    layout = [[(0, back, line, 0, slots)] for back, line in [(0, 0), (0, 1), (1, 0), (3, 0)]]
    layout += [[(0, 1, 1, 0, slots), (slots, 2, 0, 0, half)], [(0, 3, 1, 0, slots), (slots, 2, 0, half, half)]]
    return layout + [[(0, 2, 1, 0, half)], [(0, 2, 1, half, half)]]


def merged_cores(slots):
    mine = merged(slots)
    swapped = [mine[0], join(mine[1:4]), mine[4], mine[5], join(mine[6:8])]
    return mine + [[(start, back, line + 2, at, size) for start, back, line, at, size in part] for part in swapped]


def join(parts):
    out, begin = [], 0
    for part in parts:
        out += [(begin + start, back, line, at, size) for start, back, line, at, size in part]
        begin += sum(piece[4] for piece in part)
    return out


def ring_apart(packed, shift):
    half = packed.shape[0] // 2
    other = shift(packed, 0, 1)
    left, right = shift(packed, 1, 0), shift(packed, -1, 0)
    other_left, other_right = shift(other, 1, 0), shift(other, -1, 0)
    far = [shift(left[:half], 1, 0), shift(right[half:], -1, 0)]
    far += [shift(other_left[:half], 1, 0), shift(other_right[half:], -1, 0)]
    return [packed, other, left, right, other_left, other_right] + far


def ring_merged(packed, shift):
    slots = packed.shape[0]
    half = slots // 2
    other = shift(packed, 0, 1)
    left, right = shift(packed, 1, 0), shift(packed, -1, 0)
    from_left = shift(jnp.concatenate([other, left[:half]]), 1, 0)
    from_right = shift(jnp.concatenate([other, right[half:]]), -1, 0)
    far = [shift(from_left[:half], 1, 0), shift(from_right[half:slots], -1, 0)]
    return [packed, other, left, right, from_left, from_right] + far


def gather_rows(packed):
    return ring_apart(packed, row_shift)


def gather_cols(packed):
    mine = ring_merged(packed, lambda value, dz, dy: col_shift(value, dz, dy, 0))
    own = [mine[0], jnp.concatenate(mine[1:4]), mine[4], mine[5], jnp.concatenate(mine[6:8])]
    return mine + [col_shift(part, 0, 0, 1) for part in own]


ROWS = merged(PACK)
COLS = merged_cores(PACK)
SQUARES = apart(4 * KS)
NR, NC, NS = len(ROWS), len(COLS), len(SQUARES)


def pieces(layout):
    return sum(len(part) for part in layout)


def on_device(density, pattern, square_filter, step_filter):
    place = jnp.stack([lax.axis_index("row"), lax.axis_index("col")]).astype(jnp.int32)
    sent = call(
        slice_kernel,
        jax.ShapeDtypeStruct((TR, 9, SL, 4 * BLOCK), BF),
        [ANY] * 4,
        VMEM,
        [pltpu.VMEM((SL, BLOCK), jnp.float32), pltpu.VMEM((3, 4, 8), jnp.int32), pltpu.SemaphoreType.DMA((TR + 3,))],
        0,
        2 << 20,
    )(density.reshape(8, TR, SL, 4 * BLOCK), pattern.T, square_filter.T, step_filter.T)
    sliced = lax.all_to_all(sent, "row", 0, 0, tiled=True)

    packed, pattern_lists, flags = call(
        pack_kernel,
        (
            jax.ShapeDtypeStruct((PACK, SL, BLOCK), BF),
            jax.ShapeDtypeStruct((4, 32), jnp.int32),
            jax.ShapeDtypeStruct((SL, BLOCK), jnp.int32),
        ),
        [VMEM],
        (VMEM, SMEM, VMEM),
        [pltpu.SMEM((SL, BLOCK), jnp.int32), pltpu.SemaphoreType.DMA],
        0,
        2 << 20,
    )(sliced)
    lists = call(lists_kernel, jax.ShapeDtypeStruct((8, 32), jnp.int32), [SMEM], SMEM, [], 0, 1 << 14)(flags)

    row_parts = ring_merged(packed, row_shift)
    col_parts = gather_cols(packed)
    square_packed, table = call(
        square_kernel,
        (
            jax.ShapeDtypeStruct((4 * KS, SL, BLOCK), BF),
            jax.ShapeDtypeStruct((NB + 8, BLOCK), jnp.int32),
        ),
        [SMEM] * 3 + [ANY] * (NR + NC),
        (VMEM, SMEM),
        [
            pltpu.VMEM((PACK, TR, SL, BLOCK), BF),
            pltpu.VMEM((TC * PACK, SL, BLOCK), BF),
            pltpu.VMEM((NB, BLOCK), jnp.float32),
            pltpu.VMEM((NB + 8, BLOCK), jnp.int32),
            pltpu.SemaphoreType.DMA((pieces(COLS),)),
            pltpu.SemaphoreType.DMA((pieces(ROWS),)),
            pltpu.SemaphoreType.DMA,
        ],
        2 * 4 * KS * SL * KP * BLOCK * BLOCK,
        8 << 20,
    )(place, pattern_lists, lists, *row_parts, *col_parts)

    square_parts = gather_rows(square_packed)
    stepped = call(
        step_kernel,
        jax.ShapeDtypeStruct((NB, SL, 4 * BLOCK), BF),
        [SMEM] * 3 + [ANY] * (NS + NC),
        VMEM,
        [
            pltpu.VMEM((4 * KS, TR, SL, BLOCK), BF),
            pltpu.VMEM((TC * PACK, SL, BLOCK), BF),
            pltpu.SemaphoreType.DMA((pieces(COLS),)),
            pltpu.SemaphoreType.DMA((pieces(SQUARES),)),
        ],
        2 * 4 * KT * SL * KS * BLOCK * BLOCK,
        9 << 20,
    )(place, lists, table, *square_parts, *col_parts)
    back = lax.all_to_all(stepped, "row", 0, 0, tiled=True)
    square = call(
        square_rows_kernel,
        jax.ShapeDtypeStruct((8, TR, SL, 4 * BLOCK), BF),
        [SMEM, SMEM] + [ANY] * NS,
        VMEM,
        [pltpu.VMEM((4 * KS, TR, SL, BLOCK), BF), pltpu.SemaphoreType.DMA((pieces(SQUARES),))],
        0,
        4 << 20,
    )(place, lists, *square_parts)
    square = square.reshape(8 * BLOCK, 4 * BLOCK)
    stepped = back.reshape(TR, 8, SL, 4 * BLOCK).transpose(1, 0, 2, 3).reshape(8 * BLOCK, 4 * BLOCK)
    return square, stepped


def solution(mesh):
    placed = (P("row", "col"),) * 4
    return jax.shard_map(
        on_device,
        mesh=mesh,
        in_specs=placed,
        out_specs=(P("row", "col"), P("row", "col")),
        check_vma=False,
    )
```

time: 190 us -> 150 us (0.79)
  waiting for transfers between devices: 116 us -> 44.2 us
  blocking collectives: 0 us -> 22.5 us
  starting transfers between devices: 26.6 us -> 36.3 us
    ppermute x8 -> x16, waiting for transfers between devices: 58.6 us -> 24 us  [row_shift(): return lax.ppermute(value, 'row', pairs)]
    all_to_all x0 -> x1, blocking collectives: none -> 22.5 us  [on_device(): sliced = lax.all_to_all(sent, 'row', 0, 0, tiled=True)]
    all_to_all x1 -> x0, waiting for transfers between devices: 17.8 us -> none  [on_device(): sliced = lax.all_to_all(sent, 'row', 0, 0, tiled=True)]
    ppermute x8 -> x12, waiting for transfers between devices: 27 us -> 14.6 us  [col_shift(): return lax.ppermute(value, 'col', pairs)]
    ppermute x8 -> x16, starting transfers between devices: 8.18 us -> 19.9 us  [row_shift(): return lax.ppermute(value, 'row', pairs)]
    all_to_all x1, waiting for transfers between devices: 12.3 us -> 5.53 us  [on_device(): back = lax.all_to_all(stepped, 'row', 0, 0, tiled=True)]
    all_to_all x1 -> x0, starting transfers between devices: 5.4 us -> none  [on_device(): sliced = lax.all_to_all(sent, 'row', 0, 0, tiled=True)]
    ppermute x8 -> x12, starting transfers between devices: 8.79 us -> 12.8 us  [col_shift(): return lax.ppermute(value, 'col', pairs)]
  transfers between devices with their start and end apart: 18 -> 29, of which waited for: 12 -> 18; matrix products, arithmetic and copies ran while one was open for 0% -> 2% of each run, Pallas kernels for 2% -> 6%
where the time goes in v2:
time: 150 us; the launch traced here: 148 us
  waiting for transfers between devices  44.2 us (29%)
  Pallas kernels  37.9 us (25%)
  starting transfers between devices  36.3 us (24%)
  blocking collectives  22.5 us (15%)
  local copies, waits for them, and re-layouts  3.82 us (3%)
  other arithmetic  2.47 us (2%)
    ppermute x16, waiting for transfers between devices, row_shift(): return lax.ppermute(value, 'row', pairs)  24 us
    all_to_all x1, blocking collectives, on_device(): sliced = lax.all_to_all(sent, 'row', 0, 0, tiled=True)  22.5 us
    ppermute x16, starting transfers between devices, row_shift(): return lax.ppermute(value, 'row', pairs)  19.9 us
    ppermute x12, waiting for transfers between devices, col_shift(): return lax.ppermute(value, 'col', pairs)  14.6 us
    ppermute x12, starting transfers between devices, col_shift(): return lax.ppermute(value, 'col', pairs)  12.8 us
    pallas_call x1, Pallas kernels, on_device(): call(step_kernel, jax.ShapeDtypeStruct((NB, SL, 4 * BLOCK), BF), [SMEM] *...  12.5 us
    pallas_call x1, Pallas kernels, on_device(): call(square_kernel, (jax.ShapeDtypeStruct((4 * KS, SL, BLOCK), BF), jax.S...  10.1 us
    pallas_call x1, Pallas kernels, on_device(): call(square_rows_kernel, jax.ShapeDtypeStruct((8, TR, SL, 4 * BLOCK), BF)...  5.86 us
  transfers between devices with their start and end apart: 29, of which 18 were waited for; matrix products, arithmetic and copies ran while one was open for 2% of the time, Pallas kernels for 6%

profile of v2, /device:TPU:0, one launch (start us, length us, event | category | flops | bytes accessed | tf_op | source)
XLA Modules:
  0.0 148.1 jit_solution(10511777647940420916)
XLA Ops:
  0.6 2.5 %shard_map.59 = bf16[8,9,16,512]{3,2,1,0:T(8,128)(2,1)} custom-call(bf16[8,8,16,512]{3,2,1,0:T(8,128)(2,1)} %bitcast.12, s32[4,8]{1,0:T(4,128)} %bitcast.15, s32[4,8]{1,0:T(4,128)} %bitcast.16, s32[4,8]{1,0:T(4,128)} %bitcast.17), custom_call_target="tpu_custom_call" | custom-call | bytes 2097152 | tf_op jit(solution)/shard_map/pallas_call | solution.py:331
  3.1 22.5 %all_to_all.10.sliced = bf16[8,9,16,512]{3,2,1,0:T(8,128)(2,1)} all-to-all(bf16[8,9,16,512]{3,2,1,0:T(8,128)(2,1)} %shard_map.59), channel_id=1, replica_groups=mesh['row'=8,'col'=16] {'row'}, dimensions={0} | all-to-all | bytes 2359296 | tf_op jit(solution)/shard_map/all_to_all | solution.py:340
  25.6 3.9 %shard_map.60 = (bf16[72,16,128]{2,1,0:T(8,128)(2,1)}, s32[4,32]{1,0:T(4,128)}, s32[16,128]{1,0:T(8,128)}) custom-call(bf16[8,9,16,512]{3,2,1,0:T(8,128)(2,1)} %all_to_all.10.sliced), custom_call_target="tpu_custom_call" | custom-call | bytes 2097152 | tf_op jit(solution)/shard_map/pallas_call | solution.py:342
  29.5 4.1 %collective-permute-start.9 = (bf16[72,16,128]{2,1,0:T(8,128)(2,1)}, bf16[72,16,128]{2,1,0:T(8,128)(2,1)S(1)}, u32[]{:S(2)}, u32[]{:S(2)}) collective-permute-start(bf16[72,16,128]{2,1,0:T(8,128)(2,1)} %get-tuple-element.9.refs_0_.refs_8_.refs_10_), channel_id=1, source_target_pairs={{0,12},{1,13},{2,14},{3,15},{4,0},{5,1},{6,2},{7,3},{8,4},{9,5},{1... | collective-permute-start | bytes 884744 | tf_op jit(solution)/shard_map/ppermute | solution.py:44
  33.6 2.9 %collective-permute-start.7 = (bf16[72,16,128]{2,1,0:T(8,128)(2,1)}, bf16[72,16,128]{2,1,0:T(8,128)(2,1)S(1)}, u32[]{:S(2)}, u32[]{:S(2)}) collective-permute-start(bf16[72,16,128]{2,1,0:T(8,128)(2,1)} %get-tuple-element.9.refs_0_.refs_8_.refs_10_), channel_id=1, source_target_pairs={{0,2},{1,3},{2,0},{3,1},{4,6},{5,7},{6,4},{7,5},{8,10},{9,11},{10,... | collective-permute-start | bytes 884744 | tf_op jit(solution)/shard_map/ppermute | solution.py:44
  36.5 1.2 collective-permute-start.2
  37.7 0.9 collective-permute-start.1
  38.5 0.1 collective-permute-done.9.refs_11_.refs_13_
  38.6 1.1 collective-permute-start
  39.8 2.2 %collective-permute-done.8.refs_10_.refs_12_ = bf16[72,16,128]{2,1,0:T(8,128)(2,1)S(1)} collective-permute-done((bf16[72,16,128]{2,1,0:T(8,128)(2,1)}, bf16[72,16,128]{2,1,0:T(8,128)(2,1)S(1)}, u32[]{:S(2)}, u32[]{:S(2)}) %collective-permute-start.8) | collective-permute-done | bytes 294944 | tf_op jit(solution)/shard_map/ppermute | solution.py:44
  42.0 2.3 %collective-permute-done.7.refs_9_.refs_11_ = bf16[72,16,128]{2,1,0:T(8,128)(2,1)S(1)} collective-permute-done((bf16[72,16,128]{2,1,0:T(8,128)(2,1)}, bf16[72,16,128]{2,1,0:T(8,128)(2,1)S(1)}, u32[]{:S(2)}, u32[]{:S(2)}) %collective-permute-start.7) | collective-permute-done | bytes 294944 | tf_op jit(solution)/shard_map/ppermute | solution.py:44
  44.3 0.1 pad_maximum_fusion.3
  44.3 3.1 %collective-permute-start.11 = (bf16[108,16,128]{2,1,0:T(8,128)(2,1)S(1)}, bf16[108,16,128]{2,1,0:T(8,128)(2,1)S(1)}, u32[]{:S(2)}, u32[]{:S(2)}) collective-permute-start(bf16[108,16,128]{2,1,0:T(8,128)(2,1)S(1)} %get-tuple-element.12), channel_id=1, source_target_pairs={{0,12},{1,13},{2,14},{3,15},{4,0},{5,1},{6,2},{7,3},{8,4},{9,5},{1... | collective-permute-start | bytes 1327112 | tf_op jit(solution)/shard_map/ppermute | solution.py:44
  47.5 0.0 collective-permute-start.10
  47.6 0.9 collective-permute-done.refs_1_
  48.5 0.1 pad_maximum_fusion.1
  48.5 1.2 collective-permute-start.4
  49.8 1.0 pad_maximum_fusion
  50.8 0.5 collective-permute-start.14
  51.3 2.0 %collective-permute-done.11.refs_13_.refs_15_ = bf16[108,16,128]{2,1,0:T(8,128)(2,1)S(1)} collective-permute-done((bf16[108,16,128]{2,1,0:T(8,128)(2,1)S(1)}, bf16[108,16,128]{2,1,0:T(8,128)(2,1)S(1)}, u32[]{:S(2)}, u32[]{:S(2)}) %collective-permute-start.11) | collective-permute-done | bytes 442400 | tf_op jit(solution)/shard_map/ppermute | solution.py:44
  53.3 0.1 collective-permute-start.3
  53.4 3.6 %collective-permute-done.10.refs_12_.refs_14_ = bf16[108,16,128]{2,1,0:T(8,128)(2,1)S(1)} collective-permute-done((bf16[108,16,128]{2,1,0:T(8,128)(2,1)S(1)}, bf16[108,16,128]{2,1,0:T(8,128)(2,1)S(1)}, u32[]{:S(2)}, u32[]{:S(2)}) %collective-permute-start.10) | collective-permute-done | bytes 442400 | tf_op jit(solution)/shard_map/ppermute | solution.py:44
  57.0 0.2 collective-permute-start.13
  57.2 1.9 %collective-permute-start.12 = (bf16[36,16,128]{2,1,0:T(8,128)(2,1)S(1)}, bf16[36,16,128]{2,1,0:T(8,128)(2,1)S(1)}, u32[]{:S(2)}, u32[]{:S(2)}) collective-permute-start(bf16[36,16,128]{2,1,0:T(8,128)(2,1)S(1)} %slice.54), channel_id=1, source_target_pairs={{0,4},{1,5},{2,6},{3,7},{4,8},{5,9},{6,10},{7,11},{8,12},{9,13},{1... | collective-permute-start | bytes 442376 | tf_op jit(solution)/shard_map/ppermute | solution.py:44
  59.1 0.1 collective-permute-start.17
  59.2 2.9 %collective-permute-done.13.refs_15_.refs_17_ = bf16[36,16,128]{2,1,0:T(8,128)(2,1)S(1)} collective-permute-done((bf16[36,16,128]{2,1,0:T(8,128)(2,1)S(1)}, bf16[36,16,128]{2,1,0:T(8,128)(2,1)S(1)}, u32[]{:S(2)}, u32[]{:S(2)}) %collective-permute-start.13) | collective-permute-done | bytes 147488 | tf_op jit(solution)/shard_map/ppermute | solution.py:44
  62.2 1.5 collective-permute-done.12.refs_14_.refs_16_
  63.6 3.2 %collective-permute-start.6 = (bf16[36,16,128]{2,1,0:T(8,128)(2,1)S(1)}, bf16[36,16,128]{2,1,0:T(8,128)(2,1)S(1)}, u32[]{:S(2)}, u32[]{:S(2)}) collective-permute-start(bf16[36,16,128]{2,1,0:T(8,128)(2,1)S(1)} %slice.51), channel_id=1, source_target_pairs={{0,96},{16,112},{32,0},{48,16},{64,32},{80,48},{96,64},{112,80},{1... | collective-permute-start | bytes 442376 | tf_op jit(solution)/shard_map/ppermute | solution.py:34
  66.8 0.7 pad_maximum_fusion.5
  67.6 0.8 copy-done.23
  68.3 1.1 collective-permute-done.6.refs_7_
  69.5 0.8 collective-permute-start.5
  70.3 0.6 pad_add_fusion.place
  70.9 3.0 %shard_map.61.outer.lists.inner = s32[8,32]{1,0:T(8,128)} custom-call(s32[16,128]{1,0:T(8,128)} %get-tuple-element.7.flags), custom_call_target="tpu_custom_call" | custom-call | bytes 16384 | tf_op jit(solution)/shard_map/pallas_call | solution.py:355
  73.9 2.4 %collective-permute-done.5.refs_6_ = bf16[36,16,128]{2,1,0:T(8,128)(2,1)S(1)} collective-permute-done((bf16[36,16,128]{2,1,0:T(8,128)(2,1)S(1)}, bf16[36,16,128]{2,1,0:T(8,128)(2,1)S(1)}, u32[]{:S(2)}, u32[]{:S(2)}) %collective-permute-start.5) | collective-permute-done | bytes 147488 | tf_op jit(solution)/shard_map/ppermute | solution.py:34
  76.3 0.0 copy-start.3
  76.4 0.6 copy-done.27
  76.9 0.2 copy-done.11
  77.1 0.1 copy-done.12
  77.3 0.3 copy-done.3
  77.5 10.1 %shard_map.62 = (bf16[100,16,128]{2,1,0:T(8,128)(2,1)}, s32[72,128]{1,0:T(8,128)}) custom-call(s32[2]{0:T(128)} %pad_add_fusion.place, s32[4,32]{1,0:T(4,128)} %get-tuple-element.8.inner, s32[8,32]{1,0:T(8,128)} %shard_map.61.outer.lists.inner, bf16[72,16,128]{2,1,0:T(8,128)(2,1)} %get-tuple-element.9.refs_0_.refs_8_.refs_10_, ...), custom_call_target="tpu_custom_call" | custom-call | flops 891289600 | bytes 8388608 | tf_op jit(solution)/shard_map/pallas_call | solution.py:359
  87.6 0.7 collective-permute-start.19
  88.3 2.0 %collective-permute-start.21 = (bf16[100,16,128]{2,1,0:T(8,128)(2,1)}, bf16[100,16,128]{2,1,0:T(8,128)(2,1)S(1)}, u32[]{:S(2)}, u32[]{:S(2)}) collective-permute-start(bf16[100,16,128]{2,1,0:T(8,128)(2,1)} %get-tuple-element.10.refs_0_), channel_id=1, source_target_pairs={{0,96},{16,112},{32,0},{48,16},{64,32},{80,48},{96,64},{112,80},{1... | collective-permute-start | bytes 1228808 | tf_op jit(solution)/shard_map/ppermute | solution.py:34
  90.3 0.0 collective-permute-start.20
  90.3 6.1 %collective-permute-done.19.refs_1_ = bf16[100,16,128]{2,1,0:T(8,128)(2,1)S(1)} collective-permute-done((bf16[100,16,128]{2,1,0:T(8,128)(2,1)}, bf16[100,16,128]{2,1,0:T(8,128)(2,1)S(1)}, u32[]{:S(2)}, u32[]{:S(2)}) %collective-permute-start.19) | collective-permute-done | bytes 409632 | tf_op jit(solution)/shard_map/ppermute | solution.py:34
  96.4 1.5 %collective-permute-start.23 = (bf16[100,16,128]{2,1,0:T(8,128)(2,1)S(1)}, bf16[100,16,128]{2,1,0:T(8,128)(2,1)S(1)}, u32[]{:S(2)}, u32[]{:S(2)}) collective-permute-start(bf16[100,16,128]{2,1,0:T(8,128)(2,1)S(1)} %collective-permute-done.19.refs_1_), channel_id=1, source_target_pairs={{0,96},{16,112},{32,0},{48,16},{64,32},{80,48},{96,64},{112,80},{1... | collective-permute-start | bytes 1228808 | tf_op jit(solution)/shard_map/ppermute | solution.py:34
  97.9 0.5 collective-permute-start.22
  98.4 0.3 collective-permute-done.21.refs_3_
  98.7 3.7 %collective-permute-start.25 = (bf16[50,16,128]{2,1,0:T(8,128)(2,1)S(1)}, bf16[50,16,128]{2,1,0:T(8,128)(2,1)S(1)}, u32[]{:S(2)}, u32[]{:S(2)}) collective-permute-start(bf16[50,16,128]{2,1,0:T(8,128)(2,1)S(1)} %slice.57), channel_id=1, source_target_pairs={{0,96},{16,112},{32,0},{48,16},{64,32},{80,48},{96,64},{112,80},{1... | collective-permute-start | bytes 614408 | tf_op jit(solution)/shard_map/ppermute | solution.py:34
  102.3 0.2 collective-permute-done.20.refs_2_
  102.5 0.1 collective-permute-start.24
  102.6 6.1 %collective-permute-done.23.refs_5_ = bf16[100,16,128]{2,1,0:T(8,128)(2,1)S(1)} collective-permute-done((bf16[100,16,128]{2,1,0:T(8,128)(2,1)S(1)}, bf16[100,16,128]{2,1,0:T(8,128)(2,1)S(1)}, u32[]{:S(2)}, u32[]{:S(2)}) %collective-permute-start.23) | collective-permute-done | bytes 409632 | tf_op jit(solution)/shard_map/ppermute | solution.py:34
  108.8 3.0 %collective-permute-start.27 = (bf16[50,16,128]{2,1,0:T(8,128)(2,1)S(1)}, bf16[50,16,128]{2,1,0:T(8,128)(2,1)S(1)}, u32[]{:S(2)}, u32[]{:S(2)}) collective-permute-start(bf16[50,16,128]{2,1,0:T(8,128)(2,1)S(1)} %slice.59), channel_id=1, source_target_pairs={{0,96},{16,112},{32,0},{48,16},{64,32},{80,48},{96,64},{112,80},{1... | collective-permute-start | bytes 614408 | tf_op jit(solution)/shard_map/ppermute | solution.py:34
  111.8 0.1 collective-permute-start.26
  111.9 0.1 collective-permute-done.25.refs_7_
  112.0 3.0 %collective-permute-done.24.refs_6_ = bf16[50,16,128]{2,1,0:T(8,128)(2,1)S(1)} collective-permute-done((bf16[50,16,128]{2,1,0:T(8,128)(2,1)S(1)}, bf16[50,16,128]{2,1,0:T(8,128)(2,1)S(1)}, u32[]{:S(2)}, u32[]{:S(2)}) %collective-permute-start.24) | collective-permute-done | bytes 204832 | tf_op jit(solution)/shard_map/ppermute | solution.py:34
  115.0 0.0 collective-permute-done.27.refs_9_
  115.0 3.8 %collective-permute-done.26.refs_8_ = bf16[50,16,128]{2,1,0:T(8,128)(2,1)S(1)} collective-permute-done((bf16[50,16,128]{2,1,0:T(8,128)(2,1)S(1)}, bf16[50,16,128]{2,1,0:T(8,128)(2,1)S(1)}, u32[]{:S(2)}, u32[]{:S(2)}) %collective-permute-start.26) | collective-permute-done | bytes 204832 | tf_op jit(solution)/shard_map/ppermute | solution.py:34
  118.9 0.6 copy-done.21
  119.5 12.5 %shard_map.64 = bf16[64,16,512]{2,1,0:T(8,128)(2,1)} custom-call(s32[2]{0:T(128)} %pad_add_fusion.place, s32[8,32]{1,0:T(8,128)} %shard_map.61.outer.lists.inner, s32[72,128]{1,0:T(8,128)} %get-tuple-element.11.table, bf16[100,16,128]{2,1,0:T(8,128)(2,1)} %get-tuple-element.10.refs_0_, bf16[100,16,128]{2,1,0:T(8,128)(2,1)} %copy-done.13, ...), custom_call_target="tpu_custom_call" | custom-call | flops 1101004800 | bytes 9437184 | tf_op jit(solution)/shard_map/pallas_call | solution.py:381
  132.0 3.6 %all-to-all-start.1 = ((bf16[64,16,512]{2,1,0:T(8,128)(2,1)}), bf16[64,16,512]{2,1,0:T(8,128)(2,1)S(1)}, u32[]{:S(2)}, u32[]{:S(2)}) async-start(bf16[64,16,512]{2,1,0:T(8,128)(2,1)} %shard_map.64), calls=%async_computation.1 | async-start | bytes 2097152 | tf_op jit(solution)/shard_map/all_to_all | solution.py:395
  135.6 5.9 %shard_map.63 = bf16[8,8,16,512]{3,2,1,0:T(8,128)(2,1)} custom-call(s32[2]{0:T(128)} %pad_add_fusion.place, s32[8,32]{1,0:T(8,128)} %shard_map.61.outer.lists.inner, bf16[100,16,128]{2,1,0:T(8,128)(2,1)} %get-tuple-element.10.refs_0_, bf16[100,16,128]{2,1,0:T(8,128)(2,1)} %copy-done.13, bf16[100,16,128]{2,1,0:T(8,128)(2,1)} %copy-done.6, ...), custom_call_target="tpu_custom_call" | custom-call | bytes 4194304 | tf_op jit(solution)/shard_map/pallas_call | solution.py:396
  141.5 5.5 %all-to-all-done.1 = bf16[64,16,512]{2,1,0:T(8,128)(2,1)S(1)} async-done(((bf16[64,16,512]{2,1,0:T(8,128)(2,1)}), bf16[64,16,512]{2,1,0:T(8,128)(2,1)S(1)}, u32[]{:S(2)}, u32[]{:S(2)}) %all-to-all-start.1) | async-done | bytes 1048608 | tf_op jit(solution)/shard_map/all_to_all | solution.py:395
  147.0 1.1 copy.6
  (75 shorter events, 0.3 us)
Async XLA Ops:
  29.5 9.2 %collective-permute-start.9 = (bf16[72,16,128]{2,1,0:T(8,128)(2,1)}, bf16[72,16,128]{2,1,0:T(8,128)(2,1)S(1)}, u32[]{:S(2)}, u32[]{:S(2)}) collective-permute-start(bf16[72,16,128]{2,1,0:T(8,128)(2,1)} %get-tuple-element.9.refs_0_.refs_8_.refs_10_), channel_id=1, source_target_pairs={{0,12},{1,13},{2,14},{3,15},{4,0},{5,1},{6,2},{7,3},{8,4},{9,5},{1... | collective-permute-start | bytes 884744 | tf_op jit(solution)/shard_map/ppermute | solution.py:44
  33.6 8.4 %collective-permute-start.8 = (bf16[72,16,128]{2,1,0:T(8,128)(2,1)}, bf16[72,16,128]{2,1,0:T(8,128)(2,1)S(1)}, u32[]{:S(2)}, u32[]{:S(2)}) collective-permute-start(bf16[72,16,128]{2,1,0:T(8,128)(2,1)} %get-tuple-element.9.refs_0_.refs_8_.refs_10_), channel_id=1, source_target_pairs={{0,4},{1,5},{2,6},{3,7},{4,8},{5,9},{6,10},{7,11},{8,12},{9,13},{1... | collective-permute-start | bytes 884744 | tf_op jit(solution)/shard_map/ppermute | solution.py:44
  33.6 10.7 %collective-permute-start.7 = (bf16[72,16,128]{2,1,0:T(8,128)(2,1)}, bf16[72,16,128]{2,1,0:T(8,128)(2,1)S(1)}, u32[]{:S(2)}, u32[]{:S(2)}) collective-permute-start(bf16[72,16,128]{2,1,0:T(8,128)(2,1)} %get-tuple-element.9.refs_0_.refs_8_.refs_10_), channel_id=1, source_target_pairs={{0,2},{1,3},{2,0},{3,1},{4,6},{5,7},{6,4},{7,5},{8,10},{9,11},{10,... | collective-permute-start | bytes 884744 | tf_op jit(solution)/shard_map/ppermute | solution.py:44
  36.5 11.0 %collective-permute-start.2 = (bf16[72,16,128]{2,1,0:T(8,128)(2,1)}, bf16[72,16,128]{2,1,0:T(8,128)(2,1)S(1)}, u32[]{:S(2)}, u32[]{:S(2)}) collective-permute-start(bf16[72,16,128]{2,1,0:T(8,128)(2,1)} %get-tuple-element.9.refs_0_.refs_8_.refs_10_), channel_id=1, source_target_pairs={{0,96},{16,112},{32,0},{48,16},{64,32},{80,48},{96,64},{112,80},{1... | collective-permute-start | bytes 884744 | tf_op jit(solution)/shard_map/ppermute | solution.py:34
  37.7 9.9 %collective-permute-start.1 = (bf16[72,16,128]{2,1,0:T(8,128)(2,1)}, bf16[72,16,128]{2,1,0:T(8,128)(2,1)S(1)}, u32[]{:S(2)}, u32[]{:S(2)}) collective-permute-start(bf16[72,16,128]{2,1,0:T(8,128)(2,1)} %get-tuple-element.9.refs_0_.refs_8_.refs_10_), channel_id=1, source_target_pairs={{0,32},{16,48},{32,64},{48,80},{64,96},{80,112},{96,0},{112,16},{1... | collective-permute-start | bytes 884744 | tf_op jit(solution)/shard_map/ppermute | solution.py:34
  38.6 11.1 %copy-start.1 = (bf16[72,16,128]{2,1,0:T(8,128)(2,1)}, bf16[72,16,128]{2,1,0:T(8,128)(2,1)S(1)}, u32[]{:S(2)}) copy-start(bf16[72,16,128]{2,1,0:T(8,128)(2,1)S(1)} %collective-permute-done.9.refs_11_.refs_13_) | copy-start | bytes 884740
  38.6 9.8 %collective-permute-start = (bf16[72,16,128]{2,1,0:T(8,128)(2,1)}, bf16[72,16,128]{2,1,0:T(8,128)(2,1)S(1)}, u32[]{:S(2)}, u32[]{:S(2)}) collective-permute-start(bf16[72,16,128]{2,1,0:T(8,128)(2,1)} %get-tuple-element.9.refs_0_.refs_8_.refs_10_), channel_id=1, source_target_pairs={{0,16},{16,0},{32,48},{48,32},{64,80},{80,64},{96,112},{112,96},{1... | collective-permute-start | bytes 884744 | tf_op jit(solution)/shard_map/ppermute | solution.py:34
  42.0 7.8 %copy-start.2 = (bf16[72,16,128]{2,1,0:T(8,128)(2,1)}, bf16[72,16,128]{2,1,0:T(8,128)(2,1)S(1)}, u32[]{:S(2)}) copy-start(bf16[72,16,128]{2,1,0:T(8,128)(2,1)S(1)} %collective-permute-done.8.refs_10_.refs_12_) | copy-start | bytes 884740
  44.3 5.5 %copy-start = (bf16[72,16,128]{2,1,0:T(8,128)(2,1)}, bf16[72,16,128]{2,1,0:T(8,128)(2,1)S(1)}, u32[]{:S(2)}) copy-start(bf16[72,16,128]{2,1,0:T(8,128)(2,1)S(1)} %collective-permute-done.7.refs_9_.refs_11_) | copy-start | bytes 884740
  44.3 9.0 %collective-permute-start.11 = (bf16[108,16,128]{2,1,0:T(8,128)(2,1)S(1)}, bf16[108,16,128]{2,1,0:T(8,128)(2,1)S(1)}, u32[]{:S(2)}, u32[]{:S(2)}) collective-permute-start(bf16[108,16,128]{2,1,0:T(8,128)(2,1)S(1)} %get-tuple-element.12), channel_id=1, source_target_pairs={{0,12},{1,13},{2,14},{3,15},{4,0},{5,1},{6,2},{7,3},{8,4},{9,5},{1... | collective-permute-start | bytes 1327112 | tf_op jit(solution)/shard_map/ppermute | solution.py:44
  47.5 9.5 %collective-permute-start.10 = (bf16[108,16,128]{2,1,0:T(8,128)(2,1)S(1)}, bf16[108,16,128]{2,1,0:T(8,128)(2,1)S(1)}, u32[]{:S(2)}, u32[]{:S(2)}) collective-permute-start(bf16[108,16,128]{2,1,0:T(8,128)(2,1)S(1)} %get-tuple-element.13), channel_id=1, source_target_pairs={{0,4},{1,5},{2,6},{3,7},{4,8},{5,9},{6,10},{7,11},{8,12},{9,13},{1... | collective-permute-start | bytes 1327112 | tf_op jit(solution)/shard_map/ppermute | solution.py:44
  47.5 1.0 copy-start.24
  47.5 3.3 %copy-start.25 = (bf16[72,16,128]{2,1,0:T(8,128)(2,1)}, bf16[72,16,128]{2,1,0:T(8,128)(2,1)S(1)}, u32[]{:S(2)}) copy-start(bf16[72,16,128]{2,1,0:T(8,128)(2,1)S(1)} %collective-permute-done.1.refs_2_) | copy-start | bytes 884740
  48.5 1.3 copy-start.16
  48.5 2.3 %copy-start.4 = (bf16[72,16,128]{2,1,0:T(8,128)(2,1)S(1)}, bf16[72,16,128]{2,1,0:T(8,128)(2,1)}, u32[]{:S(2)}) copy-start(bf16[72,16,128]{2,1,0:T(8,128)(2,1)} %get-tuple-element.9.refs_0_.refs_8_.refs_10_) | copy-start | bytes 884740
  48.5 10.6 %collective-permute-start.4 = (bf16[108,16,128]{2,1,0:T(8,128)(2,1)S(1)}, bf16[108,16,128]{2,1,0:T(8,128)(2,1)S(1)}, u32[]{:S(2)}, u32[]{:S(2)}) collective-permute-start(bf16[108,16,128]{2,1,0:T(8,128)(2,1)S(1)} %get-tuple-element.14), channel_id=1, source_target_pairs={{0,96},{16,112},{32,0},{48,16},{64,32},{80,48},{96,64},{112,80},{1... | collective-permute-start | bytes 1327112 | tf_op jit(solution)/shard_map/ppermute | solution.py:34
  50.8 25.5 %collective-permute-start.15 = (bf16[216,16,128]{2,1,0:T(8,128)(2,1)}, bf16[216,16,128]{2,1,0:T(8,128)(2,1)S(1)}, u32[]{:S(2)}, u32[]{:S(2)}) collective-permute-start(bf16[216,16,128]{2,1,0:T(8,128)(2,1)} %pad_maximum_fusion), channel_id=1, source_target_pairs={{0,1},{1,0},{2,3},{3,2},{4,5},{5,4},{6,7},{7,6},{8,9},{9,8},{10,11... | collective-permute-start | bytes 2654216 | tf_op jit(solution)/shard_map/ppermute | solution.py:44
  50.8 6.4 %collective-permute-start.14 = (bf16[72,16,128]{2,1,0:T(8,128)(2,1)S(1)}, bf16[72,16,128]{2,1,0:T(8,128)(2,1)S(1)}, u32[]{:S(2)}, u32[]{:S(2)}) collective-permute-start(bf16[72,16,128]{2,1,0:T(8,128)(2,1)S(1)} %copy-done.4), channel_id=1, source_target_pairs={{0,1},{1,0},{2,3},{3,2},{4,5},{5,4},{6,7},{7,6},{8,9},{9,8},{10,11... | collective-permute-start | bytes 884744 | tf_op jit(solution)/shard_map/ppermute | solution.py:44
  53.3 23.0 %copy-start.9 = (bf16[108,16,128]{2,1,0:T(8,128)(2,1)}, bf16[108,16,128]{2,1,0:T(8,128)(2,1)S(1)}, u32[]{:S(2)}) copy-start(bf16[108,16,128]{2,1,0:T(8,128)(2,1)S(1)} %collective-permute-done.11.refs_13_.refs_15_) | copy-start | bytes 1327108
  53.3 14.2 %collective-permute-start.3 = (bf16[108,16,128]{2,1,0:T(8,128)(2,1)S(1)}, bf16[108,16,128]{2,1,0:T(8,128)(2,1)S(1)}, u32[]{:S(2)}, u32[]{:S(2)}) collective-permute-start(bf16[108,16,128]{2,1,0:T(8,128)(2,1)S(1)} %get-tuple-element.15), channel_id=1, source_target_pairs={{0,32},{16,48},{32,64},{48,80},{64,96},{80,112},{96,0},{112,16},{1... | collective-permute-start | bytes 1327112 | tf_op jit(solution)/shard_map/ppermute | solution.py:34
  57.0 19.4 %copy-start.10 = (bf16[108,16,128]{2,1,0:T(8,128)(2,1)}, bf16[108,16,128]{2,1,0:T(8,128)(2,1)S(1)}, u32[]{:S(2)}) copy-start(bf16[108,16,128]{2,1,0:T(8,128)(2,1)S(1)} %collective-permute-done.10.refs_12_.refs_14_) | copy-start | bytes 1327108
  57.0 5.1 %collective-permute-start.13 = (bf16[36,16,128]{2,1,0:T(8,128)(2,1)S(1)}, bf16[36,16,128]{2,1,0:T(8,128)(2,1)S(1)}, u32[]{:S(2)}, u32[]{:S(2)}) collective-permute-start(bf16[36,16,128]{2,1,0:T(8,128)(2,1)S(1)} %slice.55), channel_id=1, source_target_pairs={{0,12},{1,13},{2,14},{3,15},{4,0},{5,1},{6,2},{7,3},{8,4},{9,5},{1... | collective-permute-start | bytes 442376 | tf_op jit(solution)/shard_map/ppermute | solution.py:44
  57.2 1.9 %copy-start.17 = (bf16[72,16,128]{2,1,0:T(8,128)(2,1)}, bf16[72,16,128]{2,1,0:T(8,128)(2,1)S(1)}, u32[]{:S(2)}) copy-start(bf16[72,16,128]{2,1,0:T(8,128)(2,1)S(1)} %collective-permute-done.14.refs_16_.refs_18_) | copy-start | bytes 884740
  57.2 6.4 %collective-permute-start.12 = (bf16[36,16,128]{2,1,0:T(8,128)(2,1)S(1)}, bf16[36,16,128]{2,1,0:T(8,128)(2,1)S(1)}, u32[]{:S(2)}, u32[]{:S(2)}) collective-permute-start(bf16[36,16,128]{2,1,0:T(8,128)(2,1)S(1)} %slice.54), channel_id=1, source_target_pairs={{0,4},{1,5},{2,6},{3,7},{4,8},{5,9},{6,10},{7,11},{8,12},{9,13},{1... | collective-permute-start | bytes 442376 | tf_op jit(solution)/shard_map/ppermute | solution.py:44
  59.1 4.5 %copy-start.22 = (bf16[108,16,128]{2,1,0:T(8,128)(2,1)}, bf16[108,16,128]{2,1,0:T(8,128)(2,1)S(1)}, u32[]{:S(2)}) copy-start(bf16[108,16,128]{2,1,0:T(8,128)(2,1)S(1)} %collective-permute-done.4.refs_5_) | copy-start | bytes 1327108
  59.1 17.1 %collective-permute-start.17 = (bf16[108,16,128]{2,1,0:T(8,128)(2,1)S(1)}, bf16[108,16,128]{2,1,0:T(8,128)(2,1)S(1)}, u32[]{:S(2)}, u32[]{:S(2)}) collective-permute-start(bf16[108,16,128]{2,1,0:T(8,128)(2,1)S(1)} %collective-permute-done.11.refs_13_.refs_15_), channel_id=1, source_target_pairs={{0,1},{1,0},{2,3},{3,2},{4,5},{5,4},{6,7},{7,6},{8,9},{9,8},{10,11... | collective-permute-start | bytes 1327112 | tf_op jit(solution)/shard_map/ppermute | solution.py:44
  62.1 14.2 %copy-start.14 = (bf16[36,16,128]{2,1,0:T(8,128)(2,1)}, bf16[36,16,128]{2,1,0:T(8,128)(2,1)S(1)}, u32[]{:S(2)}) copy-start(bf16[36,16,128]{2,1,0:T(8,128)(2,1)S(1)} %collective-permute-done.13.refs_15_.refs_17_) | copy-start | bytes 442372
  62.1 14.2 %collective-permute-start.16 = (bf16[108,16,128]{2,1,0:T(8,128)(2,1)S(1)}, bf16[108,16,128]{2,1,0:T(8,128)(2,1)S(1)}, u32[]{:S(2)}, u32[]{:S(2)}) collective-permute-start(bf16[108,16,128]{2,1,0:T(8,128)(2,1)S(1)} %collective-permute-done.10.refs_12_.refs_14_), channel_id=1, source_target_pairs={{0,1},{1,0},{2,3},{3,2},{4,5},{5,4},{6,7},{7,6},{8,9},{9,8},{10,11... | collective-permute-start | bytes 1327112 | tf_op jit(solution)/shard_map/ppermute | solution.py:44
  63.6 12.7 %copy-start.15 = (bf16[36,16,128]{2,1,0:T(8,128)(2,1)}, bf16[36,16,128]{2,1,0:T(8,128)(2,1)S(1)}, u32[]{:S(2)}) copy-start(bf16[36,16,128]{2,1,0:T(8,128)(2,1)S(1)} %collective-permute-done.12.refs_14_.refs_16_) | copy-start | bytes 442372
  63.6 5.9 %collective-permute-start.6 = (bf16[36,16,128]{2,1,0:T(8,128)(2,1)S(1)}, bf16[36,16,128]{2,1,0:T(8,128)(2,1)S(1)}, u32[]{:S(2)}, u32[]{:S(2)}) collective-permute-start(bf16[36,16,128]{2,1,0:T(8,128)(2,1)S(1)} %slice.51), channel_id=1, source_target_pairs={{0,96},{16,112},{32,0},{48,16},{64,32},{80,48},{96,64},{112,80},{1... | collective-permute-start | bytes 442376 | tf_op jit(solution)/shard_map/ppermute | solution.py:34
  67.5 0.8 copy-start.23
  67.5 8.7 %collective-permute-start.18 = (bf16[72,16,128]{2,1,0:T(8,128)(2,1)}, bf16[72,16,128]{2,1,0:T(8,128)(2,1)}, u32[]{:S(2)}, u32[]{:S(2)}) collective-permute-start(bf16[72,16,128]{2,1,0:T(8,128)(2,1)} %pad_maximum_fusion.5), channel_id=1, source_target_pairs={{0,1},{1,0},{2,3},{3,2},{4,5},{5,4},{6,7},{7,6},{8,9},{9,8},{10,11... | collective-permute-start | bytes 884744 | tf_op jit(solution)/shard_map/ppermute | solution.py:44
  69.5 6.9 %copy-start.26 = (bf16[36,16,128]{2,1,0:T(8,128)(2,1)}, bf16[36,16,128]{2,1,0:T(8,128)(2,1)S(1)}, u32[]{:S(2)}) copy-start(bf16[36,16,128]{2,1,0:T(8,128)(2,1)S(1)} %collective-permute-done.6.refs_7_) | copy-start | bytes 442372
  69.5 6.8 %collective-permute-start.5 = (bf16[36,16,128]{2,1,0:T(8,128)(2,1)S(1)}, bf16[36,16,128]{2,1,0:T(8,128)(2,1)S(1)}, u32[]{:S(2)}, u32[]{:S(2)}) collective-permute-start(bf16[36,16,128]{2,1,0:T(8,128)(2,1)S(1)} %slice.50), channel_id=1, source_target_pairs={{0,32},{16,48},{32,64},{48,80},{64,96},{80,112},{96,0},{112,16},{1... | collective-permute-start | bytes 442376 | tf_op jit(solution)/shard_map/ppermute | solution.py:34
  76.3 0.7 copy-start.27
  76.3 0.8 copy-start.11
  76.3 1.0 copy-start.12
  76.3 1.2 copy-start.3
  87.6 8.8 %collective-permute-start.19 = (bf16[100,16,128]{2,1,0:T(8,128)(2,1)}, bf16[100,16,128]{2,1,0:T(8,128)(2,1)S(1)}, u32[]{:S(2)}, u32[]{:S(2)}) collective-permute-start(bf16[100,16,128]{2,1,0:T(8,128)(2,1)} %get-tuple-element.10.refs_0_), channel_id=1, source_target_pairs={{0,16},{16,0},{32,48},{48,32},{64,80},{80,64},{96,112},{112,96},{1... | collective-permute-start | bytes 1228808 | tf_op jit(solution)/shard_map/ppermute | solution.py:34
  88.3 10.4 %collective-permute-start.21 = (bf16[100,16,128]{2,1,0:T(8,128)(2,1)}, bf16[100,16,128]{2,1,0:T(8,128)(2,1)S(1)}, u32[]{:S(2)}, u32[]{:S(2)}) collective-permute-start(bf16[100,16,128]{2,1,0:T(8,128)(2,1)} %get-tuple-element.10.refs_0_), channel_id=1, source_target_pairs={{0,96},{16,112},{32,0},{48,16},{64,32},{80,48},{96,64},{112,80},{1... | collective-permute-start | bytes 1228808 | tf_op jit(solution)/shard_map/ppermute | solution.py:34
  90.3 12.2 %collective-permute-start.20 = (bf16[100,16,128]{2,1,0:T(8,128)(2,1)}, bf16[100,16,128]{2,1,0:T(8,128)(2,1)S(1)}, u32[]{:S(2)}, u32[]{:S(2)}) collective-permute-start(bf16[100,16,128]{2,1,0:T(8,128)(2,1)} %get-tuple-element.10.refs_0_), channel_id=1, source_target_pairs={{0,32},{16,48},{32,64},{48,80},{64,96},{80,112},{96,0},{112,16},{1... | collective-permute-start | bytes 1228808 | tf_op jit(solution)/shard_map/ppermute | solution.py:34
  96.4 22.5 %copy-start.13 = (bf16[100,16,128]{2,1,0:T(8,128)(2,1)}, bf16[100,16,128]{2,1,0:T(8,128)(2,1)S(1)}, u32[]{:S(2)}) copy-start(bf16[100,16,128]{2,1,0:T(8,128)(2,1)S(1)} %collective-permute-done.19.refs_1_) | copy-start | bytes 1228804
  96.4 12.4 %collective-permute-start.23 = (bf16[100,16,128]{2,1,0:T(8,128)(2,1)S(1)}, bf16[100,16,128]{2,1,0:T(8,128)(2,1)S(1)}, u32[]{:S(2)}, u32[]{:S(2)}) collective-permute-start(bf16[100,16,128]{2,1,0:T(8,128)(2,1)S(1)} %collective-permute-done.19.refs_1_), channel_id=1, source_target_pairs={{0,96},{16,112},{32,0},{48,16},{64,32},{80,48},{96,64},{112,80},{1... | collective-permute-start | bytes 1228808 | tf_op jit(solution)/shard_map/ppermute | solution.py:34
  97.9 13.9 %collective-permute-start.22 = (bf16[100,16,128]{2,1,0:T(8,128)(2,1)S(1)}, bf16[100,16,128]{2,1,0:T(8,128)(2,1)S(1)}, u32[]{:S(2)}, u32[]{:S(2)}) collective-permute-start(bf16[100,16,128]{2,1,0:T(8,128)(2,1)S(1)} %collective-permute-done.19.refs_1_), channel_id=1, source_target_pairs={{0,32},{16,48},{32,64},{48,80},{64,96},{80,112},{96,0},{112,16},{1... | collective-permute-start | bytes 1228808 | tf_op jit(solution)/shard_map/ppermute | solution.py:34
  98.7 20.2 %copy-start.5 = (bf16[100,16,128]{2,1,0:T(8,128)(2,1)}, bf16[100,16,128]{2,1,0:T(8,128)(2,1)S(1)}, u32[]{:S(2)}) copy-start(bf16[100,16,128]{2,1,0:T(8,128)(2,1)S(1)} %collective-permute-done.21.refs_3_) | copy-start | bytes 1228804
  98.7 13.4 %collective-permute-start.25 = (bf16[50,16,128]{2,1,0:T(8,128)(2,1)S(1)}, bf16[50,16,128]{2,1,0:T(8,128)(2,1)S(1)}, u32[]{:S(2)}, u32[]{:S(2)}) collective-permute-start(bf16[50,16,128]{2,1,0:T(8,128)(2,1)S(1)} %slice.57), channel_id=1, source_target_pairs={{0,96},{16,112},{32,0},{48,16},{64,32},{80,48},{96,64},{112,80},{1... | collective-permute-start | bytes 614408 | tf_op jit(solution)/shard_map/ppermute | solution.py:34
  102.5 16.3 %copy-start.6 = (bf16[100,16,128]{2,1,0:T(8,128)(2,1)}, bf16[100,16,128]{2,1,0:T(8,128)(2,1)S(1)}, u32[]{:S(2)}) copy-start(bf16[100,16,128]{2,1,0:T(8,128)(2,1)S(1)} %collective-permute-done.20.refs_2_) | copy-start | bytes 1228804
  102.5 12.5 %collective-permute-start.24 = (bf16[50,16,128]{2,1,0:T(8,128)(2,1)S(1)}, bf16[50,16,128]{2,1,0:T(8,128)(2,1)S(1)}, u32[]{:S(2)}, u32[]{:S(2)}) collective-permute-start(bf16[50,16,128]{2,1,0:T(8,128)(2,1)S(1)} %slice.56), channel_id=1, source_target_pairs={{0,32},{16,48},{32,64},{48,80},{64,96},{80,112},{96,0},{112,16},{1... | collective-permute-start | bytes 614408 | tf_op jit(solution)/shard_map/ppermute | solution.py:34
  108.8 10.1 %copy-start.7 = (bf16[100,16,128]{2,1,0:T(8,128)(2,1)}, bf16[100,16,128]{2,1,0:T(8,128)(2,1)S(1)}, u32[]{:S(2)}) copy-start(bf16[100,16,128]{2,1,0:T(8,128)(2,1)S(1)} %collective-permute-done.23.refs_5_) | copy-start | bytes 1228804
  108.8 6.2 %collective-permute-start.27 = (bf16[50,16,128]{2,1,0:T(8,128)(2,1)S(1)}, bf16[50,16,128]{2,1,0:T(8,128)(2,1)S(1)}, u32[]{:S(2)}, u32[]{:S(2)}) collective-permute-start(bf16[50,16,128]{2,1,0:T(8,128)(2,1)S(1)} %slice.59), channel_id=1, source_target_pairs={{0,96},{16,112},{32,0},{48,16},{64,32},{80,48},{96,64},{112,80},{1... | collective-permute-start | bytes 614408 | tf_op jit(solution)/shard_map/ppermute | solution.py:34
  111.8 7.1 %copy-start.8 = (bf16[100,16,128]{2,1,0:T(8,128)(2,1)}, bf16[100,16,128]{2,1,0:T(8,128)(2,1)S(1)}, u32[]{:S(2)}) copy-start(bf16[100,16,128]{2,1,0:T(8,128)(2,1)S(1)} %collective-permute-done.22.refs_4_) | copy-start | bytes 1228804
  111.8 7.0 %collective-permute-start.26 = (bf16[50,16,128]{2,1,0:T(8,128)(2,1)S(1)}, bf16[50,16,128]{2,1,0:T(8,128)(2,1)S(1)}, u32[]{:S(2)}, u32[]{:S(2)}) collective-permute-start(bf16[50,16,128]{2,1,0:T(8,128)(2,1)S(1)} %slice.58), channel_id=1, source_target_pairs={{0,32},{16,48},{32,64},{48,80},{64,96},{80,112},{96,0},{112,16},{1... | collective-permute-start | bytes 614408 | tf_op jit(solution)/shard_map/ppermute | solution.py:34
  112.0 6.8 %copy-start.18 = (bf16[50,16,128]{2,1,0:T(8,128)(2,1)}, bf16[50,16,128]{2,1,0:T(8,128)(2,1)S(1)}, u32[]{:S(2)}) copy-start(bf16[50,16,128]{2,1,0:T(8,128)(2,1)S(1)} %collective-permute-done.25.refs_7_) | copy-start | bytes 614404
  115.0 3.8 %copy-start.19 = (bf16[50,16,128]{2,1,0:T(8,128)(2,1)}, bf16[50,16,128]{2,1,0:T(8,128)(2,1)S(1)}, u32[]{:S(2)}) copy-start(bf16[50,16,128]{2,1,0:T(8,128)(2,1)S(1)} %collective-permute-done.24.refs_6_) | copy-start | bytes 614404
  115.0 3.8 %copy-start.20 = (bf16[50,16,128]{2,1,0:T(8,128)(2,1)}, bf16[50,16,128]{2,1,0:T(8,128)(2,1)S(1)}, u32[]{:S(2)}) copy-start(bf16[50,16,128]{2,1,0:T(8,128)(2,1)S(1)} %collective-permute-done.27.refs_9_) | copy-start | bytes 614404
  118.8 0.7 copy-start.21
  132.0 15.0 %all-to-all-start.1 = ((bf16[64,16,512]{2,1,0:T(8,128)(2,1)}), bf16[64,16,512]{2,1,0:T(8,128)(2,1)S(1)}, u32[]{:S(2)}, u32[]{:S(2)}) async-start(bf16[64,16,512]{2,1,0:T(8,128)(2,1)} %shard_map.64), calls=%async_computation.1 | async-start | bytes 2097152 | tf_op jit(solution)/shard_map/all_to_all | solution.py:395

commit v3 on v2

--- a/solution.py
+++ b/solution.py
@@ -45,9 +45,13 @@
 
 
 def slice_kernel(density, pattern, square_filter, step_filter, sent, small, masks, sems):
-    copies = [pltpu.make_async_copy(density.at[:, d], sent.at[d, pl.ds(0, 8)], sems.at[d]) for d in range(TR)]
+    copies = [
+        pltpu.make_async_copy(density.at[:, d, :, pl.ds(n * BLOCK, BLOCK)], sent.at[d, pl.ds(8 * n, 8)], sems.at[4 * d + n])
+        for d in range(TR)
+        for n in range(4)
+    ]
     filters = [
-        pltpu.make_async_copy(mask, masks.at[n], sems.at[TR + n])
+        pltpu.make_async_copy(mask, masks.at[n], sems.at[4 * TR + n])
         for n, mask in enumerate((pattern, square_filter, step_filter))
     ]
     for copy in filters + copies:
@@ -58,8 +62,7 @@
         small[4 * n : 4 * n + 4, 0:8] = masks[n].astype(jnp.float32)
     head = small[...].astype(BF)
     for d in range(TR):
-        sent[d, 8, :, 0:BLOCK] = head
-        sent[d, 8, :, BLOCK:] = jnp.zeros((SL, 3 * BLOCK), BF)
+        sent[d, 32] = head
     for copy in copies:
         copy.wait()
 
@@ -67,7 +70,7 @@
 def pack_kernel(sliced, packed, lists, flags, flags_s, sem):
     marks = jnp.zeros((SL, BLOCK), jnp.float32)
     for s in range(TR):
-        mark = sliced[s, 8, :, 0:BLOCK].astype(jnp.float32)
+        mark = sliced[s, 32].astype(jnp.float32)
         marks = marks + (pltpu.roll(mark, 8 * s, 1) if s else mark)
     flags[...] = marks.astype(jnp.int32)
     copy = pltpu.make_async_copy(flags, flags_s, sem)
@@ -84,7 +87,7 @@
             out = []
             for n in range(4):
                 lists[n, counts[n]] = i
-                packed[n * SLOTS + counts[n]] = sliced[b, q, :, n * BLOCK : (n + 1) * BLOCK]
+                packed[n * SLOTS + counts[n]] = sliced[b, 8 * n + q]
                 out.append(counts[n] + flags_s[n, i])
             counts = tuple(out)
         return counts
@@ -96,7 +99,8 @@
     packed[ZERO] = jnp.zeros((SL, BLOCK), BF)
 
 
-def lists_kernel(flags, lists):
+def lists_kernel(flags, *refs):
+    lists = refs[-1]
     for n in range(8):
         for t in range(KS):
             lists[n, t] = NONE
@@ -116,25 +120,36 @@
         lists[n, counts[n]] = NONE
 
 
-def fetch(parts, layout, target, sems):
+def split(layout, slots):
+    columns = [[] for _ in range(4)]
+    for n, part in enumerate(layout):
+        for start, back, line, at, size in part:
+            for q in range(0, size, slots):
+                columns[(at + q) // slots].append((n, start + q, back, line, at + q, slots))
+    return columns
+
+
+def whole(layout):
+    return [(n, *piece) for n, part in enumerate(layout) for piece in part]
+
+
+def fetch(parts, chosen, target, sems):
     copies = []
-    for part, pieces in zip(parts, layout):
-        for start, back, line, at, size in pieces:
-            n = len(copies)
-            copies.append(pltpu.make_async_copy(part.at[pl.ds(start, size)], target(back, line, at, size), sems.at[n]))
+    for q, (n, start, back, line, at, size) in enumerate(chosen):
+        copies.append(pltpu.make_async_copy(parts[n].at[pl.ds(start, size)], target(back, line, at, size), sems.at[q]))
     return copies
 
 
-def fetch_rows(place, parts, layout, rows, sems):
+def fetch_rows(place, parts, chosen, rows, sems):
     x, y = place[0] // 2, place[0] % 2
 
     def target(back, line, at, size):
         return rows.at[pl.ds(at, size), lax.rem(x - back + 4, 4) * 2 + (y + line) % 2]
 
-    return fetch(parts, layout, target, sems)
-
-
-def fetch_cols(place, parts, layout, cols, sems):
+    return fetch(parts, chosen, target, sems)
+
+
+def fetch_cols(place, parts, chosen, cols, sems):
     z, y, core = place[1] // 4, (place[1] // 2) % 2, place[1] % 2
 
     def target(back, line, at, size):
@@ -142,7 +157,7 @@
         c = lax.rem(z - back + 4, 4) * 4 + ((y + line) % 2) * 2 + (core + other) % 2
         return cols.at[pl.ds(c * PACK + at, size)]
 
-    return fetch(parts, layout, target, sems)
+    return fetch(parts, chosen, target, sems)
 
 
 def product(table, outer, inner, cols, right):
@@ -157,17 +172,28 @@
     return total
 
 
+def fetch_heads(place, parts, heads, sems):
+    z, y, core = place[1] // 4, (place[1] // 2) % 2, place[1] % 2
+    copies = []
+    for n, start, back, line, at, size in whole(COLS):
+        if at <= KP < at + size:
+            c = lax.rem(z - back + 4, 4) * 4 + ((y + line % 2) % 2) * 2 + (core + line // 2) % 2
+            copies.append(pltpu.make_async_copy(parts[n].at[start + KP - at], heads.at[c], sems.at[len(copies)]))
+    return copies
+
+
 def square_kernel(place, inner, outer, *refs):
     row_parts, col_parts = refs[:NR], refs[NR : NR + NC]
-    square, table, rows, cols, marks, index, col_sems, row_sems, sem = refs[NR + NC :]
-    from_cols = fetch_cols(place, col_parts, COLS, cols, col_sems)
-    from_rows = fetch_rows(place, row_parts, ROWS, rows, row_sems)
-    for copy in from_cols + from_rows:
+    square, table, rows, cols, marks, heads, index, col_sems, row_sems, head_sems, sem = refs[NR + NC :]
+    from_heads = fetch_heads(place, col_parts, heads, head_sems)
+    from_cols = fetch_cols(place, col_parts, whole(COLS), cols, col_sems)
+    from_rows = fetch_rows(place, row_parts, whole(ROWS), rows, row_sems)
+    for copy in from_heads + from_cols + from_rows:
         copy.start()
-    for copy in from_cols:
+    for copy in from_heads:
         copy.wait()
     for c in range(TC):
-        marks[4 * c : 4 * c + 4, :] = cols[c * PACK + KP].astype(jnp.float32)[0:4]
+        marks[4 * c : 4 * c + 4, :] = heads[c].astype(jnp.float32)[0:4]
     kept = marks[...]
     before = lax.broadcasted_iota(jnp.int32, (BLOCK, BLOCK), 0) < lax.broadcasted_iota(jnp.int32, (BLOCK, BLOCK), 1)
     rank = jnp.dot(kept.astype(BF), before.astype(jnp.float32).astype(BF), preferred_element_type=jnp.float32)
@@ -177,7 +203,7 @@
     copy = pltpu.make_async_copy(index, table, sem)
     copy.start()
     copy.wait()
-    for copy in from_rows:
+    for copy in from_cols + from_rows:
         copy.wait()
 
     def column(j, carry):
@@ -193,34 +219,46 @@
 
 def step_kernel(place, inner, table, *refs):
     row_parts, col_parts = refs[:NS], refs[NS : NS + NC]
-    stepped, rows, cols, col_sems, row_sems = refs[NS + NC :]
-    copies = fetch_cols(place, col_parts, COLS, cols, col_sems)
-    copies += fetch_rows(place, row_parts, SQUARES, rows, row_sems)
-    for copy in copies:
+    stepped, rows, cols, results, col_sems, row_sems, out_sems = refs[NS + NC :]
+    from_cols = fetch_cols(place, col_parts, whole(COLS), cols, col_sems)
+    from_rows = [
+        fetch_rows(place, row_parts, column, rows, row_sems.at[j]) for j, column in enumerate(split(SQUARES, KS))
+    ]
+    for copy in from_cols + sum(from_rows, []):
         copy.start()
-    stepped[...] = jnp.zeros_like(stepped)
-    for copy in copies:
-        copy.wait()
+    for copy in from_cols:
+        copy.wait()
+    out = []
     for j in range(4):
+        for copy in from_rows[j]:
+            copy.wait()
 
         def right(t, n):
             return rows[j * KS + t : j * KS + t + n].reshape(n * BLOCK, BLOCK)
 
         outer = [inner[4 + j, s] for s in range(KT)]
         second = product(table, outer, [inner[j, t] for t in range(KS)], cols, right)
+        if j >= 2:
+            out[j - 2].wait()
+        result = results.at[j % 2]
+        result[...] = jnp.zeros_like(result)
         for s, i in enumerate(outer):
             own = cols[table[place[1] * 4 + j, i]].astype(jnp.float32)
-            result = 1.5 * own - 0.5 * second[s * SL : (s + 1) * SL]
-
-            @pl.when(i < NB)
-            def _():
-                stepped[i, :, j * BLOCK : (j + 1) * BLOCK] = result.astype(BF)
+            result[i] = (1.5 * own - 0.5 * second[s * SL : (s + 1) * SL]).astype(BF)
+        out.append(
+            pltpu.make_async_copy(
+                result.at[pl.ds(0, NB)], stepped.at[:, :, pl.ds(j * BLOCK, BLOCK)], out_sems.at[j]
+            )
+        )
+        out[j].start()
+    out[2].wait()
+    out[3].wait()
 
 
 def square_rows_kernel(place, lists, *refs):
     row_parts = refs[:NS]
     out, rows, sems = refs[NS:]
-    copies = fetch_rows(place, row_parts, SQUARES, rows, sems)
+    copies = fetch_rows(place, row_parts, whole(SQUARES), rows, sems)
     for copy in copies:
         copy.start()
     out[...] = jnp.zeros_like(out)
@@ -245,9 +283,14 @@
 ANY = pl.BlockSpec(memory_space=pl.ANY)
 
 
-def call(kernel, outs, in_specs, out_specs, scratch, flops, moved):
+def column_block(rows, columns):
+    return pl.BlockSpec((1, rows, columns), lambda j: (j, 0, 0))
+
+
+def call(kernel, outs, in_specs, out_specs, scratch, flops, moved, grid=()):
     return pl.pallas_call(
         kernel,
+        grid=grid,
         out_shape=outs,
         in_specs=in_specs,
         out_specs=out_specs,
@@ -330,10 +373,10 @@
     place = jnp.stack([lax.axis_index("row"), lax.axis_index("col")]).astype(jnp.int32)
     sent = call(
         slice_kernel,
-        jax.ShapeDtypeStruct((TR, 9, SL, 4 * BLOCK), BF),
+        jax.ShapeDtypeStruct((TR, 33, SL, BLOCK), BF),
         [ANY] * 4,
         VMEM,
-        [pltpu.VMEM((SL, BLOCK), jnp.float32), pltpu.VMEM((3, 4, 8), jnp.int32), pltpu.SemaphoreType.DMA((TR + 3,))],
+        [pltpu.VMEM((SL, BLOCK), jnp.float32), pltpu.VMEM((3, 4, 8), jnp.int32), pltpu.SemaphoreType.DMA((4 * TR + 3,))],
         0,
         2 << 20,
     )(density.reshape(8, TR, SL, 4 * BLOCK), pattern.T, square_filter.T, step_filter.T)
@@ -352,10 +395,11 @@
         0,
         2 << 20,
     )(sliced)
-    lists = call(lists_kernel, jax.ShapeDtypeStruct((8, 32), jnp.int32), [SMEM], SMEM, [], 0, 1 << 14)(flags)
-
     row_parts = ring_merged(packed, row_shift)
     col_parts = gather_cols(packed)
+    lists = call(
+        lists_kernel, jax.ShapeDtypeStruct((8, 32), jnp.int32), [SMEM] + [ANY] * NC, SMEM, [], 1048576, 12582912
+    )(flags, *col_parts)
     square_packed, table = call(
         square_kernel,
         (
@@ -368,13 +412,15 @@
             pltpu.VMEM((PACK, TR, SL, BLOCK), BF),
             pltpu.VMEM((TC * PACK, SL, BLOCK), BF),
             pltpu.VMEM((NB, BLOCK), jnp.float32),
+            pltpu.VMEM((TC, SL, BLOCK), BF),
             pltpu.VMEM((NB + 8, BLOCK), jnp.int32),
             pltpu.SemaphoreType.DMA((pieces(COLS),)),
             pltpu.SemaphoreType.DMA((pieces(ROWS),)),
+            pltpu.SemaphoreType.DMA((TC,)),
             pltpu.SemaphoreType.DMA,
         ],
         2 * 4 * KS * SL * KP * BLOCK * BLOCK,
-        8 << 20,
+        9 << 20,
     )(place, pattern_lists, lists, *row_parts, *col_parts)
 
     square_parts = gather_rows(square_packed)
@@ -382,12 +428,14 @@
         step_kernel,
         jax.ShapeDtypeStruct((NB, SL, 4 * BLOCK), BF),
         [SMEM] * 3 + [ANY] * (NS + NC),
-        VMEM,
+        ANY,
         [
             pltpu.VMEM((4 * KS, TR, SL, BLOCK), BF),
             pltpu.VMEM((TC * PACK, SL, BLOCK), BF),
+            pltpu.VMEM((2, NB + 8, SL, BLOCK), BF),
             pltpu.SemaphoreType.DMA((pieces(COLS),)),
-            pltpu.SemaphoreType.DMA((pieces(SQUARES),)),
+            pltpu.SemaphoreType.DMA((4, TR)),
+            pltpu.SemaphoreType.DMA((4,)),
         ],
         2 * 4 * KT * SL * KS * BLOCK * BLOCK,
         9 << 20,

time: 150 us -> 148 us (0.987)
  waiting for transfers between devices: 44.2 us -> 42.6 us
    ppermute x12, waiting for transfers between devices: 14.6 us -> 11.8 us  [col_shift(): return lax.ppermute(value, 'col', pairs)]
  transfers between devices with their start and end apart: 29 -> 29, of which waited for: 18 -> 16; matrix products, arithmetic and copies ran while one was open for 2% -> 3% of each run, Pallas kernels for 6% -> 6%
where the time goes in v3:
time: 148 us; the launch traced here: 146 us
  waiting for transfers between devices  42.6 us (29%)
  Pallas kernels  37 us (25%)
  starting transfers between devices  36.1 us (24%)
  blocking collectives  21.8 us (15%)
  local copies, waits for them, and re-layouts  4.98 us (3%)
  other arithmetic  2.44 us (2%)
    ppermute x16, waiting for transfers between devices, row_shift(): return lax.ppermute(value, 'row', pairs)  24.5 us
    all_to_all x1, blocking collectives, on_device(): sliced = lax.all_to_all(sent, 'row', 0, 0, tiled=True)  21.8 us
    ppermute x16, starting transfers between devices, row_shift(): return lax.ppermute(value, 'row', pairs)  18.5 us
    ppermute x12, starting transfers between devices, col_shift(): return lax.ppermute(value, 'col', pairs)  14 us
    ppermute x12, waiting for transfers between devices, col_shift(): return lax.ppermute(value, 'col', pairs)  11.8 us
    pallas_call x1, Pallas kernels, on_device(): call(step_kernel, jax.ShapeDtypeStruct((NB, SL, 4 * BLOCK), BF), [SMEM] *...  11.6 us
    pallas_call x1, Pallas kernels, on_device(): call(square_kernel, (jax.ShapeDtypeStruct((4 * KS, SL, BLOCK), BF), jax.S...  10.1 us
    all_to_all x1, waiting for transfers between devices, on_device(): back = lax.all_to_all(stepped, 'row', 0, 0, tiled=True)  6.37 us
  transfers between devices with their start and end apart: 29, of which 16 were waited for; matrix products, arithmetic and copies ran while one was open for 3% of the time, Pallas kernels for 6%

profile of v3, /device:TPU:0, one launch (start us, length us, event | category | flops | bytes accessed | tf_op | source)
XLA Modules:
  0.0 146.0 jit_solution(9432429969192061439)
XLA Ops:
  0.6 2.5 %shard_map.59 = bf16[8,33,16,128]{3,2,1,0:T(8,128)(2,1)} custom-call(bf16[8,8,16,512]{3,2,1,0:T(8,128)(2,1)} %bitcast.12, s32[4,8]{1,0:T(4,128)} %bitcast.15, s32[4,8]{1,0:T(4,128)} %bitcast.16, s32[4,8]{1,0:T(4,128)} %bitcast.17), custom_call_target="tpu_custom_call" | custom-call | bytes 2097152 | tf_op jit(solution)/shard_map/pallas_call | solution.py:374
  3.2 21.8 %all_to_all.10.sliced = bf16[8,33,16,128]{3,2,1,0:T(8,128)(2,1)} all-to-all(bf16[8,33,16,128]{3,2,1,0:T(8,128)(2,1)} %shard_map.59), channel_id=1, replica_groups=mesh['row'=8,'col'=16] {'row'}, dimensions={0} | all-to-all | bytes 2162688 | tf_op jit(solution)/shard_map/all_to_all | solution.py:383
  25.0 3.8 %shard_map.60 = (bf16[72,16,128]{2,1,0:T(8,128)(2,1)}, s32[4,32]{1,0:T(4,128)}, s32[16,128]{1,0:T(8,128)}) custom-call(bf16[8,33,16,128]{3,2,1,0:T(8,128)(2,1)} %all_to_all.10.sliced), custom_call_target="tpu_custom_call" | custom-call | bytes 2097152 | tf_op jit(solution)/shard_map/pallas_call | solution.py:385
  28.8 4.1 %collective-permute-start.2 = (bf16[72,16,128]{2,1,0:T(8,128)(2,1)}, bf16[72,16,128]{2,1,0:T(8,128)(2,1)S(1)}, u32[]{:S(2)}, u32[]{:S(2)}) collective-permute-start(bf16[72,16,128]{2,1,0:T(8,128)(2,1)} %get-tuple-element.8.refs_0_.refs_8_.refs_10_), channel_id=1, source_target_pairs={{0,12},{1,13},{2,14},{3,15},{4,0},{5,1},{6,2},{7,3},{8,4},{9,5},{1... | collective-permute-start | bytes 884744 | tf_op jit(solution)/shard_map/ppermute | solution.py:44
  33.0 2.9 %collective-permute-start = (bf16[72,16,128]{2,1,0:T(8,128)(2,1)}, bf16[72,16,128]{2,1,0:T(8,128)(2,1)S(1)}, u32[]{:S(2)}, u32[]{:S(2)}) collective-permute-start(bf16[72,16,128]{2,1,0:T(8,128)(2,1)} %get-tuple-element.8.refs_0_.refs_8_.refs_10_), channel_id=1, source_target_pairs={{0,2},{1,3},{2,0},{3,1},{4,6},{5,7},{6,4},{7,5},{8,10},{9,11},{10,... | collective-permute-start | bytes 884744 | tf_op jit(solution)/shard_map/ppermute | solution.py:44
  35.9 1.2 collective-permute-start.14
  37.0 0.9 collective-permute-start.13
  37.9 0.1 collective-permute-done.2.refs_3_.refs_11_.refs_13_
  38.0 0.8 collective-permute-start.12
  38.8 2.5 %collective-permute-done.1.refs_2_.refs_10_.refs_12_ = bf16[72,16,128]{2,1,0:T(8,128)(2,1)S(1)} collective-permute-done((bf16[72,16,128]{2,1,0:T(8,128)(2,1)}, bf16[72,16,128]{2,1,0:T(8,128)(2,1)S(1)}, u32[]{:S(2)}, u32[]{:S(2)}) %collective-permute-start.1) | collective-permute-done | bytes 294944 | tf_op jit(solution)/shard_map/ppermute | solution.py:44
  41.3 2.3 %collective-permute-done.refs_1_.refs_9_.refs_11_ = bf16[72,16,128]{2,1,0:T(8,128)(2,1)S(1)} collective-permute-done((bf16[72,16,128]{2,1,0:T(8,128)(2,1)}, bf16[72,16,128]{2,1,0:T(8,128)(2,1)S(1)}, u32[]{:S(2)}, u32[]{:S(2)}) %collective-permute-start) | collective-permute-done | bytes 294944 | tf_op jit(solution)/shard_map/ppermute | solution.py:44
  43.6 0.1 pad_maximum_fusion.1
  43.7 3.2 %collective-permute-start.4 = (bf16[108,16,128]{2,1,0:T(8,128)(2,1)S(1)}, bf16[108,16,128]{2,1,0:T(8,128)(2,1)S(1)}, u32[]{:S(2)}, u32[]{:S(2)}) collective-permute-start(bf16[108,16,128]{2,1,0:T(8,128)(2,1)S(1)} %get-tuple-element.14), channel_id=1, source_target_pairs={{0,12},{1,13},{2,14},{3,15},{4,0},{5,1},{6,2},{7,3},{8,4},{9,5},{1... | collective-permute-start | bytes 1327112 | tf_op jit(solution)/shard_map/ppermute | solution.py:44
  46.9 0.0 collective-permute-done.13.refs_2_
  47.0 0.5 collective-permute-done.12.refs_1_
  47.5 0.1 pad_maximum_fusion.3
  47.6 0.6 copy-done.18
  48.2 1.2 collective-permute-start.16
  49.4 1.0 pad_maximum_fusion
  50.4 0.9 collective-permute-start.15
  51.3 1.4 collective-permute-done.4.refs_5_.refs_13_.refs_15_
  52.7 3.8 %collective-permute-start.6 = (bf16[36,16,128]{2,1,0:T(8,128)(2,1)S(1)}, bf16[36,16,128]{2,1,0:T(8,128)(2,1)S(1)}, u32[]{:S(2)}, u32[]{:S(2)}) collective-permute-start(bf16[36,16,128]{2,1,0:T(8,128)(2,1)S(1)} %slice.51), channel_id=1, source_target_pairs={{0,12},{1,13},{2,14},{3,15},{4,0},{5,1},{6,2},{7,3},{8,4},{9,5},{1... | collective-permute-start | bytes 442376 | tf_op jit(solution)/shard_map/ppermute | solution.py:44
  56.5 0.0 collective-permute-done.3.refs_4_.refs_12_.refs_14_
  56.5 0.1 collective-permute-start.5
  56.6 0.9 collective-permute-done.16.refs_5_
  57.5 0.0 collective-permute-start.10
  57.5 1.6 %collective-permute-done.6.refs_7_.refs_15_.refs_17_ = bf16[36,16,128]{2,1,0:T(8,128)(2,1)S(1)} collective-permute-done((bf16[36,16,128]{2,1,0:T(8,128)(2,1)S(1)}, bf16[36,16,128]{2,1,0:T(8,128)(2,1)S(1)}, u32[]{:S(2)}, u32[]{:S(2)}) %collective-permute-start.6) | collective-permute-done | bytes 147488 | tf_op jit(solution)/shard_map/ppermute | solution.py:44
  59.2 0.0 collective-permute-start.9
  59.2 3.8 %collective-permute-done.5.refs_6_.refs_14_.refs_16_ = bf16[36,16,128]{2,1,0:T(8,128)(2,1)S(1)} collective-permute-done((bf16[36,16,128]{2,1,0:T(8,128)(2,1)S(1)}, bf16[36,16,128]{2,1,0:T(8,128)(2,1)S(1)}, u32[]{:S(2)}, u32[]{:S(2)}) %collective-permute-start.5) | collective-permute-done | bytes 147488 | tf_op jit(solution)/shard_map/ppermute | solution.py:44
  62.9 0.0 collective-permute-start.7
  62.9 0.8 pad_maximum_fusion.5
  63.7 0.5 collective-permute-done.15.refs_4_
  64.2 0.7 slice.55
  64.9 0.7 slice.54
  65.6 1.0 collective-permute-start.18
  66.6 1.1 collective-permute-start.17
  67.7 0.6 pad_add_fusion.place
  68.3 0.0 copy-start
  68.4 0.6 copy-done.10
  69.0 0.2 copy-done.8
  69.2 0.3 copy-done
  69.4 3.0 %shard_map.61.outer.lists.inner = s32[8,32]{1,0:T(8,128)} custom-call(s32[16,128]{1,0:T(8,128)} %get-tuple-element.7.flags, bf16[72,16,128]{2,1,0:T(8,128)(2,1)} %get-tuple-element.8.refs_0_.refs_8_.refs_10_, bf16[72,16,128]{2,1,0:T(8,128)(2,1)} %copy-done.1, bf16[72,16,128]{2,1,0:T(8,128)(2,1)} %copy-done.3, bf16[72,16,128]{2,1,0:T(8,128)(2,1)} %copy-done.2, ...), custom_call_target="tpu_custom_call" | custom-call | flops 1048576 | bytes 12582912 | tf_op jit(solution)/shard_map/pallas_call | solution.py:400
  72.5 1.3 collective-permute-done.17.refs_6_
  73.8 10.1 %shard_map.62 = (bf16[100,16,128]{2,1,0:T(8,128)(2,1)}, s32[72,128]{1,0:T(8,128)}) custom-call(s32[2]{0:T(128)} %pad_add_fusion.place, s32[4,32]{1,0:T(4,128)} %get-tuple-element.9.inner, s32[8,32]{1,0:T(8,128)} %shard_map.61.outer.lists.inner, bf16[72,16,128]{2,1,0:T(8,128)(2,1)} %get-tuple-element.8.refs_0_.refs_8_.refs_10_, ...), custom_call_target="tpu_custom_call" | custom-call | flops 891289600 | bytes 9437184 | tf_op jit(solution)/shard_map/pallas_call | solution.py:403
  83.8 1.5 %collective-permute-start.19 = (bf16[100,16,128]{2,1,0:T(8,128)(2,1)}, bf16[100,16,128]{2,1,0:T(8,128)(2,1)S(1)}, u32[]{:S(2)}, u32[]{:S(2)}) collective-permute-start(bf16[100,16,128]{2,1,0:T(8,128)(2,1)} %get-tuple-element.10.refs_0_), channel_id=1, source_target_pairs={{0,16},{16,0},{32,48},{48,32},{64,80},{80,64},{96,112},{112,96},{1... | collective-permute-start | bytes 1228808 | tf_op jit(solution)/shard_map/ppermute | solution.py:34
  85.4 1.0 collective-permute-start.21
  86.3 1.1 collective-permute-start.20
  87.4 7.0 %collective-permute-done.19.refs_1_ = bf16[100,16,128]{2,1,0:T(8,128)(2,1)S(1)} collective-permute-done((bf16[100,16,128]{2,1,0:T(8,128)(2,1)}, bf16[100,16,128]{2,1,0:T(8,128)(2,1)S(1)}, u32[]{:S(2)}, u32[]{:S(2)}) %collective-permute-start.19) | collective-permute-done | bytes 409632 | tf_op jit(solution)/shard_map/ppermute | solution.py:34
  94.4 1.6 %collective-permute-start.23 = (bf16[100,16,128]{2,1,0:T(8,128)(2,1)S(1)}, bf16[100,16,128]{2,1,0:T(8,128)(2,1)S(1)}, u32[]{:S(2)}, u32[]{:S(2)}) collective-permute-start(bf16[100,16,128]{2,1,0:T(8,128)(2,1)S(1)} %collective-permute-done.19.refs_1_), channel_id=1, source_target_pairs={{0,96},{16,112},{32,0},{48,16},{64,32},{80,48},{96,64},{112,80},{1... | collective-permute-start | bytes 1228808 | tf_op jit(solution)/shard_map/ppermute | solution.py:34
  96.0 0.5 collective-permute-start.22
  96.5 2.8 %collective-permute-start.25 = (bf16[50,16,128]{2,1,0:T(8,128)(2,1)S(1)}, bf16[50,16,128]{2,1,0:T(8,128)(2,1)S(1)}, u32[]{:S(2)}, u32[]{:S(2)}) collective-permute-start(bf16[50,16,128]{2,1,0:T(8,128)(2,1)S(1)} %slice.57), channel_id=1, source_target_pairs={{0,96},{16,112},{32,0},{48,16},{64,32},{80,48},{96,64},{112,80},{1... | collective-permute-start | bytes 614408 | tf_op jit(solution)/shard_map/ppermute | solution.py:34
  99.3 0.3 collective-permute-start.24
  99.6 7.2 %collective-permute-done.23.refs_5_ = bf16[100,16,128]{2,1,0:T(8,128)(2,1)S(1)} collective-permute-done((bf16[100,16,128]{2,1,0:T(8,128)(2,1)S(1)}, bf16[100,16,128]{2,1,0:T(8,128)(2,1)S(1)}, u32[]{:S(2)}, u32[]{:S(2)}) %collective-permute-start.23) | collective-permute-done | bytes 409632 | tf_op jit(solution)/shard_map/ppermute | solution.py:34
  106.9 2.8 %collective-permute-start.27 = (bf16[50,16,128]{2,1,0:T(8,128)(2,1)S(1)}, bf16[50,16,128]{2,1,0:T(8,128)(2,1)S(1)}, u32[]{:S(2)}, u32[]{:S(2)}) collective-permute-start(bf16[50,16,128]{2,1,0:T(8,128)(2,1)S(1)} %slice.59), channel_id=1, source_target_pairs={{0,96},{16,112},{32,0},{48,16},{64,32},{80,48},{96,64},{112,80},{1... | collective-permute-start | bytes 614408 | tf_op jit(solution)/shard_map/ppermute | solution.py:34
  109.7 0.1 collective-permute-start.26
  109.8 1.2 collective-permute-done.25.refs_7_
  111.0 2.5 %collective-permute-done.24.refs_6_ = bf16[50,16,128]{2,1,0:T(8,128)(2,1)S(1)} collective-permute-done((bf16[50,16,128]{2,1,0:T(8,128)(2,1)S(1)}, bf16[50,16,128]{2,1,0:T(8,128)(2,1)S(1)}, u32[]{:S(2)}, u32[]{:S(2)}) %collective-permute-start.24) | collective-permute-done | bytes 204832 | tf_op jit(solution)/shard_map/ppermute | solution.py:34
  113.5 3.3 %collective-permute-done.26.refs_8_ = bf16[50,16,128]{2,1,0:T(8,128)(2,1)S(1)} collective-permute-done((bf16[50,16,128]{2,1,0:T(8,128)(2,1)S(1)}, bf16[50,16,128]{2,1,0:T(8,128)(2,1)S(1)}, u32[]{:S(2)}, u32[]{:S(2)}) %collective-permute-start.26) | collective-permute-done | bytes 204832 | tf_op jit(solution)/shard_map/ppermute | solution.py:34
  116.8 0.6 copy-done.22
  117.4 11.6 %shard_map.64 = bf16[64,16,512]{2,1,0:T(8,128)(2,1)} custom-call(s32[2]{0:T(128)} %pad_add_fusion.place, s32[8,32]{1,0:T(8,128)} %shard_map.61.outer.lists.inner, s32[72,128]{1,0:T(8,128)} %get-tuple-element.11.table, bf16[100,16,128]{2,1,0:T(8,128)(2,1)} %get-tuple-element.10.refs_0_, bf16[100,16,128]{2,1,0:T(8,128)(2,1)} %copy-done.17, ...), custom_call_target="tpu_custom_call" | custom-call | flops 1101004800 | bytes 9437184 | tf_op jit(solution)/shard_map/pallas_call | solution.py:427
  129.1 3.6 %all-to-all-start.1 = ((bf16[64,16,512]{2,1,0:T(8,128)(2,1)}), bf16[64,16,512]{2,1,0:T(8,128)(2,1)S(1)}, u32[]{:S(2)}, u32[]{:S(2)}) async-start(bf16[64,16,512]{2,1,0:T(8,128)(2,1)} %shard_map.64), calls=%async_computation.1 | async-start | bytes 2097152 | tf_op jit(solution)/shard_map/all_to_all | solution.py:443
  132.6 5.9 %shard_map.63 = bf16[8,8,16,512]{3,2,1,0:T(8,128)(2,1)} custom-call(s32[2]{0:T(128)} %pad_add_fusion.place, s32[8,32]{1,0:T(8,128)} %shard_map.61.outer.lists.inner, bf16[100,16,128]{2,1,0:T(8,128)(2,1)} %get-tuple-element.10.refs_0_, bf16[100,16,128]{2,1,0:T(8,128)(2,1)} %copy-done.17, bf16[100,16,128]{2,1,0:T(8,128)(2,1)} %copy-done.12, ...), custom_call_target="tpu_custom_call" | custom-call | bytes 4194304 | tf_op jit(solution)/shard_map/pallas_call | solution.py:444
  138.5 6.4 %all-to-all-done.1 = bf16[64,16,512]{2,1,0:T(8,128)(2,1)S(1)} async-done(((bf16[64,16,512]{2,1,0:T(8,128)(2,1)}), bf16[64,16,512]{2,1,0:T(8,128)(2,1)S(1)}, u32[]{:S(2)}, u32[]{:S(2)}) %all-to-all-start.1) | async-done | bytes 1048608 | tf_op jit(solution)/shard_map/all_to_all | solution.py:443
  144.9 1.1 copy.6
  (73 shorter events, 0.2 us)
Async XLA Ops:
  28.8 9.2 %collective-permute-start.2 = (bf16[72,16,128]{2,1,0:T(8,128)(2,1)}, bf16[72,16,128]{2,1,0:T(8,128)(2,1)S(1)}, u32[]{:S(2)}, u32[]{:S(2)}) collective-permute-start(bf16[72,16,128]{2,1,0:T(8,128)(2,1)} %get-tuple-element.8.refs_0_.refs_8_.refs_10_), channel_id=1, source_target_pairs={{0,12},{1,13},{2,14},{3,15},{4,0},{5,1},{6,2},{7,3},{8,4},{9,5},{1... | collective-permute-start | bytes 884744 | tf_op jit(solution)/shard_map/ppermute | solution.py:44
  33.0 8.4 %collective-permute-start.1 = (bf16[72,16,128]{2,1,0:T(8,128)(2,1)}, bf16[72,16,128]{2,1,0:T(8,128)(2,1)S(1)}, u32[]{:S(2)}, u32[]{:S(2)}) collective-permute-start(bf16[72,16,128]{2,1,0:T(8,128)(2,1)} %get-tuple-element.8.refs_0_.refs_8_.refs_10_), channel_id=1, source_target_pairs={{0,4},{1,5},{2,6},{3,7},{4,8},{5,9},{6,10},{7,11},{8,12},{9,13},{1... | collective-permute-start | bytes 884744 | tf_op jit(solution)/shard_map/ppermute | solution.py:44
  33.0 10.7 %collective-permute-start = (bf16[72,16,128]{2,1,0:T(8,128)(2,1)}, bf16[72,16,128]{2,1,0:T(8,128)(2,1)S(1)}, u32[]{:S(2)}, u32[]{:S(2)}) collective-permute-start(bf16[72,16,128]{2,1,0:T(8,128)(2,1)} %get-tuple-element.8.refs_0_.refs_8_.refs_10_), channel_id=1, source_target_pairs={{0,2},{1,3},{2,0},{3,1},{4,6},{5,7},{6,4},{7,5},{8,10},{9,11},{10,... | collective-permute-start | bytes 884744 | tf_op jit(solution)/shard_map/ppermute | solution.py:44
  35.9 11.0 %collective-permute-start.14 = (bf16[72,16,128]{2,1,0:T(8,128)(2,1)}, bf16[72,16,128]{2,1,0:T(8,128)(2,1)S(1)}, u32[]{:S(2)}, u32[]{:S(2)}) collective-permute-start(bf16[72,16,128]{2,1,0:T(8,128)(2,1)} %get-tuple-element.8.refs_0_.refs_8_.refs_10_), channel_id=1, source_target_pairs={{0,96},{16,112},{32,0},{48,16},{64,32},{80,48},{96,64},{112,80},{1... | collective-permute-start | bytes 884744 | tf_op jit(solution)/shard_map/ppermute | solution.py:34
  37.0 9.9 %collective-permute-start.13 = (bf16[72,16,128]{2,1,0:T(8,128)(2,1)}, bf16[72,16,128]{2,1,0:T(8,128)(2,1)S(1)}, u32[]{:S(2)}, u32[]{:S(2)}) collective-permute-start(bf16[72,16,128]{2,1,0:T(8,128)(2,1)} %get-tuple-element.8.refs_0_.refs_8_.refs_10_), channel_id=1, source_target_pairs={{0,32},{16,48},{32,64},{48,80},{64,96},{80,112},{96,0},{112,16},{1... | collective-permute-start | bytes 884744 | tf_op jit(solution)/shard_map/ppermute | solution.py:34
  38.0 11.4 %copy-start.2 = (bf16[72,16,128]{2,1,0:T(8,128)(2,1)}, bf16[72,16,128]{2,1,0:T(8,128)(2,1)S(1)}, u32[]{:S(2)}) copy-start(bf16[72,16,128]{2,1,0:T(8,128)(2,1)S(1)} %collective-permute-done.2.refs_3_.refs_11_.refs_13_) | copy-start | bytes 884740
  38.0 9.5 %collective-permute-start.12 = (bf16[72,16,128]{2,1,0:T(8,128)(2,1)}, bf16[72,16,128]{2,1,0:T(8,128)(2,1)S(1)}, u32[]{:S(2)}, u32[]{:S(2)}) collective-permute-start(bf16[72,16,128]{2,1,0:T(8,128)(2,1)} %get-tuple-element.8.refs_0_.refs_8_.refs_10_), channel_id=1, source_target_pairs={{0,16},{16,0},{32,48},{48,32},{64,80},{80,64},{96,112},{112,96},{1... | collective-permute-start | bytes 884744 | tf_op jit(solution)/shard_map/ppermute | solution.py:34
  41.3 8.1 %copy-start.3 = (bf16[72,16,128]{2,1,0:T(8,128)(2,1)}, bf16[72,16,128]{2,1,0:T(8,128)(2,1)S(1)}, u32[]{:S(2)}) copy-start(bf16[72,16,128]{2,1,0:T(8,128)(2,1)S(1)} %collective-permute-done.1.refs_2_.refs_10_.refs_12_) | copy-start | bytes 884740
  43.6 5.8 %copy-start.1 = (bf16[72,16,128]{2,1,0:T(8,128)(2,1)}, bf16[72,16,128]{2,1,0:T(8,128)(2,1)S(1)}, u32[]{:S(2)}) copy-start(bf16[72,16,128]{2,1,0:T(8,128)(2,1)S(1)} %collective-permute-done.refs_1_.refs_9_.refs_11_) | copy-start | bytes 884740
  43.7 9.0 %collective-permute-start.4 = (bf16[108,16,128]{2,1,0:T(8,128)(2,1)S(1)}, bf16[108,16,128]{2,1,0:T(8,128)(2,1)S(1)}, u32[]{:S(2)}, u32[]{:S(2)}) collective-permute-start(bf16[108,16,128]{2,1,0:T(8,128)(2,1)S(1)} %get-tuple-element.14), channel_id=1, source_target_pairs={{0,12},{1,13},{2,14},{3,15},{4,0},{5,1},{6,2},{7,3},{8,4},{9,5},{1... | collective-permute-start | bytes 1327112 | tf_op jit(solution)/shard_map/ppermute | solution.py:44
  46.9 9.6 %collective-permute-start.3 = (bf16[108,16,128]{2,1,0:T(8,128)(2,1)S(1)}, bf16[108,16,128]{2,1,0:T(8,128)(2,1)S(1)}, u32[]{:S(2)}, u32[]{:S(2)}) collective-permute-start(bf16[108,16,128]{2,1,0:T(8,128)(2,1)S(1)} %get-tuple-element.15), channel_id=1, source_target_pairs={{0,4},{1,5},{2,6},{3,7},{4,8},{5,9},{6,10},{7,11},{8,12},{9,13},{1... | collective-permute-start | bytes 1327112 | tf_op jit(solution)/shard_map/ppermute | solution.py:44
  46.9 1.3 copy-start.25
  46.9 1.3 copy-start.26
  47.5 0.7 copy-start.18
  48.2 14.7 %copy-start.6 = (bf16[72,16,128]{2,1,0:T(8,128)(2,1)S(1)}, bf16[72,16,128]{2,1,0:T(8,128)(2,1)}, u32[]{:S(2)}) copy-start(bf16[72,16,128]{2,1,0:T(8,128)(2,1)} %get-tuple-element.8.refs_0_.refs_8_.refs_10_) | copy-start | bytes 884740
  48.2 9.3 %collective-permute-start.16 = (bf16[108,16,128]{2,1,0:T(8,128)(2,1)S(1)}, bf16[108,16,128]{2,1,0:T(8,128)(2,1)S(1)}, u32[]{:S(2)}, u32[]{:S(2)}) collective-permute-start(bf16[108,16,128]{2,1,0:T(8,128)(2,1)S(1)} %get-tuple-element.12), channel_id=1, source_target_pairs={{0,96},{16,112},{32,0},{48,16},{64,32},{80,48},{96,64},{112,80},{1... | collective-permute-start | bytes 1327112 | tf_op jit(solution)/shard_map/ppermute | solution.py:34
  50.4 17.9 %collective-permute-start.8 = (bf16[216,16,128]{2,1,0:T(8,128)(2,1)}, bf16[216,16,128]{2,1,0:T(8,128)(2,1)S(1)}, u32[]{:S(2)}, u32[]{:S(2)}) collective-permute-start(bf16[216,16,128]{2,1,0:T(8,128)(2,1)} %pad_maximum_fusion), channel_id=1, source_target_pairs={{0,1},{1,0},{2,3},{3,2},{4,5},{5,4},{6,7},{7,6},{8,9},{9,8},{10,11... | collective-permute-start | bytes 2654216 | tf_op jit(solution)/shard_map/ppermute | solution.py:44
  50.4 13.8 %collective-permute-start.15 = (bf16[108,16,128]{2,1,0:T(8,128)(2,1)S(1)}, bf16[108,16,128]{2,1,0:T(8,128)(2,1)S(1)}, u32[]{:S(2)}, u32[]{:S(2)}) collective-permute-start(bf16[108,16,128]{2,1,0:T(8,128)(2,1)S(1)} %get-tuple-element.13), channel_id=1, source_target_pairs={{0,32},{16,48},{32,64},{48,80},{64,96},{80,112},{96,0},{112,16},{1... | collective-permute-start | bytes 1327112 | tf_op jit(solution)/shard_map/ppermute | solution.py:34
  52.7 15.6 %copy-start.4 = (bf16[108,16,128]{2,1,0:T(8,128)(2,1)}, bf16[108,16,128]{2,1,0:T(8,128)(2,1)S(1)}, u32[]{:S(2)}) copy-start(bf16[108,16,128]{2,1,0:T(8,128)(2,1)S(1)} %collective-permute-done.4.refs_5_.refs_13_.refs_15_) | copy-start | bytes 1327108
  52.7 6.4 %collective-permute-start.6 = (bf16[36,16,128]{2,1,0:T(8,128)(2,1)S(1)}, bf16[36,16,128]{2,1,0:T(8,128)(2,1)S(1)}, u32[]{:S(2)}, u32[]{:S(2)}) collective-permute-start(bf16[36,16,128]{2,1,0:T(8,128)(2,1)S(1)} %slice.51), channel_id=1, source_target_pairs={{0,12},{1,13},{2,14},{3,15},{4,0},{5,1},{6,2},{7,3},{8,4},{9,5},{1... | collective-permute-start | bytes 442376 | tf_op jit(solution)/shard_map/ppermute | solution.py:44
  56.5 11.8 %copy-start.5 = (bf16[108,16,128]{2,1,0:T(8,128)(2,1)}, bf16[108,16,128]{2,1,0:T(8,128)(2,1)S(1)}, u32[]{:S(2)}) copy-start(bf16[108,16,128]{2,1,0:T(8,128)(2,1)S(1)} %collective-permute-done.3.refs_4_.refs_12_.refs_14_) | copy-start | bytes 1327108
  56.5 6.4 %collective-permute-start.5 = (bf16[36,16,128]{2,1,0:T(8,128)(2,1)S(1)}, bf16[36,16,128]{2,1,0:T(8,128)(2,1)S(1)}, u32[]{:S(2)}, u32[]{:S(2)}) collective-permute-start(bf16[36,16,128]{2,1,0:T(8,128)(2,1)S(1)} %slice.50), channel_id=1, source_target_pairs={{0,4},{1,5},{2,6},{3,7},{4,8},{5,9},{6,10},{7,11},{8,12},{9,13},{1... | collective-permute-start | bytes 442376 | tf_op jit(solution)/shard_map/ppermute | solution.py:44
  57.5 9.1 %copy-start.23 = (bf16[108,16,128]{2,1,0:T(8,128)(2,1)}, bf16[108,16,128]{2,1,0:T(8,128)(2,1)S(1)}, u32[]{:S(2)}) copy-start(bf16[108,16,128]{2,1,0:T(8,128)(2,1)S(1)} %collective-permute-done.16.refs_5_) | copy-start | bytes 1327108
  57.5 9.1 %collective-permute-start.10 = (bf16[108,16,128]{2,1,0:T(8,128)(2,1)S(1)}, bf16[108,16,128]{2,1,0:T(8,128)(2,1)S(1)}, u32[]{:S(2)}, u32[]{:S(2)}) collective-permute-start(bf16[108,16,128]{2,1,0:T(8,128)(2,1)S(1)} %collective-permute-done.4.refs_5_.refs_13_.refs_15_), channel_id=1, source_target_pairs={{0,1},{1,0},{2,3},{3,2},{4,5},{5,4},{6,7},{7,6},{8,9},{9,8},{10,11... | collective-permute-start | bytes 1327112 | tf_op jit(solution)/shard_map/ppermute | solution.py:44
  59.2 9.2 %copy-start.15 = (bf16[36,16,128]{2,1,0:T(8,128)(2,1)}, bf16[36,16,128]{2,1,0:T(8,128)(2,1)S(1)}, u32[]{:S(2)}) copy-start(bf16[36,16,128]{2,1,0:T(8,128)(2,1)S(1)} %collective-permute-done.6.refs_7_.refs_15_.refs_17_) | copy-start | bytes 442372
  59.2 9.1 %collective-permute-start.9 = (bf16[108,16,128]{2,1,0:T(8,128)(2,1)S(1)}, bf16[108,16,128]{2,1,0:T(8,128)(2,1)S(1)}, u32[]{:S(2)}, u32[]{:S(2)}) collective-permute-start(bf16[108,16,128]{2,1,0:T(8,128)(2,1)S(1)} %collective-permute-done.3.refs_4_.refs_12_.refs_14_), channel_id=1, source_target_pairs={{0,1},{1,0},{2,3},{3,2},{4,5},{5,4},{6,7},{7,6},{8,9},{9,8},{10,11... | collective-permute-start | bytes 1327112 | tf_op jit(solution)/shard_map/ppermute | solution.py:44
  62.9 5.4 %copy-start.16 = (bf16[36,16,128]{2,1,0:T(8,128)(2,1)}, bf16[36,16,128]{2,1,0:T(8,128)(2,1)S(1)}, u32[]{:S(2)}) copy-start(bf16[36,16,128]{2,1,0:T(8,128)(2,1)S(1)} %collective-permute-done.5.refs_6_.refs_14_.refs_16_) | copy-start | bytes 442372
  62.9 2.7 %collective-permute-start.7 = (bf16[72,16,128]{2,1,0:T(8,128)(2,1)S(1)}, bf16[72,16,128]{2,1,0:T(8,128)(2,1)S(1)}, u32[]{:S(2)}, u32[]{:S(2)}) collective-permute-start(bf16[72,16,128]{2,1,0:T(8,128)(2,1)S(1)} %copy-done.6), channel_id=1, source_target_pairs={{0,1},{1,0},{2,3},{3,2},{4,5},{5,4},{6,7},{7,6},{8,9},{9,8},{10,11... | collective-permute-start | bytes 884744 | tf_op jit(solution)/shard_map/ppermute | solution.py:44
  64.2 3.5 %copy-start.24 = (bf16[108,16,128]{2,1,0:T(8,128)(2,1)}, bf16[108,16,128]{2,1,0:T(8,128)(2,1)S(1)}, u32[]{:S(2)}) copy-start(bf16[108,16,128]{2,1,0:T(8,128)(2,1)S(1)} %collective-permute-done.15.refs_4_) | copy-start | bytes 1327108
  64.2 4.1 %collective-permute-start.11 = (bf16[72,16,128]{2,1,0:T(8,128)(2,1)}, bf16[72,16,128]{2,1,0:T(8,128)(2,1)S(1)}, u32[]{:S(2)}, u32[]{:S(2)}) collective-permute-start(bf16[72,16,128]{2,1,0:T(8,128)(2,1)} %pad_maximum_fusion.5), channel_id=1, source_target_pairs={{0,1},{1,0},{2,3},{3,2},{4,5},{5,4},{6,7},{7,6},{8,9},{9,8},{10,11... | collective-permute-start | bytes 884744 | tf_op jit(solution)/shard_map/ppermute | solution.py:44
  65.6 2.7 %copy-start.9 = (bf16[72,16,128]{2,1,0:T(8,128)(2,1)}, bf16[72,16,128]{2,1,0:T(8,128)(2,1)S(1)}, u32[]{:S(2)}) copy-start(bf16[72,16,128]{2,1,0:T(8,128)(2,1)S(1)} %collective-permute-done.7.refs_8_.refs_16_.refs_18_) | copy-start | bytes 884740
  65.6 6.9 %collective-permute-start.18 = (bf16[36,16,128]{2,1,0:T(8,128)(2,1)}, bf16[36,16,128]{2,1,0:T(8,128)(2,1)}, u32[]{:S(2)}, u32[]{:S(2)}) collective-permute-start(bf16[36,16,128]{2,1,0:T(8,128)(2,1)} %slice.55), channel_id=1, source_target_pairs={{0,96},{16,112},{32,0},{48,16},{64,32},{80,48},{96,64},{112,80},{1... | collective-permute-start | bytes 442376 | tf_op jit(solution)/shard_map/ppermute | solution.py:34
  66.6 1.7 %copy-start.7 = (bf16[108,16,128]{2,1,0:T(8,128)(2,1)}, bf16[108,16,128]{2,1,0:T(8,128)(2,1)S(1)}, u32[]{:S(2)}) copy-start(bf16[108,16,128]{2,1,0:T(8,128)(2,1)S(1)} %collective-permute-done.10.refs_11_.refs_19_.refs_21_) | copy-start | bytes 1327108
  66.6 7.1 %collective-permute-start.17 = (bf16[36,16,128]{2,1,0:T(8,128)(2,1)}, bf16[36,16,128]{2,1,0:T(8,128)(2,1)}, u32[]{:S(2)}, u32[]{:S(2)}) collective-permute-start(bf16[36,16,128]{2,1,0:T(8,128)(2,1)} %slice.54), channel_id=1, source_target_pairs={{0,32},{16,48},{32,64},{48,80},{64,96},{80,112},{96,0},{112,16},{1... | collective-permute-start | bytes 442376 | tf_op jit(solution)/shard_map/ppermute | solution.py:34
  68.3 0.7 copy-start.10
  68.3 0.9 copy-start.8
  68.3 1.1 copy-start
  83.8 10.6 %collective-permute-start.19 = (bf16[100,16,128]{2,1,0:T(8,128)(2,1)}, bf16[100,16,128]{2,1,0:T(8,128)(2,1)S(1)}, u32[]{:S(2)}, u32[]{:S(2)}) collective-permute-start(bf16[100,16,128]{2,1,0:T(8,128)(2,1)} %get-tuple-element.10.refs_0_), channel_id=1, source_target_pairs={{0,16},{16,0},{32,48},{48,32},{64,80},{80,64},{96,112},{112,96},{1... | collective-permute-start | bytes 1228808 | tf_op jit(solution)/shard_map/ppermute | solution.py:34
  85.4 11.1 %collective-permute-start.21 = (bf16[100,16,128]{2,1,0:T(8,128)(2,1)}, bf16[100,16,128]{2,1,0:T(8,128)(2,1)S(1)}, u32[]{:S(2)}, u32[]{:S(2)}) collective-permute-start(bf16[100,16,128]{2,1,0:T(8,128)(2,1)} %get-tuple-element.10.refs_0_), channel_id=1, source_target_pairs={{0,96},{16,112},{32,0},{48,16},{64,32},{80,48},{96,64},{112,80},{1... | collective-permute-start | bytes 1228808 | tf_op jit(solution)/shard_map/ppermute | solution.py:34
  86.3 13.0 %collective-permute-start.20 = (bf16[100,16,128]{2,1,0:T(8,128)(2,1)}, bf16[100,16,128]{2,1,0:T(8,128)(2,1)S(1)}, u32[]{:S(2)}, u32[]{:S(2)}) collective-permute-start(bf16[100,16,128]{2,1,0:T(8,128)(2,1)} %get-tuple-element.10.refs_0_), channel_id=1, source_target_pairs={{0,32},{16,48},{32,64},{48,80},{64,96},{80,112},{96,0},{112,16},{1... | collective-permute-start | bytes 1228808 | tf_op jit(solution)/shard_map/ppermute | solution.py:34
  94.4 22.3 %copy-start.17 = (bf16[100,16,128]{2,1,0:T(8,128)(2,1)}, bf16[100,16,128]{2,1,0:T(8,128)(2,1)S(1)}, u32[]{:S(2)}) copy-start(bf16[100,16,128]{2,1,0:T(8,128)(2,1)S(1)} %collective-permute-done.19.refs_1_) | copy-start | bytes 1228804
  94.4 12.4 %collective-permute-start.23 = (bf16[100,16,128]{2,1,0:T(8,128)(2,1)S(1)}, bf16[100,16,128]{2,1,0:T(8,128)(2,1)S(1)}, u32[]{:S(2)}, u32[]{:S(2)}) collective-permute-start(bf16[100,16,128]{2,1,0:T(8,128)(2,1)S(1)} %collective-permute-done.19.refs_1_), channel_id=1, source_target_pairs={{0,96},{16,112},{32,0},{48,16},{64,32},{80,48},{96,64},{112,80},{1... | collective-permute-start | bytes 1228808 | tf_op jit(solution)/shard_map/ppermute | solution.py:34
  96.0 13.7 %collective-permute-start.22 = (bf16[100,16,128]{2,1,0:T(8,128)(2,1)S(1)}, bf16[100,16,128]{2,1,0:T(8,128)(2,1)S(1)}, u32[]{:S(2)}, u32[]{:S(2)}) collective-permute-start(bf16[100,16,128]{2,1,0:T(8,128)(2,1)S(1)} %collective-permute-done.19.refs_1_), channel_id=1, source_target_pairs={{0,32},{16,48},{32,64},{48,80},{64,96},{80,112},{96,0},{112,16},{1... | collective-permute-start | bytes 1228808 | tf_op jit(solution)/shard_map/ppermute | solution.py:34
  96.5 20.3 %copy-start.11 = (bf16[100,16,128]{2,1,0:T(8,128)(2,1)}, bf16[100,16,128]{2,1,0:T(8,128)(2,1)S(1)}, u32[]{:S(2)}) copy-start(bf16[100,16,128]{2,1,0:T(8,128)(2,1)S(1)} %collective-permute-done.21.refs_3_) | copy-start | bytes 1228804
  96.5 14.5 %collective-permute-start.25 = (bf16[50,16,128]{2,1,0:T(8,128)(2,1)S(1)}, bf16[50,16,128]{2,1,0:T(8,128)(2,1)S(1)}, u32[]{:S(2)}, u32[]{:S(2)}) collective-permute-start(bf16[50,16,128]{2,1,0:T(8,128)(2,1)S(1)} %slice.57), channel_id=1, source_target_pairs={{0,96},{16,112},{32,0},{48,16},{64,32},{80,48},{96,64},{112,80},{1... | collective-permute-start | bytes 614408 | tf_op jit(solution)/shard_map/ppermute | solution.py:34
  99.3 17.4 %copy-start.12 = (bf16[100,16,128]{2,1,0:T(8,128)(2,1)}, bf16[100,16,128]{2,1,0:T(8,128)(2,1)S(1)}, u32[]{:S(2)}) copy-start(bf16[100,16,128]{2,1,0:T(8,128)(2,1)S(1)} %collective-permute-done.20.refs_2_) | copy-start | bytes 1228804
  99.3 14.1 %collective-permute-start.24 = (bf16[50,16,128]{2,1,0:T(8,128)(2,1)S(1)}, bf16[50,16,128]{2,1,0:T(8,128)(2,1)S(1)}, u32[]{:S(2)}, u32[]{:S(2)}) collective-permute-start(bf16[50,16,128]{2,1,0:T(8,128)(2,1)S(1)} %slice.56), channel_id=1, source_target_pairs={{0,32},{16,48},{32,64},{48,80},{64,96},{80,112},{96,0},{112,16},{1... | collective-permute-start | bytes 614408 | tf_op jit(solution)/shard_map/ppermute | solution.py:34
  106.8 9.9 %copy-start.13 = (bf16[100,16,128]{2,1,0:T(8,128)(2,1)}, bf16[100,16,128]{2,1,0:T(8,128)(2,1)S(1)}, u32[]{:S(2)}) copy-start(bf16[100,16,128]{2,1,0:T(8,128)(2,1)S(1)} %collective-permute-done.23.refs_5_) | copy-start | bytes 1228804
  106.9 6.6 %collective-permute-start.27 = (bf16[50,16,128]{2,1,0:T(8,128)(2,1)S(1)}, bf16[50,16,128]{2,1,0:T(8,128)(2,1)S(1)}, u32[]{:S(2)}, u32[]{:S(2)}) collective-permute-start(bf16[50,16,128]{2,1,0:T(8,128)(2,1)S(1)} %slice.59), channel_id=1, source_target_pairs={{0,96},{16,112},{32,0},{48,16},{64,32},{80,48},{96,64},{112,80},{1... | collective-permute-start | bytes 614408 | tf_op jit(solution)/shard_map/ppermute | solution.py:34
  109.7 7.1 %copy-start.14 = (bf16[100,16,128]{2,1,0:T(8,128)(2,1)}, bf16[100,16,128]{2,1,0:T(8,128)(2,1)S(1)}, u32[]{:S(2)}) copy-start(bf16[100,16,128]{2,1,0:T(8,128)(2,1)S(1)} %collective-permute-done.22.refs_4_) | copy-start | bytes 1228804
  109.7 7.0 %collective-permute-start.26 = (bf16[50,16,128]{2,1,0:T(8,128)(2,1)S(1)}, bf16[50,16,128]{2,1,0:T(8,128)(2,1)S(1)}, u32[]{:S(2)}, u32[]{:S(2)}) collective-permute-start(bf16[50,16,128]{2,1,0:T(8,128)(2,1)S(1)} %slice.58), channel_id=1, source_target_pairs={{0,32},{16,48},{32,64},{48,80},{64,96},{80,112},{96,0},{112,16},{1... | collective-permute-start | bytes 614408 | tf_op jit(solution)/shard_map/ppermute | solution.py:34
  111.0 5.8 %copy-start.19 = (bf16[50,16,128]{2,1,0:T(8,128)(2,1)}, bf16[50,16,128]{2,1,0:T(8,128)(2,1)S(1)}, u32[]{:S(2)}) copy-start(bf16[50,16,128]{2,1,0:T(8,128)(2,1)S(1)} %collective-permute-done.25.refs_7_) | copy-start | bytes 614404
  113.5 3.3 %copy-start.20 = (bf16[50,16,128]{2,1,0:T(8,128)(2,1)}, bf16[50,16,128]{2,1,0:T(8,128)(2,1)S(1)}, u32[]{:S(2)}) copy-start(bf16[50,16,128]{2,1,0:T(8,128)(2,1)S(1)} %collective-permute-done.24.refs_6_) | copy-start | bytes 614404
  113.5 3.3 %copy-start.21 = (bf16[50,16,128]{2,1,0:T(8,128)(2,1)}, bf16[50,16,128]{2,1,0:T(8,128)(2,1)S(1)}, u32[]{:S(2)}) copy-start(bf16[50,16,128]{2,1,0:T(8,128)(2,1)S(1)} %collective-permute-done.27.refs_9_) | copy-start | bytes 614404
  116.8 0.7 copy-start.22
  129.1 15.8 %all-to-all-start.1 = ((bf16[64,16,512]{2,1,0:T(8,128)(2,1)}), bf16[64,16,512]{2,1,0:T(8,128)(2,1)S(1)}, u32[]{:S(2)}, u32[]{:S(2)}) async-start(bf16[64,16,512]{2,1,0:T(8,128)(2,1)} %shard_map.64), calls=%async_computation.1 | async-start | bytes 2097152 | tf_op jit(solution)/shard_map/all_to_all | solution.py:443

commit v4 on v3

--- a/solution.py
+++ b/solution.py
@@ -67,7 +67,7 @@
         copy.wait()
 
 
-def pack_kernel(sliced, packed, lists, flags, flags_s, sem):
+def pack_kernel(sliced, packed, flags, flags_s, sem):
     marks = jnp.zeros((SL, BLOCK), jnp.float32)
     for s in range(TR):
         mark = sliced[s, 32].astype(jnp.float32)
@@ -76,9 +76,6 @@
     copy = pltpu.make_async_copy(flags, flags_s, sem)
     copy.start()
     packed[...] = jnp.zeros_like(packed)
-    for n in range(4):
-        for t in range(KP):
-            lists[n, t] = NONE
     copy.wait()
 
     def kept(b, counts):
@@ -86,38 +83,14 @@
             i = 8 * b + q
             out = []
             for n in range(4):
-                lists[n, counts[n]] = i
                 packed[n * SLOTS + counts[n]] = sliced[b, 8 * n + q]
                 out.append(counts[n] + flags_s[n, i])
             counts = tuple(out)
         return counts
 
-    counts = lax.fori_loop(0, TR, kept, (jnp.int32(0),) * 4)
-    for n in range(4):
-        lists[n, counts[n]] = NONE
+    lax.fori_loop(0, TR, kept, (jnp.int32(0),) * 4)
     packed[KP] = marks.astype(BF)
     packed[ZERO] = jnp.zeros((SL, BLOCK), BF)
-
-
-def lists_kernel(flags, *refs):
-    lists = refs[-1]
-    for n in range(8):
-        for t in range(KS):
-            lists[n, t] = NONE
-
-    def kept(b, counts):
-        for q in range(8):
-            i = 8 * b + q
-            out = []
-            for n in range(8):
-                lists[n, counts[n]] = i
-                out.append(counts[n] + flags[4 + n, i])
-            counts = tuple(out)
-        return counts
-
-    counts = lax.fori_loop(0, TR, kept, (jnp.int32(0),) * 8)
-    for n in range(8):
-        lists[n, counts[n]] = NONE
 
 
 def split(layout, slots):
@@ -160,16 +133,36 @@
     return fetch(parts, chosen, target, sems)
 
 
-def product(table, outer, inner, cols, right):
+def product(slot, n_outer, n_inner, cols, right):
     total = None
-    for t in range(0, len(inner), 2):
-        pair = inner[t : t + 2]
+    for t in range(0, n_inner, 2):
+        pair = range(t, min(t + 2, n_inner))
         left = jnp.concatenate(
-            [jnp.concatenate([cols[table[k, i]] for k in pair], axis=1) for i in outer], axis=0
+            [jnp.concatenate([cols[slot(q, s)] for q in pair], axis=1) for s in range(n_outer)], axis=0
         )
         part = jnp.dot(left, right(t, len(pair)), preferred_element_type=jnp.float32)
         total = part if total is None else total + part
     return total
+
+
+def exact_dot(left, right, contract=(1, 0)):
+    dims = (((contract[0],), (contract[1],)), ((), ()))
+    return lax.dot_general(left.astype(BF), right.astype(BF), dims, preferred_element_type=jnp.float32)
+
+
+def picks(flags, ranks, first):
+    at = lax.broadcasted_iota(jnp.int32, (32, BLOCK), 0).astype(jnp.float32)
+    parts = []
+    for n in range(first, first + 4):
+        hit = (at == ranks[n : n + 1]) & (flags[n : n + 1] > 0.5)
+        parts.append(jnp.where(hit, 1.0, 0.0))
+    return jnp.concatenate(parts, axis=0)
+
+
+def slots_of(inner, outer, high, low):
+    parts = [exact_dot(exact_dot(inner, half), outer, (1, 1)) for half in (high, low)]
+    found = 32.0 * parts[0] + parts[1]
+    return jnp.where(found > 0.5, found - 1.0, float(ZERO)).astype(jnp.int32)
 
 
 def fetch_heads(place, parts, heads, sems):
@@ -182,51 +175,72 @@
     return copies
 
 
-def square_kernel(place, inner, outer, *refs):
-    row_parts, col_parts = refs[:NR], refs[NR : NR + NC]
-    square, table, rows, cols, marks, heads, index, col_sems, row_sems, head_sems, sem = refs[NR + NC :]
-    from_heads = fetch_heads(place, col_parts, heads, head_sems)
-    from_cols = fetch_cols(place, col_parts, whole(COLS), cols, col_sems)
-    from_rows = fetch_rows(place, row_parts, whole(ROWS), rows, row_sems)
-    for copy in from_heads + from_cols + from_rows:
+def plan_kernel(place, flags, *refs):
+    square_slots, step_slots, lists, marks, heads, head_sems = refs[NC:]
+    from_heads = fetch_heads(place, refs[:NC], heads, head_sems)
+    for copy in from_heads:
         copy.start()
+    line = lax.broadcasted_iota(jnp.int32, (BLOCK, BLOCK), 0)
+    lane = lax.broadcasted_iota(jnp.int32, (BLOCK, BLOCK), 1)
+    before = jnp.where(line < lane, 1.0, 0.0)
+    mine = flags[...].astype(jnp.float32)
+    ranks = exact_dot(mine, before)
+    of_pattern, of_square, of_step = (picks(mine, ranks, n) for n in (0, 4, 8))
+    own = (line % 32 == 31) & (lane == place[1] * 4 + line // 32)
+    of_step_inner = jnp.where(own, 1.0, of_square)
+    names = (line + 1).astype(jnp.float32)
+    found = exact_dot(of_square, jnp.where(lane < NB, names, 0.0)) + exact_dot(of_step, jnp.where(lane < NB, 0.0, names))
+    lists[...] = jnp.where(found > 0.5, found - 1.0, float(NONE)).astype(jnp.int32)
+    marks[...] = jnp.zeros_like(marks)
     for copy in from_heads:
         copy.wait()
     for c in range(TC):
         marks[4 * c : 4 * c + 4, :] = heads[c].astype(jnp.float32)[0:4]
     kept = marks[...]
-    before = lax.broadcasted_iota(jnp.int32, (BLOCK, BLOCK), 0) < lax.broadcasted_iota(jnp.int32, (BLOCK, BLOCK), 1)
-    rank = jnp.dot(kept.astype(BF), before.astype(jnp.float32).astype(BF), preferred_element_type=jnp.float32)
-    slot = lax.broadcasted_iota(jnp.int32, (NB, BLOCK), 0) * SLOTS + rank.astype(jnp.int32)
-    index[0:NB, :] = jnp.where(kept > 0.5, slot, ZERO)
-    index[NB : NB + 8, :] = jnp.full((8, BLOCK), ZERO, jnp.int32)
-    copy = pltpu.make_async_copy(index, table, sem)
-    copy.start()
-    copy.wait()
-    for copy in from_cols + from_rows:
+    rank = exact_dot(kept, before).astype(jnp.int32)
+    slot = jnp.where(kept > 0.5, line * SLOTS + rank + 1, 0)
+    high = (slot // 32).astype(jnp.float32)
+    low = (slot % 32).astype(jnp.float32)
+    square_slots[...] = slots_of(of_pattern, of_square, high, low)
+    step_slots[...] = slots_of(of_step_inner, of_step, high, low)
+
+
+def square_kernel(place, square_slots, *refs):
+    row_parts, col_parts = refs[:NR], refs[NR : NR + NC]
+    square, rows, cols, slots, col_sems, row_sems, sem = refs[NR + NC :]
+    from_slots = pltpu.make_async_copy(square_slots, slots, sem)
+    from_cols = fetch_cols(place, col_parts, whole(COLS), cols, col_sems)
+    from_rows = fetch_rows(place, row_parts, whole(ROWS), rows, row_sems)
+    for copy in [from_slots] + from_cols + from_rows:
+        copy.start()
+    for copy in [from_slots] + from_cols + from_rows:
         copy.wait()
 
     def column(j, carry):
         def right(t, n):
             return rows[pl.ds(j * SLOTS + t, n)].reshape(n * BLOCK, BLOCK)
 
-        result = product(table, [outer[j, s] for s in range(KS)], [inner[j, t] for t in range(KP)], cols, right)
+        result = product(lambda t, s: slots[j * 32 + t, j * 32 + s], KS, KP, cols, right)
         square[pl.ds(j * KS, KS)] = result.astype(BF).reshape(KS, SL, BLOCK)
         return carry
 
     lax.fori_loop(0, 4, column, 0)
 
 
-def step_kernel(place, inner, table, *refs):
+def step_kernel(place, all_lists, step_slots, *refs):
     row_parts, col_parts = refs[:NS], refs[NS : NS + NC]
-    stepped, rows, cols, results, col_sems, row_sems, out_sems = refs[NS + NC :]
+    stepped, rows, cols, results, slots, lists, col_sems, row_sems, out_sems, sems = refs[NS + NC :]
     from_cols = fetch_cols(place, col_parts, whole(COLS), cols, col_sems)
     from_rows = [
         fetch_rows(place, row_parts, column, rows, row_sems.at[j]) for j, column in enumerate(split(SQUARES, KS))
     ]
-    for copy in from_cols + sum(from_rows, []):
+    tables = [
+        pltpu.make_async_copy(step_slots, slots, sems.at[0]),
+        pltpu.make_async_copy(all_lists, lists, sems.at[1]),
+    ]
+    for copy in tables + from_cols + sum(from_rows, []):
         copy.start()
-    for copy in from_cols:
+    for copy in tables + from_cols:
         copy.wait()
     out = []
     for j in range(4):
@@ -236,15 +250,14 @@
         def right(t, n):
             return rows[j * KS + t : j * KS + t + n].reshape(n * BLOCK, BLOCK)
 
-        outer = [inner[4 + j, s] for s in range(KT)]
-        second = product(table, outer, [inner[j, t] for t in range(KS)], cols, right)
+        second = product(lambda t, s: slots[j * 32 + t, j * 32 + s], KT, KS, cols, right)
         if j >= 2:
             out[j - 2].wait()
         result = results.at[j % 2]
         result[...] = jnp.zeros_like(result)
-        for s, i in enumerate(outer):
-            own = cols[table[place[1] * 4 + j, i]].astype(jnp.float32)
-            result[i] = (1.5 * own - 0.5 * second[s * SL : (s + 1) * SL]).astype(BF)
+        for s in range(KT):
+            own = cols[slots[j * 32 + 31, j * 32 + s]].astype(jnp.float32)
+            result[lists[32 * j + s, NB]] = (1.5 * own - 0.5 * second[s * SL : (s + 1) * SL]).astype(BF)
         out.append(
             pltpu.make_async_copy(
                 result.at[pl.ds(0, NB)], stepped.at[:, :, pl.ds(j * BLOCK, BLOCK)], out_sems.at[j]
@@ -267,7 +280,7 @@
     for j in range(4):
 
         def one(s, carry):
-            i = lists[j, s]
+            i = lists[32 * j + s, 0]
 
             @pl.when(i // 8 == place[0])
             def _():
@@ -382,64 +395,71 @@
     )(density.reshape(8, TR, SL, 4 * BLOCK), pattern.T, square_filter.T, step_filter.T)
     sliced = lax.all_to_all(sent, "row", 0, 0, tiled=True)
 
-    packed, pattern_lists, flags = call(
+    packed, flags = call(
         pack_kernel,
         (
             jax.ShapeDtypeStruct((PACK, SL, BLOCK), BF),
-            jax.ShapeDtypeStruct((4, 32), jnp.int32),
             jax.ShapeDtypeStruct((SL, BLOCK), jnp.int32),
         ),
         [VMEM],
-        (VMEM, SMEM, VMEM),
+        (VMEM, VMEM),
         [pltpu.SMEM((SL, BLOCK), jnp.int32), pltpu.SemaphoreType.DMA],
         0,
         2 << 20,
     )(sliced)
     row_parts = ring_merged(packed, row_shift)
     col_parts = gather_cols(packed)
-    lists = call(
-        lists_kernel, jax.ShapeDtypeStruct((8, 32), jnp.int32), [SMEM] + [ANY] * NC, SMEM, [], 1048576, 12582912
-    )(flags, *col_parts)
-    square_packed, table = call(
+    table = jax.ShapeDtypeStruct((BLOCK, BLOCK), jnp.int32)
+    square_slots, step_slots, lists = call(
+        plan_kernel,
+        (table, table, table),
+        [SMEM, VMEM] + [ANY] * NC,
+        (VMEM, VMEM, VMEM),
+        [
+            pltpu.VMEM((BLOCK, BLOCK), jnp.float32),
+            pltpu.VMEM((TC, SL, BLOCK), BF),
+            pltpu.SemaphoreType.DMA((TC,)),
+        ],
+        1048576,
+        12582912,
+    )(place, flags, *col_parts)
+    square_packed = call(
         square_kernel,
-        (
-            jax.ShapeDtypeStruct((4 * KS, SL, BLOCK), BF),
-            jax.ShapeDtypeStruct((NB + 8, BLOCK), jnp.int32),
-        ),
-        [SMEM] * 3 + [ANY] * (NR + NC),
-        (VMEM, SMEM),
+        jax.ShapeDtypeStruct((4 * KS, SL, BLOCK), BF),
+        [SMEM] + [ANY] * (1 + NR + NC),
+        VMEM,
         [
             pltpu.VMEM((PACK, TR, SL, BLOCK), BF),
             pltpu.VMEM((TC * PACK, SL, BLOCK), BF),
-            pltpu.VMEM((NB, BLOCK), jnp.float32),
-            pltpu.VMEM((TC, SL, BLOCK), BF),
-            pltpu.VMEM((NB + 8, BLOCK), jnp.int32),
+            pltpu.SMEM((BLOCK, BLOCK), jnp.int32),
             pltpu.SemaphoreType.DMA((pieces(COLS),)),
             pltpu.SemaphoreType.DMA((pieces(ROWS),)),
-            pltpu.SemaphoreType.DMA((TC,)),
             pltpu.SemaphoreType.DMA,
         ],
         2 * 4 * KS * SL * KP * BLOCK * BLOCK,
         9 << 20,
-    )(place, pattern_lists, lists, *row_parts, *col_parts)
+    )(place, square_slots, *row_parts, *col_parts)
 
     square_parts = gather_rows(square_packed)
     stepped = call(
         step_kernel,
         jax.ShapeDtypeStruct((NB, SL, 4 * BLOCK), BF),
-        [SMEM] * 3 + [ANY] * (NS + NC),
+        [SMEM] + [ANY] * (2 + NS + NC),
         ANY,
         [
             pltpu.VMEM((4 * KS, TR, SL, BLOCK), BF),
             pltpu.VMEM((TC * PACK, SL, BLOCK), BF),
             pltpu.VMEM((2, NB + 8, SL, BLOCK), BF),
+            pltpu.SMEM((BLOCK, BLOCK), jnp.int32),
+            pltpu.SMEM((BLOCK, BLOCK), jnp.int32),
             pltpu.SemaphoreType.DMA((pieces(COLS),)),
             pltpu.SemaphoreType.DMA((4, TR)),
             pltpu.SemaphoreType.DMA((4,)),
+            pltpu.SemaphoreType.DMA((2,)),
         ],
         2 * 4 * KT * SL * KS * BLOCK * BLOCK,
         9 << 20,
-    )(place, lists, table, *square_parts, *col_parts)
+    )(place, lists, step_slots, *square_parts, *col_parts)
     back = lax.all_to_all(stepped, "row", 0, 0, tiled=True)
     square = call(
         square_rows_kernel,

time: 148 us -> 145 us (0.980)
  Pallas kernels: 37 us -> 34.6 us
    pallas_call x3, Pallas kernels: 24.7 us -> 21.9 us  [the longest x1 10.6 us: on_device(): call(step_kernel, jax.ShapeDtypeStruct((NB, SL, 4 * BLOCK), BF), [SMEM] +...]
  transfers between devices with their start and end apart: 29 -> 29, of which waited for: 16 -> 16; matrix products, arithmetic and copies ran while one was open for 3% -> 3% of each run, Pallas kernels for 6% -> 7%
where the time goes in v4:
time: 145 us; the launch traced here: 143 us
  waiting for transfers between devices  42.4 us (29%)
  starting transfers between devices  35.8 us (25%)
  Pallas kernels  34.6 us (24%)
  blocking collectives  21.8 us (15%)
  local copies, waits for them, and re-layouts  4.99 us (3%)
  other arithmetic  2.44 us (2%)
    ppermute x16, waiting for transfers between devices, row_shift(): return lax.ppermute(value, 'row', pairs)  25.1 us
    all_to_all x1, blocking collectives, on_device(): sliced = lax.all_to_all(sent, 'row', 0, 0, tiled=True)  21.8 us
    ppermute x16, starting transfers between devices, row_shift(): return lax.ppermute(value, 'row', pairs)  18.2 us
    ppermute x12, starting transfers between devices, col_shift(): return lax.ppermute(value, 'col', pairs)  14 us
    ppermute x12, waiting for transfers between devices, col_shift(): return lax.ppermute(value, 'col', pairs)  11.7 us
    pallas_call x1, Pallas kernels, on_device(): call(step_kernel, jax.ShapeDtypeStruct((NB, SL, 4 * BLOCK), BF), [SMEM] +...  10.6 us
    pallas_call x1, Pallas kernels, on_device(): call(square_kernel, jax.ShapeDtypeStruct((4 * KS, SL, BLOCK), BF), [SMEM]...  8.4 us
    pallas_call x1, Pallas kernels, on_device(): call(square_rows_kernel, jax.ShapeDtypeStruct((8, TR, SL, 4 * BLOCK), BF)...  6.81 us
  transfers between devices with their start and end apart: 29, of which 16 were waited for; matrix products, arithmetic and copies ran while one was open for 3% of the time, Pallas kernels for 7%

profile of v4, /device:TPU:0, one launch (start us, length us, event | category | flops | bytes accessed | tf_op | source)
XLA Modules:
  0.0 143.0 jit_solution(14873959993421800528)
XLA Ops:
  0.6 2.5 %shard_map.59 = bf16[8,33,16,128]{3,2,1,0:T(8,128)(2,1)} custom-call(bf16[8,8,16,512]{3,2,1,0:T(8,128)(2,1)} %bitcast.13, s32[4,8]{1,0:T(4,128)} %bitcast.15, s32[4,8]{1,0:T(4,128)} %bitcast.16, s32[4,8]{1,0:T(4,128)} %bitcast.17), custom_call_target="tpu_custom_call" | custom-call | bytes 2097152 | tf_op jit(solution)/shard_map/pallas_call | solution.py:387
  3.2 21.8 %all_to_all.10.sliced = bf16[8,33,16,128]{3,2,1,0:T(8,128)(2,1)} all-to-all(bf16[8,33,16,128]{3,2,1,0:T(8,128)(2,1)} %shard_map.59), channel_id=1, replica_groups=mesh['row'=8,'col'=16] {'row'}, dimensions={0} | all-to-all | bytes 2162688 | tf_op jit(solution)/shard_map/all_to_all | solution.py:396
  25.0 3.4 %shard_map.60 = (bf16[72,16,128]{2,1,0:T(8,128)(2,1)}, s32[16,128]{1,0:T(8,128)}) custom-call(bf16[8,33,16,128]{3,2,1,0:T(8,128)(2,1)} %all_to_all.10.sliced), custom_call_target="tpu_custom_call" | custom-call | bytes 2097152 | tf_op jit(solution)/shard_map/pallas_call | solution.py:398
  28.4 4.1 %collective-permute-start.2 = (bf16[72,16,128]{2,1,0:T(8,128)(2,1)}, bf16[72,16,128]{2,1,0:T(8,128)(2,1)S(1)}, u32[]{:S(2)}, u32[]{:S(2)}) collective-permute-start(bf16[72,16,128]{2,1,0:T(8,128)(2,1)} %get-tuple-element.8.refs_0_.refs_8_.refs_10_), channel_id=1, source_target_pairs={{0,12},{1,13},{2,14},{3,15},{4,0},{5,1},{6,2},{7,3},{8,4},{9,5},{1... | collective-permute-start | bytes 884744 | tf_op jit(solution)/shard_map/ppermute | solution.py:44
  32.5 2.9 %collective-permute-start = (bf16[72,16,128]{2,1,0:T(8,128)(2,1)}, bf16[72,16,128]{2,1,0:T(8,128)(2,1)S(1)}, u32[]{:S(2)}, u32[]{:S(2)}) collective-permute-start(bf16[72,16,128]{2,1,0:T(8,128)(2,1)} %get-tuple-element.8.refs_0_.refs_8_.refs_10_), channel_id=1, source_target_pairs={{0,2},{1,3},{2,0},{3,1},{4,6},{5,7},{6,4},{7,5},{8,10},{9,11},{10,... | collective-permute-start | bytes 884744 | tf_op jit(solution)/shard_map/ppermute | solution.py:44
  35.4 1.2 collective-permute-start.14
  36.5 0.9 collective-permute-start.13
  37.4 0.1 collective-permute-done.2.refs_3_.refs_11_.refs_13_
  37.5 0.8 collective-permute-start.12
  38.4 2.5 %collective-permute-done.1.refs_2_.refs_10_.refs_12_ = bf16[72,16,128]{2,1,0:T(8,128)(2,1)S(1)} collective-permute-done((bf16[72,16,128]{2,1,0:T(8,128)(2,1)}, bf16[72,16,128]{2,1,0:T(8,128)(2,1)S(1)}, u32[]{:S(2)}, u32[]{:S(2)}) %collective-permute-start.1) | collective-permute-done | bytes 294944 | tf_op jit(solution)/shard_map/ppermute | solution.py:44
  40.9 2.3 %collective-permute-done.refs_1_.refs_9_.refs_11_ = bf16[72,16,128]{2,1,0:T(8,128)(2,1)S(1)} collective-permute-done((bf16[72,16,128]{2,1,0:T(8,128)(2,1)}, bf16[72,16,128]{2,1,0:T(8,128)(2,1)S(1)}, u32[]{:S(2)}, u32[]{:S(2)}) %collective-permute-start) | collective-permute-done | bytes 294944 | tf_op jit(solution)/shard_map/ppermute | solution.py:44
  43.2 0.1 pad_maximum_fusion.1
  43.2 3.2 %collective-permute-start.4 = (bf16[108,16,128]{2,1,0:T(8,128)(2,1)S(1)}, bf16[108,16,128]{2,1,0:T(8,128)(2,1)S(1)}, u32[]{:S(2)}, u32[]{:S(2)}) collective-permute-start(bf16[108,16,128]{2,1,0:T(8,128)(2,1)S(1)} %get-tuple-element.14), channel_id=1, source_target_pairs={{0,12},{1,13},{2,14},{3,15},{4,0},{5,1},{6,2},{7,3},{8,4},{9,5},{1... | collective-permute-start | bytes 1327112 | tf_op jit(solution)/shard_map/ppermute | solution.py:44
  46.4 0.0 collective-permute-start.3
  46.4 0.0 collective-permute-done.13.refs_2_
  46.5 0.5 collective-permute-done.12.refs_1_
  47.0 0.1 pad_maximum_fusion.3
  47.1 0.7 copy-done.18
  47.8 1.2 collective-permute-start.16
  48.9 1.0 pad_maximum_fusion
  49.9 0.9 collective-permute-start.15
  50.8 1.4 collective-permute-done.4.refs_5_.refs_13_.refs_15_
  52.3 3.8 %collective-permute-start.6 = (bf16[36,16,128]{2,1,0:T(8,128)(2,1)S(1)}, bf16[36,16,128]{2,1,0:T(8,128)(2,1)S(1)}, u32[]{:S(2)}, u32[]{:S(2)}) collective-permute-start(bf16[36,16,128]{2,1,0:T(8,128)(2,1)S(1)} %slice.51), channel_id=1, source_target_pairs={{0,12},{1,13},{2,14},{3,15},{4,0},{5,1},{6,2},{7,3},{8,4},{9,5},{1... | collective-permute-start | bytes 442376 | tf_op jit(solution)/shard_map/ppermute | solution.py:44
  56.0 0.0 collective-permute-done.3.refs_4_.refs_12_.refs_14_
  56.0 0.1 collective-permute-start.5
  56.1 0.9 collective-permute-done.16.refs_5_
  57.1 0.0 collective-permute-start.10
  57.1 1.6 %collective-permute-done.6.refs_7_.refs_15_.refs_17_ = bf16[36,16,128]{2,1,0:T(8,128)(2,1)S(1)} collective-permute-done((bf16[36,16,128]{2,1,0:T(8,128)(2,1)S(1)}, bf16[36,16,128]{2,1,0:T(8,128)(2,1)S(1)}, u32[]{:S(2)}, u32[]{:S(2)}) %collective-permute-start.6) | collective-permute-done | bytes 147488 | tf_op jit(solution)/shard_map/ppermute | solution.py:44
  58.7 0.0 collective-permute-start.9
  58.7 3.8 %collective-permute-done.5.refs_6_.refs_14_.refs_16_ = bf16[36,16,128]{2,1,0:T(8,128)(2,1)S(1)} collective-permute-done((bf16[36,16,128]{2,1,0:T(8,128)(2,1)S(1)}, bf16[36,16,128]{2,1,0:T(8,128)(2,1)S(1)}, u32[]{:S(2)}, u32[]{:S(2)}) %collective-permute-start.5) | collective-permute-done | bytes 147488 | tf_op jit(solution)/shard_map/ppermute | solution.py:44
  62.5 0.8 pad_maximum_fusion.5
  63.2 0.5 collective-permute-done.15.refs_4_
  63.7 0.7 slice.55
  64.5 0.7 slice.54
  65.1 1.0 collective-permute-start.18
  66.1 1.1 collective-permute-start.17
  67.2 0.6 pad_add_fusion.place
  67.8 0.0 copy-start
  67.9 0.6 copy-done.10
  68.5 0.1 copy-done.8
  68.7 0.3 copy-done
  68.9 2.9 %shard_map.61 = (s32[128,128]{1,0:T(8,128)}, s32[128,128]{1,0:T(8,128)}, s32[128,128]{1,0:T(8,128)}) custom-call(s32[2]{0:T(128)} %pad_add_fusion.place, s32[16,128]{1,0:T(8,128)} %get-tuple-element.7.flags, bf16[72,16,128]{2,1,0:T(8,128)(2,1)} %get-tuple-element.8.refs_0_.refs_8_.refs_10_, bf16[72,16,128]{2,1,0:T(8,128)(2,1)} %copy-done.1, ...), custom_call_target="tpu_custom_call" | custom-call | flops 1048576 | bytes 12582912 | tf_op jit(solution)/shard_map/pallas_call | solution.py:413
  71.8 1.4 %collective-permute-done.17.refs_6_ = bf16[36,16,128]{2,1,0:T(8,128)(2,1)} collective-permute-done((bf16[36,16,128]{2,1,0:T(8,128)(2,1)}, bf16[36,16,128]{2,1,0:T(8,128)(2,1)}, u32[]{:S(2)}, u32[]{:S(2)}) %collective-permute-start.17) | collective-permute-done | bytes 147488 | tf_op jit(solution)/shard_map/ppermute | solution.py:34
  73.3 8.4 %shard_map.62.refs_0_ = bf16[100,16,128]{2,1,0:T(8,128)(2,1)} custom-call(s32[2]{0:T(128)} %pad_add_fusion.place, s32[128,128]{1,0:T(8,128)} %get-tuple-element.10.square_slots, bf16[72,16,128]{2,1,0:T(8,128)(2,1)} %get-tuple-element.8.refs_0_.refs_8_.refs_10_, bf16[72,16,128]{2,1,0:T(8,128)(2,1)} %copy-done.18, bf16[72,16,128]{2,1,0:T(8,128)(2,1)} %copy-done.26, ...), custom_call_target="tpu_custom_call" | custom-call | flops 891289600 | bytes 9437184 | tf_op jit(solution)/shard_map/pallas_call | solution.py:426
  81.7 1.5 %collective-permute-start.19 = (bf16[100,16,128]{2,1,0:T(8,128)(2,1)}, bf16[100,16,128]{2,1,0:T(8,128)(2,1)S(1)}, u32[]{:S(2)}, u32[]{:S(2)}) collective-permute-start(bf16[100,16,128]{2,1,0:T(8,128)(2,1)} %shard_map.62.refs_0_), channel_id=1, source_target_pairs={{0,16},{16,0},{32,48},{48,32},{64,80},{80,64},{96,112},{112,96},{1... | collective-permute-start | bytes 1228808 | tf_op jit(solution)/shard_map/ppermute | solution.py:34
  83.2 0.8 collective-permute-start.21
  84.0 1.2 collective-permute-start.20
  85.2 7.1 %collective-permute-done.19.refs_1_ = bf16[100,16,128]{2,1,0:T(8,128)(2,1)S(1)} collective-permute-done((bf16[100,16,128]{2,1,0:T(8,128)(2,1)}, bf16[100,16,128]{2,1,0:T(8,128)(2,1)S(1)}, u32[]{:S(2)}, u32[]{:S(2)}) %collective-permute-start.19) | collective-permute-done | bytes 409632 | tf_op jit(solution)/shard_map/ppermute | solution.py:34
  92.3 1.4 collective-permute-start.23
  93.7 0.6 collective-permute-start.22
  94.4 2.7 %collective-permute-start.25 = (bf16[50,16,128]{2,1,0:T(8,128)(2,1)S(1)}, bf16[50,16,128]{2,1,0:T(8,128)(2,1)S(1)}, u32[]{:S(2)}, u32[]{:S(2)}) collective-permute-start(bf16[50,16,128]{2,1,0:T(8,128)(2,1)S(1)} %slice.57), channel_id=1, source_target_pairs={{0,96},{16,112},{32,0},{48,16},{64,32},{80,48},{96,64},{112,80},{1... | collective-permute-start | bytes 614408 | tf_op jit(solution)/shard_map/ppermute | solution.py:34
  97.0 0.1 collective-permute-start.24
  97.1 7.6 %collective-permute-done.23.refs_5_ = bf16[100,16,128]{2,1,0:T(8,128)(2,1)S(1)} collective-permute-done((bf16[100,16,128]{2,1,0:T(8,128)(2,1)S(1)}, bf16[100,16,128]{2,1,0:T(8,128)(2,1)S(1)}, u32[]{:S(2)}, u32[]{:S(2)}) %collective-permute-start.23) | collective-permute-done | bytes 409632 | tf_op jit(solution)/shard_map/ppermute | solution.py:34
  104.7 2.8 %collective-permute-start.27 = (bf16[50,16,128]{2,1,0:T(8,128)(2,1)S(1)}, bf16[50,16,128]{2,1,0:T(8,128)(2,1)S(1)}, u32[]{:S(2)}, u32[]{:S(2)}) collective-permute-start(bf16[50,16,128]{2,1,0:T(8,128)(2,1)S(1)} %slice.59), channel_id=1, source_target_pairs={{0,96},{16,112},{32,0},{48,16},{64,32},{80,48},{96,64},{112,80},{1... | collective-permute-start | bytes 614408 | tf_op jit(solution)/shard_map/ppermute | solution.py:34
  107.6 0.1 collective-permute-start.26
  107.7 1.2 collective-permute-done.25.refs_7_
  108.8 2.4 %collective-permute-done.24.refs_6_ = bf16[50,16,128]{2,1,0:T(8,128)(2,1)S(1)} collective-permute-done((bf16[50,16,128]{2,1,0:T(8,128)(2,1)S(1)}, bf16[50,16,128]{2,1,0:T(8,128)(2,1)S(1)}, u32[]{:S(2)}, u32[]{:S(2)}) %collective-permute-start.24) | collective-permute-done | bytes 204832 | tf_op jit(solution)/shard_map/ppermute | solution.py:34
  111.2 3.4 %collective-permute-done.26.refs_8_ = bf16[50,16,128]{2,1,0:T(8,128)(2,1)S(1)} collective-permute-done((bf16[50,16,128]{2,1,0:T(8,128)(2,1)S(1)}, bf16[50,16,128]{2,1,0:T(8,128)(2,1)S(1)}, u32[]{:S(2)}, u32[]{:S(2)}) %collective-permute-start.26) | collective-permute-done | bytes 204832 | tf_op jit(solution)/shard_map/ppermute | solution.py:34
  114.7 0.6 copy-done.22
  115.3 10.6 %shard_map.64 = bf16[64,16,512]{2,1,0:T(8,128)(2,1)} custom-call(s32[2]{0:T(128)} %pad_add_fusion.place, s32[128,128]{1,0:T(8,128)} %get-tuple-element.9.lists.all_lists, s32[128,128]{1,0:T(8,128)} %get-tuple-element.11.step_slots, bf16[100,16,128]{2,1,0:T(8,128)(2,1)} %shard_map.62.refs_0_, bf16[100,16,128]{2,1,0:T(8,128)(2,1)} %copy-done.17, ...), custom_call_target="tpu_custom_call" | custom-call | flops 1101004800 | bytes 9437184 | tf_op jit(solution)/shard_map/pallas_call | solution.py:444
  125.9 3.6 %all-to-all-start.1 = ((bf16[64,16,512]{2,1,0:T(8,128)(2,1)}), bf16[64,16,512]{2,1,0:T(8,128)(2,1)S(1)}, u32[]{:S(2)}, u32[]{:S(2)}) async-start(bf16[64,16,512]{2,1,0:T(8,128)(2,1)} %shard_map.64), calls=%async_computation.1 | async-start | bytes 2097152 | tf_op jit(solution)/shard_map/all_to_all | solution.py:463
  129.5 6.8 %shard_map.63 = bf16[8,8,16,512]{3,2,1,0:T(8,128)(2,1)} custom-call(s32[2]{0:T(128)} %pad_add_fusion.place, s32[128,128]{1,0:T(8,128)} %get-tuple-element.9.lists.all_lists, bf16[100,16,128]{2,1,0:T(8,128)(2,1)} %shard_map.62.refs_0_, bf16[100,16,128]{2,1,0:T(8,128)(2,1)} %copy-done.17, bf16[100,16,128]{2,1,0:T(8,128)(2,1)} %copy-done.12, ...), custom_call_target="tpu_custom_call" | custom-call | bytes 4194304 | tf_op jit(solution)/shard_map/pallas_call | solution.py:464
  136.3 5.5 %all-to-all-done.1 = bf16[64,16,512]{2,1,0:T(8,128)(2,1)S(1)} async-done(((bf16[64,16,512]{2,1,0:T(8,128)(2,1)}), bf16[64,16,512]{2,1,0:T(8,128)(2,1)S(1)}, u32[]{:S(2)}, u32[]{:S(2)}) %all-to-all-start.1) | async-done | bytes 1048608 | tf_op jit(solution)/shard_map/all_to_all | solution.py:463
  141.9 1.1 copy.6
  (73 shorter events, 0.2 us)
Async XLA Ops:
  28.4 9.2 %collective-permute-start.2 = (bf16[72,16,128]{2,1,0:T(8,128)(2,1)}, bf16[72,16,128]{2,1,0:T(8,128)(2,1)S(1)}, u32[]{:S(2)}, u32[]{:S(2)}) collective-permute-start(bf16[72,16,128]{2,1,0:T(8,128)(2,1)} %get-tuple-element.8.refs_0_.refs_8_.refs_10_), channel_id=1, source_target_pairs={{0,12},{1,13},{2,14},{3,15},{4,0},{5,1},{6,2},{7,3},{8,4},{9,5},{1... | collective-permute-start | bytes 884744 | tf_op jit(solution)/shard_map/ppermute | solution.py:44
  32.5 8.4 %collective-permute-start.1 = (bf16[72,16,128]{2,1,0:T(8,128)(2,1)}, bf16[72,16,128]{2,1,0:T(8,128)(2,1)S(1)}, u32[]{:S(2)}, u32[]{:S(2)}) collective-permute-start(bf16[72,16,128]{2,1,0:T(8,128)(2,1)} %get-tuple-element.8.refs_0_.refs_8_.refs_10_), channel_id=1, source_target_pairs={{0,4},{1,5},{2,6},{3,7},{4,8},{5,9},{6,10},{7,11},{8,12},{9,13},{1... | collective-permute-start | bytes 884744 | tf_op jit(solution)/shard_map/ppermute | solution.py:44
  32.5 10.7 %collective-permute-start = (bf16[72,16,128]{2,1,0:T(8,128)(2,1)}, bf16[72,16,128]{2,1,0:T(8,128)(2,1)S(1)}, u32[]{:S(2)}, u32[]{:S(2)}) collective-permute-start(bf16[72,16,128]{2,1,0:T(8,128)(2,1)} %get-tuple-element.8.refs_0_.refs_8_.refs_10_), channel_id=1, source_target_pairs={{0,2},{1,3},{2,0},{3,1},{4,6},{5,7},{6,4},{7,5},{8,10},{9,11},{10,... | collective-permute-start | bytes 884744 | tf_op jit(solution)/shard_map/ppermute | solution.py:44
  35.4 11.0 %collective-permute-start.14 = (bf16[72,16,128]{2,1,0:T(8,128)(2,1)}, bf16[72,16,128]{2,1,0:T(8,128)(2,1)S(1)}, u32[]{:S(2)}, u32[]{:S(2)}) collective-permute-start(bf16[72,16,128]{2,1,0:T(8,128)(2,1)} %get-tuple-element.8.refs_0_.refs_8_.refs_10_), channel_id=1, source_target_pairs={{0,96},{16,112},{32,0},{48,16},{64,32},{80,48},{96,64},{112,80},{1... | collective-permute-start | bytes 884744 | tf_op jit(solution)/shard_map/ppermute | solution.py:34
  36.5 9.9 %collective-permute-start.13 = (bf16[72,16,128]{2,1,0:T(8,128)(2,1)}, bf16[72,16,128]{2,1,0:T(8,128)(2,1)S(1)}, u32[]{:S(2)}, u32[]{:S(2)}) collective-permute-start(bf16[72,16,128]{2,1,0:T(8,128)(2,1)} %get-tuple-element.8.refs_0_.refs_8_.refs_10_), channel_id=1, source_target_pairs={{0,32},{16,48},{32,64},{48,80},{64,96},{80,112},{96,0},{112,16},{1... | collective-permute-start | bytes 884744 | tf_op jit(solution)/shard_map/ppermute | solution.py:34
  37.5 11.4 %copy-start.2 = (bf16[72,16,128]{2,1,0:T(8,128)(2,1)}, bf16[72,16,128]{2,1,0:T(8,128)(2,1)S(1)}, u32[]{:S(2)}) copy-start(bf16[72,16,128]{2,1,0:T(8,128)(2,1)S(1)} %collective-permute-done.2.refs_3_.refs_11_.refs_13_) | copy-start | bytes 884740
  37.5 9.5 %collective-permute-start.12 = (bf16[72,16,128]{2,1,0:T(8,128)(2,1)}, bf16[72,16,128]{2,1,0:T(8,128)(2,1)S(1)}, u32[]{:S(2)}, u32[]{:S(2)}) collective-permute-start(bf16[72,16,128]{2,1,0:T(8,128)(2,1)} %get-tuple-element.8.refs_0_.refs_8_.refs_10_), channel_id=1, source_target_pairs={{0,16},{16,0},{32,48},{48,32},{64,80},{80,64},{96,112},{112,96},{1... | collective-permute-start | bytes 884744 | tf_op jit(solution)/shard_map/ppermute | solution.py:34
  40.8 8.1 %copy-start.3 = (bf16[72,16,128]{2,1,0:T(8,128)(2,1)}, bf16[72,16,128]{2,1,0:T(8,128)(2,1)S(1)}, u32[]{:S(2)}) copy-start(bf16[72,16,128]{2,1,0:T(8,128)(2,1)S(1)} %collective-permute-done.1.refs_2_.refs_10_.refs_12_) | copy-start | bytes 884740
  43.2 5.8 %copy-start.1 = (bf16[72,16,128]{2,1,0:T(8,128)(2,1)}, bf16[72,16,128]{2,1,0:T(8,128)(2,1)S(1)}, u32[]{:S(2)}) copy-start(bf16[72,16,128]{2,1,0:T(8,128)(2,1)S(1)} %collective-permute-done.refs_1_.refs_9_.refs_11_) | copy-start | bytes 884740
  43.2 9.0 %collective-permute-start.4 = (bf16[108,16,128]{2,1,0:T(8,128)(2,1)S(1)}, bf16[108,16,128]{2,1,0:T(8,128)(2,1)S(1)}, u32[]{:S(2)}, u32[]{:S(2)}) collective-permute-start(bf16[108,16,128]{2,1,0:T(8,128)(2,1)S(1)} %get-tuple-element.14), channel_id=1, source_target_pairs={{0,12},{1,13},{2,14},{3,15},{4,0},{5,1},{6,2},{7,3},{8,4},{9,5},{1... | collective-permute-start | bytes 1327112 | tf_op jit(solution)/shard_map/ppermute | solution.py:44
  46.4 9.6 %collective-permute-start.3 = (bf16[108,16,128]{2,1,0:T(8,128)(2,1)S(1)}, bf16[108,16,128]{2,1,0:T(8,128)(2,1)S(1)}, u32[]{:S(2)}, u32[]{:S(2)}) collective-permute-start(bf16[108,16,128]{2,1,0:T(8,128)(2,1)S(1)} %get-tuple-element.15), channel_id=1, source_target_pairs={{0,4},{1,5},{2,6},{3,7},{4,8},{5,9},{6,10},{7,11},{8,12},{9,13},{1... | collective-permute-start | bytes 1327112 | tf_op jit(solution)/shard_map/ppermute | solution.py:44
  46.4 1.3 copy-start.25
  46.5 1.3 copy-start.26
  47.0 0.7 copy-start.18
  47.8 14.7 %copy-start.6 = (bf16[72,16,128]{2,1,0:T(8,128)(2,1)S(1)}, bf16[72,16,128]{2,1,0:T(8,128)(2,1)}, u32[]{:S(2)}) copy-start(bf16[72,16,128]{2,1,0:T(8,128)(2,1)} %get-tuple-element.8.refs_0_.refs_8_.refs_10_) | copy-start | bytes 884740
  47.8 9.3 %collective-permute-start.16 = (bf16[108,16,128]{2,1,0:T(8,128)(2,1)S(1)}, bf16[108,16,128]{2,1,0:T(8,128)(2,1)S(1)}, u32[]{:S(2)}, u32[]{:S(2)}) collective-permute-start(bf16[108,16,128]{2,1,0:T(8,128)(2,1)S(1)} %get-tuple-element.12), channel_id=1, source_target_pairs={{0,96},{16,112},{32,0},{48,16},{64,32},{80,48},{96,64},{112,80},{1... | collective-permute-start | bytes 1327112 | tf_op jit(solution)/shard_map/ppermute | solution.py:34
  49.9 17.9 %collective-permute-start.8 = (bf16[216,16,128]{2,1,0:T(8,128)(2,1)}, bf16[216,16,128]{2,1,0:T(8,128)(2,1)S(1)}, u32[]{:S(2)}, u32[]{:S(2)}) collective-permute-start(bf16[216,16,128]{2,1,0:T(8,128)(2,1)} %pad_maximum_fusion), channel_id=1, source_target_pairs={{0,1},{1,0},{2,3},{3,2},{4,5},{5,4},{6,7},{7,6},{8,9},{9,8},{10,11... | collective-permute-start | bytes 2654216 | tf_op jit(solution)/shard_map/ppermute | solution.py:44
  49.9 13.8 %collective-permute-start.15 = (bf16[108,16,128]{2,1,0:T(8,128)(2,1)S(1)}, bf16[108,16,128]{2,1,0:T(8,128)(2,1)S(1)}, u32[]{:S(2)}, u32[]{:S(2)}) collective-permute-start(bf16[108,16,128]{2,1,0:T(8,128)(2,1)S(1)} %get-tuple-element.13), channel_id=1, source_target_pairs={{0,32},{16,48},{32,64},{48,80},{64,96},{80,112},{96,0},{112,16},{1... | collective-permute-start | bytes 1327112 | tf_op jit(solution)/shard_map/ppermute | solution.py:34
  52.2 15.6 %copy-start.4 = (bf16[108,16,128]{2,1,0:T(8,128)(2,1)}, bf16[108,16,128]{2,1,0:T(8,128)(2,1)S(1)}, u32[]{:S(2)}) copy-start(bf16[108,16,128]{2,1,0:T(8,128)(2,1)S(1)} %collective-permute-done.4.refs_5_.refs_13_.refs_15_) | copy-start | bytes 1327108
  52.3 6.4 %collective-permute-start.6 = (bf16[36,16,128]{2,1,0:T(8,128)(2,1)S(1)}, bf16[36,16,128]{2,1,0:T(8,128)(2,1)S(1)}, u32[]{:S(2)}, u32[]{:S(2)}) collective-permute-start(bf16[36,16,128]{2,1,0:T(8,128)(2,1)S(1)} %slice.51), channel_id=1, source_target_pairs={{0,12},{1,13},{2,14},{3,15},{4,0},{5,1},{6,2},{7,3},{8,4},{9,5},{1... | collective-permute-start | bytes 442376 | tf_op jit(solution)/shard_map/ppermute | solution.py:44
  56.0 11.8 %copy-start.5 = (bf16[108,16,128]{2,1,0:T(8,128)(2,1)}, bf16[108,16,128]{2,1,0:T(8,128)(2,1)S(1)}, u32[]{:S(2)}) copy-start(bf16[108,16,128]{2,1,0:T(8,128)(2,1)S(1)} %collective-permute-done.3.refs_4_.refs_12_.refs_14_) | copy-start | bytes 1327108
  56.0 6.4 %collective-permute-start.5 = (bf16[36,16,128]{2,1,0:T(8,128)(2,1)S(1)}, bf16[36,16,128]{2,1,0:T(8,128)(2,1)S(1)}, u32[]{:S(2)}, u32[]{:S(2)}) collective-permute-start(bf16[36,16,128]{2,1,0:T(8,128)(2,1)S(1)} %slice.50), channel_id=1, source_target_pairs={{0,4},{1,5},{2,6},{3,7},{4,8},{5,9},{6,10},{7,11},{8,12},{9,13},{1... | collective-permute-start | bytes 442376 | tf_op jit(solution)/shard_map/ppermute | solution.py:44
  57.1 9.1 %copy-start.23 = (bf16[108,16,128]{2,1,0:T(8,128)(2,1)}, bf16[108,16,128]{2,1,0:T(8,128)(2,1)S(1)}, u32[]{:S(2)}) copy-start(bf16[108,16,128]{2,1,0:T(8,128)(2,1)S(1)} %collective-permute-done.16.refs_5_) | copy-start | bytes 1327108
  57.1 9.1 %collective-permute-start.10 = (bf16[108,16,128]{2,1,0:T(8,128)(2,1)S(1)}, bf16[108,16,128]{2,1,0:T(8,128)(2,1)S(1)}, u32[]{:S(2)}, u32[]{:S(2)}) collective-permute-start(bf16[108,16,128]{2,1,0:T(8,128)(2,1)S(1)} %collective-permute-done.4.refs_5_.refs_13_.refs_15_), channel_id=1, source_target_pairs={{0,1},{1,0},{2,3},{3,2},{4,5},{5,4},{6,7},{7,6},{8,9},{9,8},{10,11... | collective-permute-start | bytes 1327112 | tf_op jit(solution)/shard_map/ppermute | solution.py:44
  58.7 9.2 %copy-start.15 = (bf16[36,16,128]{2,1,0:T(8,128)(2,1)}, bf16[36,16,128]{2,1,0:T(8,128)(2,1)S(1)}, u32[]{:S(2)}) copy-start(bf16[36,16,128]{2,1,0:T(8,128)(2,1)S(1)} %collective-permute-done.6.refs_7_.refs_15_.refs_17_) | copy-start | bytes 442372
  58.7 9.1 %collective-permute-start.9 = (bf16[108,16,128]{2,1,0:T(8,128)(2,1)S(1)}, bf16[108,16,128]{2,1,0:T(8,128)(2,1)S(1)}, u32[]{:S(2)}, u32[]{:S(2)}) collective-permute-start(bf16[108,16,128]{2,1,0:T(8,128)(2,1)S(1)} %collective-permute-done.3.refs_4_.refs_12_.refs_14_), channel_id=1, source_target_pairs={{0,1},{1,0},{2,3},{3,2},{4,5},{5,4},{6,7},{7,6},{8,9},{9,8},{10,11... | collective-permute-start | bytes 1327112 | tf_op jit(solution)/shard_map/ppermute | solution.py:44
  62.5 5.4 %copy-start.16 = (bf16[36,16,128]{2,1,0:T(8,128)(2,1)}, bf16[36,16,128]{2,1,0:T(8,128)(2,1)S(1)}, u32[]{:S(2)}) copy-start(bf16[36,16,128]{2,1,0:T(8,128)(2,1)S(1)} %collective-permute-done.5.refs_6_.refs_14_.refs_16_) | copy-start | bytes 442372
  62.5 2.7 %collective-permute-start.7 = (bf16[72,16,128]{2,1,0:T(8,128)(2,1)S(1)}, bf16[72,16,128]{2,1,0:T(8,128)(2,1)S(1)}, u32[]{:S(2)}, u32[]{:S(2)}) collective-permute-start(bf16[72,16,128]{2,1,0:T(8,128)(2,1)S(1)} %copy-done.6), channel_id=1, source_target_pairs={{0,1},{1,0},{2,3},{3,2},{4,5},{5,4},{6,7},{7,6},{8,9},{9,8},{10,11... | collective-permute-start | bytes 884744 | tf_op jit(solution)/shard_map/ppermute | solution.py:44
  63.7 3.5 %copy-start.24 = (bf16[108,16,128]{2,1,0:T(8,128)(2,1)}, bf16[108,16,128]{2,1,0:T(8,128)(2,1)S(1)}, u32[]{:S(2)}) copy-start(bf16[108,16,128]{2,1,0:T(8,128)(2,1)S(1)} %collective-permute-done.15.refs_4_) | copy-start | bytes 1327108
  63.7 4.0 %collective-permute-start.11 = (bf16[72,16,128]{2,1,0:T(8,128)(2,1)}, bf16[72,16,128]{2,1,0:T(8,128)(2,1)S(1)}, u32[]{:S(2)}, u32[]{:S(2)}) collective-permute-start(bf16[72,16,128]{2,1,0:T(8,128)(2,1)} %pad_maximum_fusion.5), channel_id=1, source_target_pairs={{0,1},{1,0},{2,3},{3,2},{4,5},{5,4},{6,7},{7,6},{8,9},{9,8},{10,11... | collective-permute-start | bytes 884744 | tf_op jit(solution)/shard_map/ppermute | solution.py:44
  65.1 2.7 %copy-start.9 = (bf16[72,16,128]{2,1,0:T(8,128)(2,1)}, bf16[72,16,128]{2,1,0:T(8,128)(2,1)S(1)}, u32[]{:S(2)}) copy-start(bf16[72,16,128]{2,1,0:T(8,128)(2,1)S(1)} %collective-permute-done.7.refs_8_.refs_16_.refs_18_) | copy-start | bytes 884740
  65.1 6.7 %collective-permute-start.18 = (bf16[36,16,128]{2,1,0:T(8,128)(2,1)}, bf16[36,16,128]{2,1,0:T(8,128)(2,1)}, u32[]{:S(2)}, u32[]{:S(2)}) collective-permute-start(bf16[36,16,128]{2,1,0:T(8,128)(2,1)} %slice.55), channel_id=1, source_target_pairs={{0,96},{16,112},{32,0},{48,16},{64,32},{80,48},{96,64},{112,80},{1... | collective-permute-start | bytes 442376 | tf_op jit(solution)/shard_map/ppermute | solution.py:34
  66.1 1.8 %copy-start.7 = (bf16[108,16,128]{2,1,0:T(8,128)(2,1)}, bf16[108,16,128]{2,1,0:T(8,128)(2,1)S(1)}, u32[]{:S(2)}) copy-start(bf16[108,16,128]{2,1,0:T(8,128)(2,1)S(1)} %collective-permute-done.10.refs_11_.refs_19_.refs_21_) | copy-start | bytes 1327108
  66.1 7.2 %collective-permute-start.17 = (bf16[36,16,128]{2,1,0:T(8,128)(2,1)}, bf16[36,16,128]{2,1,0:T(8,128)(2,1)}, u32[]{:S(2)}, u32[]{:S(2)}) collective-permute-start(bf16[36,16,128]{2,1,0:T(8,128)(2,1)} %slice.54), channel_id=1, source_target_pairs={{0,32},{16,48},{32,64},{48,80},{64,96},{80,112},{96,0},{112,16},{1... | collective-permute-start | bytes 442376 | tf_op jit(solution)/shard_map/ppermute | solution.py:34
  67.8 0.7 copy-start.10
  67.8 0.9 copy-start.8
  67.8 1.1 copy-start
  81.7 10.6 %collective-permute-start.19 = (bf16[100,16,128]{2,1,0:T(8,128)(2,1)}, bf16[100,16,128]{2,1,0:T(8,128)(2,1)S(1)}, u32[]{:S(2)}, u32[]{:S(2)}) collective-permute-start(bf16[100,16,128]{2,1,0:T(8,128)(2,1)} %shard_map.62.refs_0_), channel_id=1, source_target_pairs={{0,16},{16,0},{32,48},{48,32},{64,80},{80,64},{96,112},{112,96},{1... | collective-permute-start | bytes 1228808 | tf_op jit(solution)/shard_map/ppermute | solution.py:34
  83.2 11.1 %collective-permute-start.21 = (bf16[100,16,128]{2,1,0:T(8,128)(2,1)}, bf16[100,16,128]{2,1,0:T(8,128)(2,1)S(1)}, u32[]{:S(2)}, u32[]{:S(2)}) collective-permute-start(bf16[100,16,128]{2,1,0:T(8,128)(2,1)} %shard_map.62.refs_0_), channel_id=1, source_target_pairs={{0,96},{16,112},{32,0},{48,16},{64,32},{80,48},{96,64},{112,80},{1... | collective-permute-start | bytes 1228808 | tf_op jit(solution)/shard_map/ppermute | solution.py:34
  84.0 13.0 %collective-permute-start.20 = (bf16[100,16,128]{2,1,0:T(8,128)(2,1)}, bf16[100,16,128]{2,1,0:T(8,128)(2,1)S(1)}, u32[]{:S(2)}, u32[]{:S(2)}) collective-permute-start(bf16[100,16,128]{2,1,0:T(8,128)(2,1)} %shard_map.62.refs_0_), channel_id=1, source_target_pairs={{0,32},{16,48},{32,64},{48,80},{64,96},{80,112},{96,0},{112,16},{1... | collective-permute-start | bytes 1228808 | tf_op jit(solution)/shard_map/ppermute | solution.py:34
  92.3 22.3 %copy-start.17 = (bf16[100,16,128]{2,1,0:T(8,128)(2,1)}, bf16[100,16,128]{2,1,0:T(8,128)(2,1)S(1)}, u32[]{:S(2)}) copy-start(bf16[100,16,128]{2,1,0:T(8,128)(2,1)S(1)} %collective-permute-done.19.refs_1_) | copy-start | bytes 1228804
  92.3 12.4 %collective-permute-start.23 = (bf16[100,16,128]{2,1,0:T(8,128)(2,1)S(1)}, bf16[100,16,128]{2,1,0:T(8,128)(2,1)S(1)}, u32[]{:S(2)}, u32[]{:S(2)}) collective-permute-start(bf16[100,16,128]{2,1,0:T(8,128)(2,1)S(1)} %collective-permute-done.19.refs_1_), channel_id=1, source_target_pairs={{0,96},{16,112},{32,0},{48,16},{64,32},{80,48},{96,64},{112,80},{1... | collective-permute-start | bytes 1228808 | tf_op jit(solution)/shard_map/ppermute | solution.py:34
  93.7 13.9 %collective-permute-start.22 = (bf16[100,16,128]{2,1,0:T(8,128)(2,1)S(1)}, bf16[100,16,128]{2,1,0:T(8,128)(2,1)S(1)}, u32[]{:S(2)}, u32[]{:S(2)}) collective-permute-start(bf16[100,16,128]{2,1,0:T(8,128)(2,1)S(1)} %collective-permute-done.19.refs_1_), channel_id=1, source_target_pairs={{0,32},{16,48},{32,64},{48,80},{64,96},{80,112},{96,0},{112,16},{1... | collective-permute-start | bytes 1228808 | tf_op jit(solution)/shard_map/ppermute | solution.py:34
  94.3 20.3 %copy-start.11 = (bf16[100,16,128]{2,1,0:T(8,128)(2,1)}, bf16[100,16,128]{2,1,0:T(8,128)(2,1)S(1)}, u32[]{:S(2)}) copy-start(bf16[100,16,128]{2,1,0:T(8,128)(2,1)S(1)} %collective-permute-done.21.refs_3_) | copy-start | bytes 1228804
  94.4 14.5 %collective-permute-start.25 = (bf16[50,16,128]{2,1,0:T(8,128)(2,1)S(1)}, bf16[50,16,128]{2,1,0:T(8,128)(2,1)S(1)}, u32[]{:S(2)}, u32[]{:S(2)}) collective-permute-start(bf16[50,16,128]{2,1,0:T(8,128)(2,1)S(1)} %slice.57), channel_id=1, source_target_pairs={{0,96},{16,112},{32,0},{48,16},{64,32},{80,48},{96,64},{112,80},{1... | collective-permute-start | bytes 614408 | tf_op jit(solution)/shard_map/ppermute | solution.py:34
  97.0 17.6 %copy-start.12 = (bf16[100,16,128]{2,1,0:T(8,128)(2,1)}, bf16[100,16,128]{2,1,0:T(8,128)(2,1)S(1)}, u32[]{:S(2)}) copy-start(bf16[100,16,128]{2,1,0:T(8,128)(2,1)S(1)} %collective-permute-done.20.refs_2_) | copy-start | bytes 1228804
  97.0 14.2 %collective-permute-start.24 = (bf16[50,16,128]{2,1,0:T(8,128)(2,1)S(1)}, bf16[50,16,128]{2,1,0:T(8,128)(2,1)S(1)}, u32[]{:S(2)}, u32[]{:S(2)}) collective-permute-start(bf16[50,16,128]{2,1,0:T(8,128)(2,1)S(1)} %slice.56), channel_id=1, source_target_pairs={{0,32},{16,48},{32,64},{48,80},{64,96},{80,112},{96,0},{112,16},{1... | collective-permute-start | bytes 614408 | tf_op jit(solution)/shard_map/ppermute | solution.py:34
  104.7 9.9 %copy-start.13 = (bf16[100,16,128]{2,1,0:T(8,128)(2,1)}, bf16[100,16,128]{2,1,0:T(8,128)(2,1)S(1)}, u32[]{:S(2)}) copy-start(bf16[100,16,128]{2,1,0:T(8,128)(2,1)S(1)} %collective-permute-done.23.refs_5_) | copy-start | bytes 1228804
  104.7 6.5 %collective-permute-start.27 = (bf16[50,16,128]{2,1,0:T(8,128)(2,1)S(1)}, bf16[50,16,128]{2,1,0:T(8,128)(2,1)S(1)}, u32[]{:S(2)}, u32[]{:S(2)}) collective-permute-start(bf16[50,16,128]{2,1,0:T(8,128)(2,1)S(1)} %slice.59), channel_id=1, source_target_pairs={{0,96},{16,112},{32,0},{48,16},{64,32},{80,48},{96,64},{112,80},{1... | collective-permute-start | bytes 614408 | tf_op jit(solution)/shard_map/ppermute | solution.py:34
  107.6 7.1 %copy-start.14 = (bf16[100,16,128]{2,1,0:T(8,128)(2,1)}, bf16[100,16,128]{2,1,0:T(8,128)(2,1)S(1)}, u32[]{:S(2)}) copy-start(bf16[100,16,128]{2,1,0:T(8,128)(2,1)S(1)} %collective-permute-done.22.refs_4_) | copy-start | bytes 1228804
  107.6 7.0 %collective-permute-start.26 = (bf16[50,16,128]{2,1,0:T(8,128)(2,1)S(1)}, bf16[50,16,128]{2,1,0:T(8,128)(2,1)S(1)}, u32[]{:S(2)}, u32[]{:S(2)}) collective-permute-start(bf16[50,16,128]{2,1,0:T(8,128)(2,1)S(1)} %slice.58), channel_id=1, source_target_pairs={{0,32},{16,48},{32,64},{48,80},{64,96},{80,112},{96,0},{112,16},{1... | collective-permute-start | bytes 614408 | tf_op jit(solution)/shard_map/ppermute | solution.py:34
  108.8 5.8 %copy-start.19 = (bf16[50,16,128]{2,1,0:T(8,128)(2,1)}, bf16[50,16,128]{2,1,0:T(8,128)(2,1)S(1)}, u32[]{:S(2)}) copy-start(bf16[50,16,128]{2,1,0:T(8,128)(2,1)S(1)} %collective-permute-done.25.refs_7_) | copy-start | bytes 614404
  111.2 3.5 %copy-start.20 = (bf16[50,16,128]{2,1,0:T(8,128)(2,1)}, bf16[50,16,128]{2,1,0:T(8,128)(2,1)S(1)}, u32[]{:S(2)}) copy-start(bf16[50,16,128]{2,1,0:T(8,128)(2,1)S(1)} %collective-permute-done.24.refs_6_) | copy-start | bytes 614404
  111.2 3.5 %copy-start.21 = (bf16[50,16,128]{2,1,0:T(8,128)(2,1)}, bf16[50,16,128]{2,1,0:T(8,128)(2,1)S(1)}, u32[]{:S(2)}) copy-start(bf16[50,16,128]{2,1,0:T(8,128)(2,1)S(1)} %collective-permute-done.27.refs_9_) | copy-start | bytes 614404
  114.6 0.7 copy-start.22
  125.9 15.9 %all-to-all-start.1 = ((bf16[64,16,512]{2,1,0:T(8,128)(2,1)}), bf16[64,16,512]{2,1,0:T(8,128)(2,1)S(1)}, u32[]{:S(2)}, u32[]{:S(2)}) async-start(bf16[64,16,512]{2,1,0:T(8,128)(2,1)} %shard_map.64), calls=%async_computation.1 | async-start | bytes 2097152 | tf_op jit(solution)/shard_map/all_to_all | solution.py:463

commit v5 on v4

--- a/solution.py
+++ b/solution.py
@@ -224,7 +224,8 @@
         square[pl.ds(j * KS, KS)] = result.astype(BF).reshape(KS, SL, BLOCK)
         return carry
 
-    lax.fori_loop(0, 4, column, 0)
+    for j in range(4):
+        column(j, 0)
 
 
 def step_kernel(place, all_lists, step_slots, *refs):
@@ -240,21 +241,18 @@
     ]
     for copy in tables + from_cols + sum(from_rows, []):
         copy.start()
-    for copy in tables + from_cols:
+    for n in range(4):
+        results[n] = jnp.zeros_like(results[n])
+    for copy in tables + from_cols + sum(from_rows, []):
         copy.wait()
     out = []
     for j in range(4):
-        for copy in from_rows[j]:
-            copy.wait()
 
         def right(t, n):
             return rows[j * KS + t : j * KS + t + n].reshape(n * BLOCK, BLOCK)
 
         second = product(lambda t, s: slots[j * 32 + t, j * 32 + s], KT, KS, cols, right)
-        if j >= 2:
-            out[j - 2].wait()
-        result = results.at[j % 2]
-        result[...] = jnp.zeros_like(result)
+        result = results.at[j]
         for s in range(KT):
             own = cols[slots[j * 32 + 31, j * 32 + s]].astype(jnp.float32)
             result[lists[32 * j + s, NB]] = (1.5 * own - 0.5 * second[s * SL : (s + 1) * SL]).astype(BF)
@@ -264,8 +262,8 @@
             )
         )
         out[j].start()
-    out[2].wait()
-    out[3].wait()
+    for copy in out:
+        copy.wait()
 
 
 def square_rows_kernel(place, lists, *refs):
@@ -320,6 +318,14 @@
     return layout + [[(0, 2, line, at, half)] for line in range(2) for at in (0, half)]
 
 
+def crossed(slots):
+    half = slots // 2
+    layout = [[(0, back, line, 0, slots)] for back, line in [(0, 0), (0, 1), (1, 0), (3, 0)]]
+    layout += [[(0, 1, 1, 0, half)], [(0, 2, 0, 0, half)], [(0, 3, 1, half, half)], [(0, 2, 0, half, half)]]
+    layout += [[(0, 3, 1, 0, half), (half, 1, 1, half, half)]]
+    return layout + [[(0, 2, 1, 0, half)], [(0, 2, 1, half, half)]]
+
+
 def merged(slots):
     half = slots // 2
     layout = [[(0, back, line, 0, slots)] for back, line in [(0, 0), (0, 1), (1, 0), (3, 0)]]
@@ -363,7 +369,14 @@
 
 
 def gather_rows(packed):
-    return ring_apart(packed, row_shift)
+    half = packed.shape[0] // 2
+    other = row_shift(packed, 0, 1)
+    left, right = row_shift(packed, 1, 0), row_shift(packed, -1, 0)
+    other_left, other_right = row_shift(other[:half], 1, 0), row_shift(other[half:], -1, 0)
+    near = [other_left, row_shift(left[:half], 1, 0), other_right, row_shift(right[half:], -1, 0)]
+    far = [row_shift(other_left, 1, 0), row_shift(other_right, -1, 0)]
+    cross = row_shift(jnp.concatenate([right[:half], left[half:]]), 0, 1)
+    return [packed, other, left, right, *near, cross, *far]
 
 
 def gather_cols(packed):
@@ -374,7 +387,7 @@
 
 ROWS = merged(PACK)
 COLS = merged_cores(PACK)
-SQUARES = apart(4 * KS)
+SQUARES = crossed(4 * KS)
 NR, NC, NS = len(ROWS), len(COLS), len(SQUARES)
 
 
@@ -449,11 +462,11 @@
         [
             pltpu.VMEM((4 * KS, TR, SL, BLOCK), BF),
             pltpu.VMEM((TC * PACK, SL, BLOCK), BF),
-            pltpu.VMEM((2, NB + 8, SL, BLOCK), BF),
+            pltpu.VMEM((4, NB + 8, SL, BLOCK), BF),
             pltpu.SMEM((BLOCK, BLOCK), jnp.int32),
             pltpu.SMEM((BLOCK, BLOCK), jnp.int32),
             pltpu.SemaphoreType.DMA((pieces(COLS),)),
-            pltpu.SemaphoreType.DMA((4, TR)),
+            pltpu.SemaphoreType.DMA((4, 16)),
             pltpu.SemaphoreType.DMA((4,)),
             pltpu.SemaphoreType.DMA((2,)),
         ],

time: 145 us -> 139 us (0.959); the launches traced: 143 us -> 138 us
  Pallas kernels: 34.6 us -> 30.6 us
    pallas_call x1, Pallas kernels: 10.6 us -> 8.2 us  [on_device(): call(step_kernel, jax.ShapeDtypeStruct((NB, SL, 4 * BLOCK), BF), [SMEM] +...]
    pallas_call x1, Pallas kernels: 8.4 us -> 6.79 us  [on_device(): call(square_kernel, jax.ShapeDtypeStruct((4 * KS, SL, BLOCK), BF), [SMEM]...]
    ppermute x16 -> x17, waiting for transfers between devices: 25.1 us -> 23.6 us  [row_shift(): return lax.ppermute(value, 'row', pairs)]
    ppermute x16 -> x17, starting transfers between devices: 18.2 us -> 18.4 us  [row_shift(): return lax.ppermute(value, 'row', pairs)]
  transfers between devices with their start and end apart: 29 -> 30, of which waited for: 16 -> 17; matrix products, arithmetic and copies ran while one was open for 3% -> 3% of each run, Pallas kernels for 7% -> 7%
where the time goes in v5:
time: 139 us; the launch traced here: 138 us
  waiting for transfers between devices  41.6 us (30%)
  starting transfers between devices  36 us (26%)
  Pallas kernels  30.6 us (22%)
  blocking collectives  21.8 us (16%)
  local copies, waits for them, and re-layouts  5.05 us (4%)
  other arithmetic  2.51 us (2%)
    ppermute x17, waiting for transfers between devices, row_shift(): return lax.ppermute(value, 'row', pairs)  23.6 us
    all_to_all x1, blocking collectives, on_device(): sliced = lax.all_to_all(sent, 'row', 0, 0, tiled=True)  21.8 us
    ppermute x17, starting transfers between devices, row_shift(): return lax.ppermute(value, 'row', pairs)  18.4 us
    ppermute x12, starting transfers between devices, col_shift(): return lax.ppermute(value, 'col', pairs)  14 us
    ppermute x12, waiting for transfers between devices, col_shift(): return lax.ppermute(value, 'col', pairs)  11.7 us
    pallas_call x1, Pallas kernels, on_device(): call(step_kernel, jax.ShapeDtypeStruct((NB, SL, 4 * BLOCK), BF), [SMEM] +...  8.2 us
    pallas_call x1, Pallas kernels, on_device(): call(square_rows_kernel, jax.ShapeDtypeStruct((8, TR, SL, 4 * BLOCK), BF)...  6.82 us
    pallas_call x1, Pallas kernels, on_device(): call(square_kernel, jax.ShapeDtypeStruct((4 * KS, SL, BLOCK), BF), [SMEM]...  6.79 us
  transfers between devices with their start and end apart: 30, of which 17 were waited for; matrix products, arithmetic and copies ran while one was open for 3% of the time, Pallas kernels for 7%

profile of v5, /device:TPU:0, one launch (start us, length us, event | category | flops | bytes accessed | tf_op | source)
XLA Modules:
  0.0 138.5 jit_solution(4224651666553282239)
XLA Ops:
  0.6 2.5 %shard_map.59 = bf16[8,33,16,128]{3,2,1,0:T(8,128)(2,1)} custom-call(bf16[8,8,16,512]{3,2,1,0:T(8,128)(2,1)} %bitcast.13, s32[4,8]{1,0:T(4,128)} %bitcast.15, s32[4,8]{1,0:T(4,128)} %bitcast.16, s32[4,8]{1,0:T(4,128)} %bitcast.17), custom_call_target="tpu_custom_call" | custom-call | bytes 2097152 | tf_op jit(solution)/shard_map/pallas_call | solution.py:400
  3.2 21.8 %all_to_all.10.sliced = bf16[8,33,16,128]{3,2,1,0:T(8,128)(2,1)} all-to-all(bf16[8,33,16,128]{3,2,1,0:T(8,128)(2,1)} %shard_map.59), channel_id=1, replica_groups=mesh['row'=8,'col'=16] {'row'}, dimensions={0} | all-to-all | bytes 2162688 | tf_op jit(solution)/shard_map/all_to_all | solution.py:409
  25.0 3.3 %shard_map.60 = (bf16[72,16,128]{2,1,0:T(8,128)(2,1)}, s32[16,128]{1,0:T(8,128)}) custom-call(bf16[8,33,16,128]{3,2,1,0:T(8,128)(2,1)} %all_to_all.10.sliced), custom_call_target="tpu_custom_call" | custom-call | bytes 2097152 | tf_op jit(solution)/shard_map/pallas_call | solution.py:411
  28.3 4.1 %collective-permute-start.2 = (bf16[72,16,128]{2,1,0:T(8,128)(2,1)}, bf16[72,16,128]{2,1,0:T(8,128)(2,1)S(1)}, u32[]{:S(2)}, u32[]{:S(2)}) collective-permute-start(bf16[72,16,128]{2,1,0:T(8,128)(2,1)} %get-tuple-element.8.refs_0_.refs_8_.refs_11_), channel_id=1, source_target_pairs={{0,12},{1,13},{2,14},{3,15},{4,0},{5,1},{6,2},{7,3},{8,4},{9,5},{1... | collective-permute-start | bytes 884744 | tf_op jit(solution)/shard_map/ppermute | solution.py:44
  32.5 0.0 collective-permute-start.1
  32.5 2.9 %collective-permute-start = (bf16[72,16,128]{2,1,0:T(8,128)(2,1)}, bf16[72,16,128]{2,1,0:T(8,128)(2,1)S(1)}, u32[]{:S(2)}, u32[]{:S(2)}) collective-permute-start(bf16[72,16,128]{2,1,0:T(8,128)(2,1)} %get-tuple-element.8.refs_0_.refs_8_.refs_11_), channel_id=1, source_target_pairs={{0,2},{1,3},{2,0},{3,1},{4,6},{5,7},{6,4},{7,5},{8,10},{9,11},{10,... | collective-permute-start | bytes 884744 | tf_op jit(solution)/shard_map/ppermute | solution.py:44
  35.4 1.2 collective-permute-start.14
  36.5 0.9 collective-permute-start.13
  37.4 0.1 collective-permute-done.2.refs_3_.refs_11_.refs_14_
  37.5 0.8 collective-permute-start.12
  38.3 2.5 %collective-permute-done.1.refs_2_.refs_10_.refs_13_ = bf16[72,16,128]{2,1,0:T(8,128)(2,1)S(1)} collective-permute-done((bf16[72,16,128]{2,1,0:T(8,128)(2,1)}, bf16[72,16,128]{2,1,0:T(8,128)(2,1)S(1)}, u32[]{:S(2)}, u32[]{:S(2)}) %collective-permute-start.1) | collective-permute-done | bytes 294944 | tf_op jit(solution)/shard_map/ppermute | solution.py:44
  40.8 2.3 %collective-permute-done.refs_1_.refs_9_.refs_12_ = bf16[72,16,128]{2,1,0:T(8,128)(2,1)S(1)} collective-permute-done((bf16[72,16,128]{2,1,0:T(8,128)(2,1)}, bf16[72,16,128]{2,1,0:T(8,128)(2,1)S(1)}, u32[]{:S(2)}, u32[]{:S(2)}) %collective-permute-start) | collective-permute-done | bytes 294944 | tf_op jit(solution)/shard_map/ppermute | solution.py:44
  43.1 0.1 pad_maximum_fusion.1
  43.2 3.2 %collective-permute-start.4 = (bf16[108,16,128]{2,1,0:T(8,128)(2,1)S(1)}, bf16[108,16,128]{2,1,0:T(8,128)(2,1)S(1)}, u32[]{:S(2)}, u32[]{:S(2)}) collective-permute-start(bf16[108,16,128]{2,1,0:T(8,128)(2,1)S(1)} %get-tuple-element.20), channel_id=1, source_target_pairs={{0,12},{1,13},{2,14},{3,15},{4,0},{5,1},{6,2},{7,3},{8,4},{9,5},{1... | collective-permute-start | bytes 1327112 | tf_op jit(solution)/shard_map/ppermute | solution.py:44
  46.4 0.0 collective-permute-start.3
  46.4 0.0 collective-permute-done.14.refs_3_
  46.5 0.5 collective-permute-done.12.refs_1_
  47.0 0.1 pad_maximum_fusion.3
  47.1 0.7 copy-done.17
  47.7 1.2 collective-permute-start.16
  48.9 1.0 pad_maximum_fusion
  49.9 0.9 collective-permute-start.15
  50.8 1.4 %collective-permute-done.4.refs_5_.refs_13_.refs_16_ = bf16[108,16,128]{2,1,0:T(8,128)(2,1)S(1)} collective-permute-done((bf16[108,16,128]{2,1,0:T(8,128)(2,1)S(1)}, bf16[108,16,128]{2,1,0:T(8,128)(2,1)S(1)}, u32[]{:S(2)}, u32[]{:S(2)}) %collective-permute-start.4) | collective-permute-done | bytes 442400 | tf_op jit(solution)/shard_map/ppermute | solution.py:44
  52.2 3.8 %collective-permute-start.6 = (bf16[36,16,128]{2,1,0:T(8,128)(2,1)S(1)}, bf16[36,16,128]{2,1,0:T(8,128)(2,1)S(1)}, u32[]{:S(2)}, u32[]{:S(2)}) collective-permute-start(bf16[36,16,128]{2,1,0:T(8,128)(2,1)S(1)} %slice.59), channel_id=1, source_target_pairs={{0,12},{1,13},{2,14},{3,15},{4,0},{5,1},{6,2},{7,3},{8,4},{9,5},{1... | collective-permute-start | bytes 442376 | tf_op jit(solution)/shard_map/ppermute | solution.py:44
  56.0 0.1 collective-permute-start.5
  56.1 0.9 collective-permute-done.16.refs_5_
  57.0 1.6 %collective-permute-done.6.refs_7_.refs_15_.refs_18_ = bf16[36,16,128]{2,1,0:T(8,128)(2,1)S(1)} collective-permute-done((bf16[36,16,128]{2,1,0:T(8,128)(2,1)S(1)}, bf16[36,16,128]{2,1,0:T(8,128)(2,1)S(1)}, u32[]{:S(2)}, u32[]{:S(2)}) %collective-permute-start.6) | collective-permute-done | bytes 147488 | tf_op jit(solution)/shard_map/ppermute | solution.py:44
  58.7 3.8 %collective-permute-done.5.refs_6_.refs_14_.refs_17_ = bf16[36,16,128]{2,1,0:T(8,128)(2,1)S(1)} collective-permute-done((bf16[36,16,128]{2,1,0:T(8,128)(2,1)S(1)}, bf16[36,16,128]{2,1,0:T(8,128)(2,1)S(1)}, u32[]{:S(2)}, u32[]{:S(2)}) %collective-permute-start.5) | collective-permute-done | bytes 147488 | tf_op jit(solution)/shard_map/ppermute | solution.py:44
  62.4 0.8 pad_maximum_fusion.6
  63.2 0.5 collective-permute-done.15.refs_4_
  63.7 0.7 slice.63
  64.4 0.7 slice.62
  65.1 1.0 collective-permute-start.18
  66.1 1.1 collective-permute-start.17
  67.2 0.6 pad_add_fusion.place
  67.8 0.0 copy-start
  67.9 0.6 copy-done.13
  68.5 0.2 copy-done.8
  68.7 0.3 copy-done
  69.0 2.9 %shard_map.61 = (s32[128,128]{1,0:T(8,128)}, s32[128,128]{1,0:T(8,128)}, s32[128,128]{1,0:T(8,128)}) custom-call(s32[2]{0:T(128)} %pad_add_fusion.place, s32[16,128]{1,0:T(8,128)} %get-tuple-element.7.flags, bf16[72,16,128]{2,1,0:T(8,128)(2,1)} %get-tuple-element.8.refs_0_.refs_8_.refs_11_, bf16[72,16,128]{2,1,0:T(8,128)(2,1)} %copy-done.1, ...), custom_call_target="tpu_custom_call" | custom-call | flops 1048576 | bytes 12582912 | tf_op jit(solution)/shard_map/pallas_call | solution.py:426
  71.9 1.4 %collective-permute-done.17.refs_6_ = bf16[36,16,128]{2,1,0:T(8,128)(2,1)} collective-permute-done((bf16[36,16,128]{2,1,0:T(8,128)(2,1)}, bf16[36,16,128]{2,1,0:T(8,128)(2,1)}, u32[]{:S(2)}, u32[]{:S(2)}) %collective-permute-start.17) | collective-permute-done | bytes 147488 | tf_op jit(solution)/shard_map/ppermute | solution.py:34
  73.3 6.8 %shard_map.62.refs_0_ = bf16[100,16,128]{2,1,0:T(8,128)(2,1)} custom-call(s32[2]{0:T(128)} %pad_add_fusion.place, s32[128,128]{1,0:T(8,128)} %get-tuple-element.10.square_slots, bf16[72,16,128]{2,1,0:T(8,128)(2,1)} %get-tuple-element.8.refs_0_.refs_8_.refs_11_, bf16[72,16,128]{2,1,0:T(8,128)(2,1)} %copy-done.17, bf16[72,16,128]{2,1,0:T(8,128)(2,1)} %copy-done.27, ...), custom_call_target="tpu_custom_call" | custom-call | flops 891289600 | bytes 9437184 | tf_op jit(solution)/shard_map/pallas_call | solution.py:439
  80.1 0.9 collective-permute-start.21
  81.0 1.2 collective-permute-start.20
  82.2 1.4 %collective-permute-start.19 = (bf16[100,16,128]{2,1,0:T(8,128)(2,1)}, bf16[100,16,128]{2,1,0:T(8,128)(2,1)S(1)}, u32[]{:S(2)}, u32[]{:S(2)}) collective-permute-start(bf16[100,16,128]{2,1,0:T(8,128)(2,1)} %shard_map.62.refs_0_), channel_id=1, source_target_pairs={{0,16},{16,0},{32,48},{48,32},{64,80},{80,64},{96,112},{112,96},{1... | collective-permute-start | bytes 1228808 | tf_op jit(solution)/shard_map/ppermute | solution.py:34
  83.6 7.0 %collective-permute-done.21.refs_3_ = bf16[100,16,128]{2,1,0:T(8,128)(2,1)S(1)} collective-permute-done((bf16[100,16,128]{2,1,0:T(8,128)(2,1)}, bf16[100,16,128]{2,1,0:T(8,128)(2,1)S(1)}, u32[]{:S(2)}, u32[]{:S(2)}) %collective-permute-start.21) | collective-permute-done | bytes 409632 | tf_op jit(solution)/shard_map/ppermute | solution.py:34
  90.7 2.3 %collective-permute-done.20.refs_2_ = bf16[100,16,128]{2,1,0:T(8,128)(2,1)S(1)} collective-permute-done((bf16[100,16,128]{2,1,0:T(8,128)(2,1)}, bf16[100,16,128]{2,1,0:T(8,128)(2,1)S(1)}, u32[]{:S(2)}, u32[]{:S(2)}) %collective-permute-start.20) | collective-permute-done | bytes 409632 | tf_op jit(solution)/shard_map/ppermute | solution.py:34
  93.1 1.5 %collective-permute-start.26 = (bf16[100,16,128]{2,1,0:T(8,128)(2,1)S(1)}, bf16[100,16,128]{2,1,0:T(8,128)(2,1)S(1)}, u32[]{:S(2)}, u32[]{:S(2)}) collective-permute-start(bf16[100,16,128]{2,1,0:T(8,128)(2,1)S(1)} %pad_maximum_fusion.5), channel_id=1, source_target_pairs={{0,16},{16,0},{32,48},{48,32},{64,80},{80,64},{96,112},{112,96},{1... | collective-permute-start | bytes 1228808 | tf_op jit(solution)/shard_map/ppermute | solution.py:34
  94.7 1.1 collective-permute-start.24
  95.8 1.1 collective-permute-start.22
  96.9 2.1 %collective-permute-start.25 = (bf16[50,16,128]{2,1,0:T(8,128)(2,1)S(1)}, bf16[50,16,128]{2,1,0:T(8,128)(2,1)S(1)}, u32[]{:S(2)}, u32[]{:S(2)}) collective-permute-start(bf16[50,16,128]{2,1,0:T(8,128)(2,1)S(1)} %get-tuple-element.13), channel_id=1, source_target_pairs={{0,96},{16,112},{32,0},{48,16},{64,32},{80,48},{96,64},{112,80},{1... | collective-permute-start | bytes 614408 | tf_op jit(solution)/shard_map/ppermute | solution.py:34
  99.0 3.9 %collective-permute-done.24.refs_6_ = bf16[50,16,128]{2,1,0:T(8,128)(2,1)S(1)} collective-permute-done((bf16[50,16,128]{2,1,0:T(8,128)(2,1)S(1)}, bf16[50,16,128]{2,1,0:T(8,128)(2,1)S(1)}, u32[]{:S(2)}, u32[]{:S(2)}) %collective-permute-start.24) | collective-permute-done | bytes 204832 | tf_op jit(solution)/shard_map/ppermute | solution.py:34
  102.9 2.0 %collective-permute-start.28 = (bf16[50,16,128]{2,1,0:T(8,128)(2,1)S(1)}, bf16[50,16,128]{2,1,0:T(8,128)(2,1)S(1)}, u32[]{:S(2)}, u32[]{:S(2)}) collective-permute-start(bf16[50,16,128]{2,1,0:T(8,128)(2,1)S(1)} %collective-permute-done.24.refs_6_), channel_id=1, source_target_pairs={{0,96},{16,112},{32,0},{48,16},{64,32},{80,48},{96,64},{112,80},{1... | collective-permute-start | bytes 614408 | tf_op jit(solution)/shard_map/ppermute | solution.py:34
  104.9 0.0 collective-permute-done.22.refs_4_
  105.0 0.0 collective-permute-start.27
  105.0 1.6 %collective-permute-done.25.refs_7_ = bf16[50,16,128]{2,1,0:T(8,128)(2,1)S(1)} collective-permute-done((bf16[50,16,128]{2,1,0:T(8,128)(2,1)S(1)}, bf16[50,16,128]{2,1,0:T(8,128)(2,1)S(1)}, u32[]{:S(2)}, u32[]{:S(2)}) %collective-permute-start.25) | collective-permute-done | bytes 204832 | tf_op jit(solution)/shard_map/ppermute | solution.py:34
  106.5 2.6 %collective-permute-done.23.refs_5_ = bf16[50,16,128]{2,1,0:T(8,128)(2,1)S(1)} collective-permute-done((bf16[50,16,128]{2,1,0:T(8,128)(2,1)S(1)}, bf16[50,16,128]{2,1,0:T(8,128)(2,1)S(1)}, u32[]{:S(2)}, u32[]{:S(2)}) %collective-permute-start.23) | collective-permute-done | bytes 204832 | tf_op jit(solution)/shard_map/ppermute | solution.py:34
  109.1 2.8 %collective-permute-done.27.refs_9_ = bf16[50,16,128]{2,1,0:T(8,128)(2,1)S(1)} collective-permute-done((bf16[50,16,128]{2,1,0:T(8,128)(2,1)S(1)}, bf16[50,16,128]{2,1,0:T(8,128)(2,1)S(1)}, u32[]{:S(2)}, u32[]{:S(2)}) %collective-permute-start.27) | collective-permute-done | bytes 204832 | tf_op jit(solution)/shard_map/ppermute | solution.py:34
  112.0 0.6 copy-done.23
  112.6 8.2 %shard_map.64 = bf16[64,16,512]{2,1,0:T(8,128)(2,1)} custom-call(s32[2]{0:T(128)} %pad_add_fusion.place, s32[128,128]{1,0:T(8,128)} %get-tuple-element.9.lists.all_lists, s32[128,128]{1,0:T(8,128)} %get-tuple-element.11.step_slots, bf16[100,16,128]{2,1,0:T(8,128)(2,1)} %shard_map.62.refs_0_, bf16[100,16,128]{2,1,0:T(8,128)(2,1)} %copy-done.11, ...), custom_call_target="tpu_custom_call" | custom-call | flops 1101004800 | bytes 9437184 | tf_op jit(solution)/shard_map/pallas_call | solution.py:457
  120.8 3.6 %all-to-all-start.1 = ((bf16[64,16,512]{2,1,0:T(8,128)(2,1)}), bf16[64,16,512]{2,1,0:T(8,128)(2,1)S(1)}, u32[]{:S(2)}, u32[]{:S(2)}) async-start(bf16[64,16,512]{2,1,0:T(8,128)(2,1)} %shard_map.64), calls=%async_computation.1 | async-start | bytes 2097152 | tf_op jit(solution)/shard_map/all_to_all | solution.py:476
  124.4 6.8 %shard_map.63 = bf16[8,8,16,512]{3,2,1,0:T(8,128)(2,1)} custom-call(s32[2]{0:T(128)} %pad_add_fusion.place, s32[128,128]{1,0:T(8,128)} %get-tuple-element.9.lists.all_lists, bf16[100,16,128]{2,1,0:T(8,128)(2,1)} %shard_map.62.refs_0_, bf16[100,16,128]{2,1,0:T(8,128)(2,1)} %copy-done.11, bf16[100,16,128]{2,1,0:T(8,128)(2,1)} %copy-done.10, ...), custom_call_target="tpu_custom_call" | custom-call | bytes 4194304 | tf_op jit(solution)/shard_map/pallas_call | solution.py:477
  131.2 6.2 %all-to-all-done.1 = bf16[64,16,512]{2,1,0:T(8,128)(2,1)S(1)} async-done(((bf16[64,16,512]{2,1,0:T(8,128)(2,1)}), bf16[64,16,512]{2,1,0:T(8,128)(2,1)S(1)}, u32[]{:S(2)}, u32[]{:S(2)}) %all-to-all-start.1) | async-done | bytes 1048608 | tf_op jit(solution)/shard_map/all_to_all | solution.py:476
  137.4 1.1 copy.6
  (77 shorter events, 0.3 us)
Async XLA Ops:
  28.3 9.2 %collective-permute-start.2 = (bf16[72,16,128]{2,1,0:T(8,128)(2,1)}, bf16[72,16,128]{2,1,0:T(8,128)(2,1)S(1)}, u32[]{:S(2)}, u32[]{:S(2)}) collective-permute-start(bf16[72,16,128]{2,1,0:T(8,128)(2,1)} %get-tuple-element.8.refs_0_.refs_8_.refs_11_), channel_id=1, source_target_pairs={{0,12},{1,13},{2,14},{3,15},{4,0},{5,1},{6,2},{7,3},{8,4},{9,5},{1... | collective-permute-start | bytes 884744 | tf_op jit(solution)/shard_map/ppermute | solution.py:44
  32.5 8.4 %collective-permute-start.1 = (bf16[72,16,128]{2,1,0:T(8,128)(2,1)}, bf16[72,16,128]{2,1,0:T(8,128)(2,1)S(1)}, u32[]{:S(2)}, u32[]{:S(2)}) collective-permute-start(bf16[72,16,128]{2,1,0:T(8,128)(2,1)} %get-tuple-element.8.refs_0_.refs_8_.refs_11_), channel_id=1, source_target_pairs={{0,4},{1,5},{2,6},{3,7},{4,8},{5,9},{6,10},{7,11},{8,12},{9,13},{1... | collective-permute-start | bytes 884744 | tf_op jit(solution)/shard_map/ppermute | solution.py:44
  32.5 10.7 %collective-permute-start = (bf16[72,16,128]{2,1,0:T(8,128)(2,1)}, bf16[72,16,128]{2,1,0:T(8,128)(2,1)S(1)}, u32[]{:S(2)}, u32[]{:S(2)}) collective-permute-start(bf16[72,16,128]{2,1,0:T(8,128)(2,1)} %get-tuple-element.8.refs_0_.refs_8_.refs_11_), channel_id=1, source_target_pairs={{0,2},{1,3},{2,0},{3,1},{4,6},{5,7},{6,4},{7,5},{8,10},{9,11},{10,... | collective-permute-start | bytes 884744 | tf_op jit(solution)/shard_map/ppermute | solution.py:44
  35.4 11.0 %collective-permute-start.14 = (bf16[72,16,128]{2,1,0:T(8,128)(2,1)}, bf16[72,16,128]{2,1,0:T(8,128)(2,1)S(1)}, u32[]{:S(2)}, u32[]{:S(2)}) collective-permute-start(bf16[72,16,128]{2,1,0:T(8,128)(2,1)} %get-tuple-element.8.refs_0_.refs_8_.refs_11_), channel_id=1, source_target_pairs={{0,96},{16,112},{32,0},{48,16},{64,32},{80,48},{96,64},{112,80},{1... | collective-permute-start | bytes 884744 | tf_op jit(solution)/shard_map/ppermute | solution.py:34
  36.5 9.9 %collective-permute-start.13 = (bf16[72,16,128]{2,1,0:T(8,128)(2,1)}, bf16[72,16,128]{2,1,0:T(8,128)(2,1)S(1)}, u32[]{:S(2)}, u32[]{:S(2)}) collective-permute-start(bf16[72,16,128]{2,1,0:T(8,128)(2,1)} %get-tuple-element.8.refs_0_.refs_8_.refs_11_), channel_id=1, source_target_pairs={{0,32},{16,48},{32,64},{48,80},{64,96},{80,112},{96,0},{112,16},{1... | collective-permute-start | bytes 884744 | tf_op jit(solution)/shard_map/ppermute | solution.py:34
  37.5 11.4 %copy-start.2 = (bf16[72,16,128]{2,1,0:T(8,128)(2,1)}, bf16[72,16,128]{2,1,0:T(8,128)(2,1)S(1)}, u32[]{:S(2)}) copy-start(bf16[72,16,128]{2,1,0:T(8,128)(2,1)S(1)} %collective-permute-done.2.refs_3_.refs_11_.refs_14_) | copy-start | bytes 884740
  37.5 9.5 %collective-permute-start.12 = (bf16[72,16,128]{2,1,0:T(8,128)(2,1)}, bf16[72,16,128]{2,1,0:T(8,128)(2,1)S(1)}, u32[]{:S(2)}, u32[]{:S(2)}) collective-permute-start(bf16[72,16,128]{2,1,0:T(8,128)(2,1)} %get-tuple-element.8.refs_0_.refs_8_.refs_11_), channel_id=1, source_target_pairs={{0,16},{16,0},{32,48},{48,32},{64,80},{80,64},{96,112},{112,96},{1... | collective-permute-start | bytes 884744 | tf_op jit(solution)/shard_map/ppermute | solution.py:34
  40.8 8.1 %copy-start.3 = (bf16[72,16,128]{2,1,0:T(8,128)(2,1)}, bf16[72,16,128]{2,1,0:T(8,128)(2,1)S(1)}, u32[]{:S(2)}) copy-start(bf16[72,16,128]{2,1,0:T(8,128)(2,1)S(1)} %collective-permute-done.1.refs_2_.refs_10_.refs_13_) | copy-start | bytes 884740
  43.1 5.8 %copy-start.1 = (bf16[72,16,128]{2,1,0:T(8,128)(2,1)}, bf16[72,16,128]{2,1,0:T(8,128)(2,1)S(1)}, u32[]{:S(2)}) copy-start(bf16[72,16,128]{2,1,0:T(8,128)(2,1)S(1)} %collective-permute-done.refs_1_.refs_9_.refs_12_) | copy-start | bytes 884740
  43.2 9.0 %collective-permute-start.4 = (bf16[108,16,128]{2,1,0:T(8,128)(2,1)S(1)}, bf16[108,16,128]{2,1,0:T(8,128)(2,1)S(1)}, u32[]{:S(2)}, u32[]{:S(2)}) collective-permute-start(bf16[108,16,128]{2,1,0:T(8,128)(2,1)S(1)} %get-tuple-element.20), channel_id=1, source_target_pairs={{0,12},{1,13},{2,14},{3,15},{4,0},{5,1},{6,2},{7,3},{8,4},{9,5},{1... | collective-permute-start | bytes 1327112 | tf_op jit(solution)/shard_map/ppermute | solution.py:44
  46.4 9.6 %collective-permute-start.3 = (bf16[108,16,128]{2,1,0:T(8,128)(2,1)S(1)}, bf16[108,16,128]{2,1,0:T(8,128)(2,1)S(1)}, u32[]{:S(2)}, u32[]{:S(2)}) collective-permute-start(bf16[108,16,128]{2,1,0:T(8,128)(2,1)S(1)} %get-tuple-element.21), channel_id=1, source_target_pairs={{0,4},{1,5},{2,6},{3,7},{4,8},{5,9},{6,10},{7,11},{8,12},{9,13},{1... | collective-permute-start | bytes 1327112 | tf_op jit(solution)/shard_map/ppermute | solution.py:44
  46.4 1.3 copy-start.26
  46.4 1.3 copy-start.27
  47.0 0.7 copy-start.17
  47.7 14.7 %copy-start.6 = (bf16[72,16,128]{2,1,0:T(8,128)(2,1)S(1)}, bf16[72,16,128]{2,1,0:T(8,128)(2,1)}, u32[]{:S(2)}) copy-start(bf16[72,16,128]{2,1,0:T(8,128)(2,1)} %get-tuple-element.8.refs_0_.refs_8_.refs_11_) | copy-start | bytes 884740
  47.7 9.3 %collective-permute-start.16 = (bf16[108,16,128]{2,1,0:T(8,128)(2,1)S(1)}, bf16[108,16,128]{2,1,0:T(8,128)(2,1)S(1)}, u32[]{:S(2)}, u32[]{:S(2)}) collective-permute-start(bf16[108,16,128]{2,1,0:T(8,128)(2,1)S(1)} %get-tuple-element.18), channel_id=1, source_target_pairs={{0,96},{16,112},{32,0},{48,16},{64,32},{80,48},{96,64},{112,80},{1... | collective-permute-start | bytes 1327112 | tf_op jit(solution)/shard_map/ppermute | solution.py:34
  49.9 17.9 %collective-permute-start.8 = (bf16[216,16,128]{2,1,0:T(8,128)(2,1)}, bf16[216,16,128]{2,1,0:T(8,128)(2,1)S(1)}, u32[]{:S(2)}, u32[]{:S(2)}) collective-permute-start(bf16[216,16,128]{2,1,0:T(8,128)(2,1)} %pad_maximum_fusion), channel_id=1, source_target_pairs={{0,1},{1,0},{2,3},{3,2},{4,5},{5,4},{6,7},{7,6},{8,9},{9,8},{10,11... | collective-permute-start | bytes 2654216 | tf_op jit(solution)/shard_map/ppermute | solution.py:44
  49.9 13.8 %collective-permute-start.15 = (bf16[108,16,128]{2,1,0:T(8,128)(2,1)S(1)}, bf16[108,16,128]{2,1,0:T(8,128)(2,1)S(1)}, u32[]{:S(2)}, u32[]{:S(2)}) collective-permute-start(bf16[108,16,128]{2,1,0:T(8,128)(2,1)S(1)} %get-tuple-element.19), channel_id=1, source_target_pairs={{0,32},{16,48},{32,64},{48,80},{64,96},{80,112},{96,0},{112,16},{1... | collective-permute-start | bytes 1327112 | tf_op jit(solution)/shard_map/ppermute | solution.py:34
  52.2 15.6 %copy-start.4 = (bf16[108,16,128]{2,1,0:T(8,128)(2,1)}, bf16[108,16,128]{2,1,0:T(8,128)(2,1)S(1)}, u32[]{:S(2)}) copy-start(bf16[108,16,128]{2,1,0:T(8,128)(2,1)S(1)} %collective-permute-done.4.refs_5_.refs_13_.refs_16_) | copy-start | bytes 1327108
  52.2 6.4 %collective-permute-start.6 = (bf16[36,16,128]{2,1,0:T(8,128)(2,1)S(1)}, bf16[36,16,128]{2,1,0:T(8,128)(2,1)S(1)}, u32[]{:S(2)}, u32[]{:S(2)}) collective-permute-start(bf16[36,16,128]{2,1,0:T(8,128)(2,1)S(1)} %slice.59), channel_id=1, source_target_pairs={{0,12},{1,13},{2,14},{3,15},{4,0},{5,1},{6,2},{7,3},{8,4},{9,5},{1... | collective-permute-start | bytes 442376 | tf_op jit(solution)/shard_map/ppermute | solution.py:44
  56.0 11.9 %copy-start.5 = (bf16[108,16,128]{2,1,0:T(8,128)(2,1)}, bf16[108,16,128]{2,1,0:T(8,128)(2,1)S(1)}, u32[]{:S(2)}) copy-start(bf16[108,16,128]{2,1,0:T(8,128)(2,1)S(1)} %collective-permute-done.3.refs_4_.refs_12_.refs_15_) | copy-start | bytes 1327108
  56.0 6.4 %collective-permute-start.5 = (bf16[36,16,128]{2,1,0:T(8,128)(2,1)S(1)}, bf16[36,16,128]{2,1,0:T(8,128)(2,1)S(1)}, u32[]{:S(2)}, u32[]{:S(2)}) collective-permute-start(bf16[36,16,128]{2,1,0:T(8,128)(2,1)S(1)} %slice.58), channel_id=1, source_target_pairs={{0,4},{1,5},{2,6},{3,7},{4,8},{5,9},{6,10},{7,11},{8,12},{9,13},{1... | collective-permute-start | bytes 442376 | tf_op jit(solution)/shard_map/ppermute | solution.py:44
  57.0 9.1 %copy-start.24 = (bf16[108,16,128]{2,1,0:T(8,128)(2,1)}, bf16[108,16,128]{2,1,0:T(8,128)(2,1)S(1)}, u32[]{:S(2)}) copy-start(bf16[108,16,128]{2,1,0:T(8,128)(2,1)S(1)} %collective-permute-done.16.refs_5_) | copy-start | bytes 1327108
  57.0 9.1 %collective-permute-start.10 = (bf16[108,16,128]{2,1,0:T(8,128)(2,1)S(1)}, bf16[108,16,128]{2,1,0:T(8,128)(2,1)S(1)}, u32[]{:S(2)}, u32[]{:S(2)}) collective-permute-start(bf16[108,16,128]{2,1,0:T(8,128)(2,1)S(1)} %collective-permute-done.4.refs_5_.refs_13_.refs_16_), channel_id=1, source_target_pairs={{0,1},{1,0},{2,3},{3,2},{4,5},{5,4},{6,7},{7,6},{8,9},{9,8},{10,11... | collective-permute-start | bytes 1327112 | tf_op jit(solution)/shard_map/ppermute | solution.py:44
  58.7 9.2 %copy-start.14 = (bf16[36,16,128]{2,1,0:T(8,128)(2,1)}, bf16[36,16,128]{2,1,0:T(8,128)(2,1)S(1)}, u32[]{:S(2)}) copy-start(bf16[36,16,128]{2,1,0:T(8,128)(2,1)S(1)} %collective-permute-done.6.refs_7_.refs_15_.refs_18_) | copy-start | bytes 442372
  58.7 9.1 %collective-permute-start.9 = (bf16[108,16,128]{2,1,0:T(8,128)(2,1)S(1)}, bf16[108,16,128]{2,1,0:T(8,128)(2,1)S(1)}, u32[]{:S(2)}, u32[]{:S(2)}) collective-permute-start(bf16[108,16,128]{2,1,0:T(8,128)(2,1)S(1)} %collective-permute-done.3.refs_4_.refs_12_.refs_15_), channel_id=1, source_target_pairs={{0,1},{1,0},{2,3},{3,2},{4,5},{5,4},{6,7},{7,6},{8,9},{9,8},{10,11... | collective-permute-start | bytes 1327112 | tf_op jit(solution)/shard_map/ppermute | solution.py:44
  62.4 5.4 %copy-start.15 = (bf16[36,16,128]{2,1,0:T(8,128)(2,1)}, bf16[36,16,128]{2,1,0:T(8,128)(2,1)S(1)}, u32[]{:S(2)}) copy-start(bf16[36,16,128]{2,1,0:T(8,128)(2,1)S(1)} %collective-permute-done.5.refs_6_.refs_14_.refs_17_) | copy-start | bytes 442372
  62.4 2.7 %collective-permute-start.7 = (bf16[72,16,128]{2,1,0:T(8,128)(2,1)S(1)}, bf16[72,16,128]{2,1,0:T(8,128)(2,1)S(1)}, u32[]{:S(2)}, u32[]{:S(2)}) collective-permute-start(bf16[72,16,128]{2,1,0:T(8,128)(2,1)S(1)} %copy-done.6), channel_id=1, source_target_pairs={{0,1},{1,0},{2,3},{3,2},{4,5},{5,4},{6,7},{7,6},{8,9},{9,8},{10,11... | collective-permute-start | bytes 884744 | tf_op jit(solution)/shard_map/ppermute | solution.py:44
  63.7 3.5 %copy-start.25 = (bf16[108,16,128]{2,1,0:T(8,128)(2,1)}, bf16[108,16,128]{2,1,0:T(8,128)(2,1)S(1)}, u32[]{:S(2)}) copy-start(bf16[108,16,128]{2,1,0:T(8,128)(2,1)S(1)} %collective-permute-done.15.refs_4_) | copy-start | bytes 1327108
  63.7 4.1 %collective-permute-start.11 = (bf16[72,16,128]{2,1,0:T(8,128)(2,1)}, bf16[72,16,128]{2,1,0:T(8,128)(2,1)S(1)}, u32[]{:S(2)}, u32[]{:S(2)}) collective-permute-start(bf16[72,16,128]{2,1,0:T(8,128)(2,1)} %pad_maximum_fusion.6), channel_id=1, source_target_pairs={{0,1},{1,0},{2,3},{3,2},{4,5},{5,4},{6,7},{7,6},{8,9},{9,8},{10,11... | collective-permute-start | bytes 884744 | tf_op jit(solution)/shard_map/ppermute | solution.py:44
  65.1 2.8 %copy-start.12 = (bf16[72,16,128]{2,1,0:T(8,128)(2,1)}, bf16[72,16,128]{2,1,0:T(8,128)(2,1)S(1)}, u32[]{:S(2)}) copy-start(bf16[72,16,128]{2,1,0:T(8,128)(2,1)S(1)} %collective-permute-done.7.refs_8_.refs_16_.refs_19_) | copy-start | bytes 884740
  65.1 6.7 %collective-permute-start.18 = (bf16[36,16,128]{2,1,0:T(8,128)(2,1)}, bf16[36,16,128]{2,1,0:T(8,128)(2,1)}, u32[]{:S(2)}, u32[]{:S(2)}) collective-permute-start(bf16[36,16,128]{2,1,0:T(8,128)(2,1)} %slice.63), channel_id=1, source_target_pairs={{0,96},{16,112},{32,0},{48,16},{64,32},{80,48},{96,64},{112,80},{1... | collective-permute-start | bytes 442376 | tf_op jit(solution)/shard_map/ppermute | solution.py:34
  66.1 1.8 %copy-start.7 = (bf16[108,16,128]{2,1,0:T(8,128)(2,1)}, bf16[108,16,128]{2,1,0:T(8,128)(2,1)S(1)}, u32[]{:S(2)}) copy-start(bf16[108,16,128]{2,1,0:T(8,128)(2,1)S(1)} %collective-permute-done.10.refs_11_.refs_19_.refs_22_) | copy-start | bytes 1327108
  66.1 7.1 %collective-permute-start.17 = (bf16[36,16,128]{2,1,0:T(8,128)(2,1)}, bf16[36,16,128]{2,1,0:T(8,128)(2,1)}, u32[]{:S(2)}, u32[]{:S(2)}) collective-permute-start(bf16[36,16,128]{2,1,0:T(8,128)(2,1)} %slice.62), channel_id=1, source_target_pairs={{0,32},{16,48},{32,64},{48,80},{64,96},{80,112},{96,0},{112,16},{1... | collective-permute-start | bytes 442376 | tf_op jit(solution)/shard_map/ppermute | solution.py:34
  67.8 0.7 copy-start.13
  67.8 0.9 copy-start.8
  67.8 1.1 copy-start
  80.1 10.6 %collective-permute-start.21 = (bf16[100,16,128]{2,1,0:T(8,128)(2,1)}, bf16[100,16,128]{2,1,0:T(8,128)(2,1)S(1)}, u32[]{:S(2)}, u32[]{:S(2)}) collective-permute-start(bf16[100,16,128]{2,1,0:T(8,128)(2,1)} %shard_map.62.refs_0_), channel_id=1, source_target_pairs={{0,96},{16,112},{32,0},{48,16},{64,32},{80,48},{96,64},{112,80},{1... | collective-permute-start | bytes 1228808 | tf_op jit(solution)/shard_map/ppermute | solution.py:34
  81.0 12.0 %collective-permute-start.20 = (bf16[100,16,128]{2,1,0:T(8,128)(2,1)}, bf16[100,16,128]{2,1,0:T(8,128)(2,1)S(1)}, u32[]{:S(2)}, u32[]{:S(2)}) collective-permute-start(bf16[100,16,128]{2,1,0:T(8,128)(2,1)} %shard_map.62.refs_0_), channel_id=1, source_target_pairs={{0,32},{16,48},{32,64},{48,80},{64,96},{80,112},{96,0},{112,16},{1... | collective-permute-start | bytes 1228808 | tf_op jit(solution)/shard_map/ppermute | solution.py:34
  82.2 12.5 %collective-permute-start.19 = (bf16[100,16,128]{2,1,0:T(8,128)(2,1)}, bf16[100,16,128]{2,1,0:T(8,128)(2,1)S(1)}, u32[]{:S(2)}, u32[]{:S(2)}) collective-permute-start(bf16[100,16,128]{2,1,0:T(8,128)(2,1)} %shard_map.62.refs_0_), channel_id=1, source_target_pairs={{0,16},{16,0},{32,48},{48,32},{64,80},{80,64},{96,112},{112,96},{1... | collective-permute-start | bytes 1228808 | tf_op jit(solution)/shard_map/ppermute | solution.py:34
  90.6 2.4 %copy-start.9 = (bf16[100,16,128]{2,1,0:T(8,128)(2,1)}, bf16[100,16,128]{2,1,0:T(8,128)(2,1)S(1)}, u32[]{:S(2)}) copy-start(bf16[100,16,128]{2,1,0:T(8,128)(2,1)S(1)} %collective-permute-done.21.refs_3_) | copy-start | bytes 1228804
  93.0 1.7 %copy-start.10 = (bf16[100,16,128]{2,1,0:T(8,128)(2,1)}, bf16[100,16,128]{2,1,0:T(8,128)(2,1)S(1)}, u32[]{:S(2)}) copy-start(bf16[100,16,128]{2,1,0:T(8,128)(2,1)S(1)} %collective-permute-done.20.refs_2_) | copy-start | bytes 1228804
  93.1 16.0 %collective-permute-start.26 = (bf16[100,16,128]{2,1,0:T(8,128)(2,1)S(1)}, bf16[100,16,128]{2,1,0:T(8,128)(2,1)S(1)}, u32[]{:S(2)}, u32[]{:S(2)}) collective-permute-start(bf16[100,16,128]{2,1,0:T(8,128)(2,1)S(1)} %pad_maximum_fusion.5), channel_id=1, source_target_pairs={{0,16},{16,0},{32,48},{48,32},{64,80},{80,64},{96,112},{112,96},{1... | collective-permute-start | bytes 1228808 | tf_op jit(solution)/shard_map/ppermute | solution.py:34
  94.6 17.3 %copy-start.11 = (bf16[100,16,128]{2,1,0:T(8,128)(2,1)}, bf16[100,16,128]{2,1,0:T(8,128)(2,1)S(1)}, u32[]{:S(2)}) copy-start(bf16[100,16,128]{2,1,0:T(8,128)(2,1)S(1)} %collective-permute-done.19.refs_1_) | copy-start | bytes 1228804
  94.7 8.3 %collective-permute-start.24 = (bf16[50,16,128]{2,1,0:T(8,128)(2,1)S(1)}, bf16[50,16,128]{2,1,0:T(8,128)(2,1)S(1)}, u32[]{:S(2)}, u32[]{:S(2)}) collective-permute-start(bf16[50,16,128]{2,1,0:T(8,128)(2,1)S(1)} %get-tuple-element.16), channel_id=1, source_target_pairs={{0,96},{16,112},{32,0},{48,16},{64,32},{80,48},{96,64},{112,80},{1... | collective-permute-start | bytes 614408 | tf_op jit(solution)/shard_map/ppermute | solution.py:34
  95.8 9.2 %collective-permute-start.22 = (bf16[50,16,128]{2,1,0:T(8,128)(2,1)S(1)}, bf16[50,16,128]{2,1,0:T(8,128)(2,1)S(1)}, u32[]{:S(2)}, u32[]{:S(2)}) collective-permute-start(bf16[50,16,128]{2,1,0:T(8,128)(2,1)S(1)} %get-tuple-element.17), channel_id=1, source_target_pairs={{0,32},{16,48},{32,64},{48,80},{64,96},{80,112},{96,0},{112,16},{1... | collective-permute-start | bytes 614408 | tf_op jit(solution)/shard_map/ppermute | solution.py:34
  96.9 9.6 %collective-permute-start.25 = (bf16[50,16,128]{2,1,0:T(8,128)(2,1)S(1)}, bf16[50,16,128]{2,1,0:T(8,128)(2,1)S(1)}, u32[]{:S(2)}, u32[]{:S(2)}) collective-permute-start(bf16[50,16,128]{2,1,0:T(8,128)(2,1)S(1)} %get-tuple-element.13), channel_id=1, source_target_pairs={{0,96},{16,112},{32,0},{48,16},{64,32},{80,48},{96,64},{112,80},{1... | collective-permute-start | bytes 614408 | tf_op jit(solution)/shard_map/ppermute | solution.py:34
  99.0 10.1 %collective-permute-start.23 = (bf16[50,16,128]{2,1,0:T(8,128)(2,1)S(1)}, bf16[50,16,128]{2,1,0:T(8,128)(2,1)S(1)}, u32[]{:S(2)}, u32[]{:S(2)}) collective-permute-start(bf16[50,16,128]{2,1,0:T(8,128)(2,1)S(1)} %get-tuple-element.15), channel_id=1, source_target_pairs={{0,32},{16,48},{32,64},{48,80},{64,96},{80,112},{96,0},{112,16},{1... | collective-permute-start | bytes 614408 | tf_op jit(solution)/shard_map/ppermute | solution.py:34
  102.9 9.0 %copy-start.18 = (bf16[50,16,128]{2,1,0:T(8,128)(2,1)}, bf16[50,16,128]{2,1,0:T(8,128)(2,1)S(1)}, u32[]{:S(2)}) copy-start(bf16[50,16,128]{2,1,0:T(8,128)(2,1)S(1)} %collective-permute-done.24.refs_6_) | copy-start | bytes 614404
  102.9 6.2 %collective-permute-start.28 = (bf16[50,16,128]{2,1,0:T(8,128)(2,1)S(1)}, bf16[50,16,128]{2,1,0:T(8,128)(2,1)S(1)}, u32[]{:S(2)}, u32[]{:S(2)}) collective-permute-start(bf16[50,16,128]{2,1,0:T(8,128)(2,1)S(1)} %collective-permute-done.24.refs_6_), channel_id=1, source_target_pairs={{0,96},{16,112},{32,0},{48,16},{64,32},{80,48},{96,64},{112,80},{1... | collective-permute-start | bytes 614408 | tf_op jit(solution)/shard_map/ppermute | solution.py:34
  105.0 7.0 %copy-start.19 = (bf16[50,16,128]{2,1,0:T(8,128)(2,1)}, bf16[50,16,128]{2,1,0:T(8,128)(2,1)S(1)}, u32[]{:S(2)}) copy-start(bf16[50,16,128]{2,1,0:T(8,128)(2,1)S(1)} %collective-permute-done.22.refs_4_) | copy-start | bytes 614404
  105.0 7.0 %collective-permute-start.27 = (bf16[50,16,128]{2,1,0:T(8,128)(2,1)S(1)}, bf16[50,16,128]{2,1,0:T(8,128)(2,1)S(1)}, u32[]{:S(2)}, u32[]{:S(2)}) collective-permute-start(bf16[50,16,128]{2,1,0:T(8,128)(2,1)S(1)} %collective-permute-done.22.refs_4_), channel_id=1, source_target_pairs={{0,32},{16,48},{32,64},{48,80},{64,96},{80,112},{96,0},{112,16},{1... | collective-permute-start | bytes 614408 | tf_op jit(solution)/shard_map/ppermute | solution.py:34
  106.5 5.4 %copy-start.20 = (bf16[50,16,128]{2,1,0:T(8,128)(2,1)}, bf16[50,16,128]{2,1,0:T(8,128)(2,1)S(1)}, u32[]{:S(2)}) copy-start(bf16[50,16,128]{2,1,0:T(8,128)(2,1)S(1)} %collective-permute-done.25.refs_7_) | copy-start | bytes 614404
  109.1 2.8 %copy-start.21 = (bf16[50,16,128]{2,1,0:T(8,128)(2,1)}, bf16[50,16,128]{2,1,0:T(8,128)(2,1)S(1)}, u32[]{:S(2)}) copy-start(bf16[50,16,128]{2,1,0:T(8,128)(2,1)S(1)} %collective-permute-done.23.refs_5_) | copy-start | bytes 614404
  109.1 2.9 %copy-start.16 = (bf16[100,16,128]{2,1,0:T(8,128)(2,1)}, bf16[100,16,128]{2,1,0:T(8,128)(2,1)S(1)}, u32[]{:S(2)}) copy-start(bf16[100,16,128]{2,1,0:T(8,128)(2,1)S(1)} %collective-permute-done.26.refs_8_) | copy-start | bytes 1228804
  109.1 2.9 %copy-start.22 = (bf16[50,16,128]{2,1,0:T(8,128)(2,1)}, bf16[50,16,128]{2,1,0:T(8,128)(2,1)S(1)}, u32[]{:S(2)}) copy-start(bf16[50,16,128]{2,1,0:T(8,128)(2,1)S(1)} %collective-permute-done.28.refs_10_) | copy-start | bytes 614404
  111.9 0.7 copy-start.23
  120.8 16.6 %all-to-all-start.1 = ((bf16[64,16,512]{2,1,0:T(8,128)(2,1)}), bf16[64,16,512]{2,1,0:T(8,128)(2,1)S(1)}, u32[]{:S(2)}, u32[]{:S(2)}) async-start(bf16[64,16,512]{2,1,0:T(8,128)(2,1)} %shard_map.64), calls=%async_computation.1 | async-start | bytes 2097152 | tf_op jit(solution)/shard_map/all_to_all | solution.py:476

commit v6 on v5

--- a/solution.py
+++ b/solution.py
@@ -78,17 +78,11 @@
     packed[...] = jnp.zeros_like(packed)
     copy.wait()
 
-    def kept(b, counts):
-        for q in range(8):
-            i = 8 * b + q
-            out = []
-            for n in range(4):
-                packed[n * SLOTS + counts[n]] = sliced[b, 8 * n + q]
-                out.append(counts[n] + flags_s[n, i])
-            counts = tuple(out)
-        return counts
-
-    lax.fori_loop(0, TR, kept, (jnp.int32(0),) * 4)
+    counts = [jnp.int32(0)] * 4
+    for i in range(NB):
+        for n in range(4):
+            packed[n * SLOTS + counts[n]] = sliced[i // 8, 8 * n + i % 8]
+            counts[n] = counts[n] + flags_s[n, i]
     packed[KP] = marks.astype(BF)
     packed[ZERO] = jnp.zeros((SL, BLOCK), BF)
 

time: 139 us -> 139 us (level)
  no operation moved by 1% of the time
where the time goes in v6:
time: 139 us; the launch traced here: 138 us
  waiting for transfers between devices  41.4 us (30%)
  starting transfers between devices  35.9 us (26%)
  Pallas kernels  30.3 us (22%)
  blocking collectives  21.8 us (16%)
  local copies, waits for them, and re-layouts  5.05 us (4%)
  other arithmetic  2.51 us (2%)
    ppermute x17, waiting for transfers between devices, row_shift(): return lax.ppermute(value, 'row', pairs)  23.5 us
    all_to_all x1, blocking collectives, on_device(): sliced = lax.all_to_all(sent, 'row', 0, 0, tiled=True)  21.8 us
    ppermute x17, starting transfers between devices, row_shift(): return lax.ppermute(value, 'row', pairs)  18.3 us
    ppermute x12, starting transfers between devices, col_shift(): return lax.ppermute(value, 'col', pairs)  14 us
    ppermute x12, waiting for transfers between devices, col_shift(): return lax.ppermute(value, 'col', pairs)  11.7 us
    pallas_call x1, Pallas kernels, on_device(): call(step_kernel, jax.ShapeDtypeStruct((NB, SL, 4 * BLOCK), BF), [SMEM] +...  8.19 us
    pallas_call x1, Pallas kernels, on_device(): call(square_rows_kernel, jax.ShapeDtypeStruct((8, TR, SL, 4 * BLOCK), BF)...  6.83 us
    pallas_call x1, Pallas kernels, on_device(): call(square_kernel, jax.ShapeDtypeStruct((4 * KS, SL, BLOCK), BF), [SMEM]...  6.79 us
  transfers between devices with their start and end apart: 30, of which 17 were waited for; matrix products, arithmetic and copies ran while one was open for 3% of the time, Pallas kernels for 7%

profile of v6, /device:TPU:0, one launch (start us, length us, event | category | flops | bytes accessed | tf_op | source)
XLA Modules:
  0.0 138.0 jit_solution(12943518909903977886)
XLA Ops:
  0.6 2.5 %shard_map.59 = bf16[8,33,16,128]{3,2,1,0:T(8,128)(2,1)} custom-call(bf16[8,8,16,512]{3,2,1,0:T(8,128)(2,1)} %bitcast.13, s32[4,8]{1,0:T(4,128)} %bitcast.15, s32[4,8]{1,0:T(4,128)} %bitcast.16, s32[4,8]{1,0:T(4,128)} %bitcast.17), custom_call_target="tpu_custom_call" | custom-call | bytes 2097152 | tf_op jit(solution)/shard_map/pallas_call | solution.py:394
  3.2 21.8 %all_to_all.10.sliced = bf16[8,33,16,128]{3,2,1,0:T(8,128)(2,1)} all-to-all(bf16[8,33,16,128]{3,2,1,0:T(8,128)(2,1)} %shard_map.59), channel_id=1, replica_groups=mesh['row'=8,'col'=16] {'row'}, dimensions={0} | all-to-all | bytes 2162688 | tf_op jit(solution)/shard_map/all_to_all | solution.py:403
  25.0 3.0 %shard_map.60 = (bf16[72,16,128]{2,1,0:T(8,128)(2,1)}, s32[16,128]{1,0:T(8,128)}) custom-call(bf16[8,33,16,128]{3,2,1,0:T(8,128)(2,1)} %all_to_all.10.sliced), custom_call_target="tpu_custom_call" | custom-call | bytes 2097152 | tf_op jit(solution)/shard_map/pallas_call | solution.py:405
  28.0 4.1 %collective-permute-start.2 = (bf16[72,16,128]{2,1,0:T(8,128)(2,1)}, bf16[72,16,128]{2,1,0:T(8,128)(2,1)S(1)}, u32[]{:S(2)}, u32[]{:S(2)}) collective-permute-start(bf16[72,16,128]{2,1,0:T(8,128)(2,1)} %get-tuple-element.8.refs_0_.refs_8_.refs_11_), channel_id=1, source_target_pairs={{0,12},{1,13},{2,14},{3,15},{4,0},{5,1},{6,2},{7,3},{8,4},{9,5},{1... | collective-permute-start | bytes 884744 | tf_op jit(solution)/shard_map/ppermute | solution.py:44
  32.1 0.0 collective-permute-start.1
  32.2 2.9 %collective-permute-start = (bf16[72,16,128]{2,1,0:T(8,128)(2,1)}, bf16[72,16,128]{2,1,0:T(8,128)(2,1)S(1)}, u32[]{:S(2)}, u32[]{:S(2)}) collective-permute-start(bf16[72,16,128]{2,1,0:T(8,128)(2,1)} %get-tuple-element.8.refs_0_.refs_8_.refs_11_), channel_id=1, source_target_pairs={{0,2},{1,3},{2,0},{3,1},{4,6},{5,7},{6,4},{7,5},{8,10},{9,11},{10,... | collective-permute-start | bytes 884744 | tf_op jit(solution)/shard_map/ppermute | solution.py:44
  35.1 1.2 collective-permute-start.14
  36.2 0.9 collective-permute-start.13
  37.1 0.1 collective-permute-done.2.refs_3_.refs_11_.refs_14_
  37.2 0.8 collective-permute-start.12
  38.0 2.5 %collective-permute-done.1.refs_2_.refs_10_.refs_13_ = bf16[72,16,128]{2,1,0:T(8,128)(2,1)S(1)} collective-permute-done((bf16[72,16,128]{2,1,0:T(8,128)(2,1)}, bf16[72,16,128]{2,1,0:T(8,128)(2,1)S(1)}, u32[]{:S(2)}, u32[]{:S(2)}) %collective-permute-start.1) | collective-permute-done | bytes 294944 | tf_op jit(solution)/shard_map/ppermute | solution.py:44
  40.5 2.3 %collective-permute-done.refs_1_.refs_9_.refs_12_ = bf16[72,16,128]{2,1,0:T(8,128)(2,1)S(1)} collective-permute-done((bf16[72,16,128]{2,1,0:T(8,128)(2,1)}, bf16[72,16,128]{2,1,0:T(8,128)(2,1)S(1)}, u32[]{:S(2)}, u32[]{:S(2)}) %collective-permute-start) | collective-permute-done | bytes 294944 | tf_op jit(solution)/shard_map/ppermute | solution.py:44
  42.8 0.1 pad_maximum_fusion.1
  42.9 3.2 %collective-permute-start.4 = (bf16[108,16,128]{2,1,0:T(8,128)(2,1)S(1)}, bf16[108,16,128]{2,1,0:T(8,128)(2,1)S(1)}, u32[]{:S(2)}, u32[]{:S(2)}) collective-permute-start(bf16[108,16,128]{2,1,0:T(8,128)(2,1)S(1)} %get-tuple-element.20), channel_id=1, source_target_pairs={{0,12},{1,13},{2,14},{3,15},{4,0},{5,1},{6,2},{7,3},{8,4},{9,5},{1... | collective-permute-start | bytes 1327112 | tf_op jit(solution)/shard_map/ppermute | solution.py:44
  46.1 0.0 collective-permute-done.14.refs_3_
  46.2 0.5 collective-permute-done.12.refs_1_
  46.7 0.1 pad_maximum_fusion.3
  46.8 0.7 copy-done.17
  47.4 1.2 collective-permute-start.16
  48.6 1.0 pad_maximum_fusion
  49.6 0.9 collective-permute-start.15
  50.5 1.4 %collective-permute-done.4.refs_5_.refs_13_.refs_16_ = bf16[108,16,128]{2,1,0:T(8,128)(2,1)S(1)} collective-permute-done((bf16[108,16,128]{2,1,0:T(8,128)(2,1)S(1)}, bf16[108,16,128]{2,1,0:T(8,128)(2,1)S(1)}, u32[]{:S(2)}, u32[]{:S(2)}) %collective-permute-start.4) | collective-permute-done | bytes 442400 | tf_op jit(solution)/shard_map/ppermute | solution.py:44
  51.9 3.8 %collective-permute-start.6 = (bf16[36,16,128]{2,1,0:T(8,128)(2,1)S(1)}, bf16[36,16,128]{2,1,0:T(8,128)(2,1)S(1)}, u32[]{:S(2)}, u32[]{:S(2)}) collective-permute-start(bf16[36,16,128]{2,1,0:T(8,128)(2,1)S(1)} %slice.59), channel_id=1, source_target_pairs={{0,12},{1,13},{2,14},{3,15},{4,0},{5,1},{6,2},{7,3},{8,4},{9,5},{1... | collective-permute-start | bytes 442376 | tf_op jit(solution)/shard_map/ppermute | solution.py:44
  55.7 0.1 collective-permute-start.5
  55.8 0.9 collective-permute-done.16.refs_5_
  56.7 1.6 %collective-permute-done.6.refs_7_.refs_15_.refs_18_ = bf16[36,16,128]{2,1,0:T(8,128)(2,1)S(1)} collective-permute-done((bf16[36,16,128]{2,1,0:T(8,128)(2,1)S(1)}, bf16[36,16,128]{2,1,0:T(8,128)(2,1)S(1)}, u32[]{:S(2)}, u32[]{:S(2)}) %collective-permute-start.6) | collective-permute-done | bytes 147488 | tf_op jit(solution)/shard_map/ppermute | solution.py:44
  58.4 3.8 %collective-permute-done.5.refs_6_.refs_14_.refs_17_ = bf16[36,16,128]{2,1,0:T(8,128)(2,1)S(1)} collective-permute-done((bf16[36,16,128]{2,1,0:T(8,128)(2,1)S(1)}, bf16[36,16,128]{2,1,0:T(8,128)(2,1)S(1)}, u32[]{:S(2)}, u32[]{:S(2)}) %collective-permute-start.5) | collective-permute-done | bytes 147488 | tf_op jit(solution)/shard_map/ppermute | solution.py:44
  62.1 0.8 pad_maximum_fusion.6
  62.9 0.5 collective-permute-done.15.refs_4_
  63.4 0.7 slice.63
  64.1 0.7 slice.62
  64.8 1.0 collective-permute-start.18
  65.8 1.1 collective-permute-start.17
  66.9 0.6 pad_add_fusion.place
  67.5 0.0 copy-start
  67.6 0.6 copy-done.13
  68.2 0.2 copy-done.8
  68.4 0.3 copy-done
  68.7 2.9 %shard_map.61 = (s32[128,128]{1,0:T(8,128)}, s32[128,128]{1,0:T(8,128)}, s32[128,128]{1,0:T(8,128)}) custom-call(s32[2]{0:T(128)} %pad_add_fusion.place, s32[16,128]{1,0:T(8,128)} %get-tuple-element.7.flags, bf16[72,16,128]{2,1,0:T(8,128)(2,1)} %get-tuple-element.8.refs_0_.refs_8_.refs_11_, bf16[72,16,128]{2,1,0:T(8,128)(2,1)} %copy-done.1, ...), custom_call_target="tpu_custom_call" | custom-call | flops 1048576 | bytes 12582912 | tf_op jit(solution)/shard_map/pallas_call | solution.py:420
  71.6 1.4 %collective-permute-done.17.refs_6_ = bf16[36,16,128]{2,1,0:T(8,128)(2,1)} collective-permute-done((bf16[36,16,128]{2,1,0:T(8,128)(2,1)}, bf16[36,16,128]{2,1,0:T(8,128)(2,1)}, u32[]{:S(2)}, u32[]{:S(2)}) %collective-permute-start.17) | collective-permute-done | bytes 147488 | tf_op jit(solution)/shard_map/ppermute | solution.py:34
  73.0 6.8 %shard_map.62.refs_0_ = bf16[100,16,128]{2,1,0:T(8,128)(2,1)} custom-call(s32[2]{0:T(128)} %pad_add_fusion.place, s32[128,128]{1,0:T(8,128)} %get-tuple-element.10.square_slots, bf16[72,16,128]{2,1,0:T(8,128)(2,1)} %get-tuple-element.8.refs_0_.refs_8_.refs_11_, bf16[72,16,128]{2,1,0:T(8,128)(2,1)} %copy-done.17, bf16[72,16,128]{2,1,0:T(8,128)(2,1)} %copy-done.27, ...), custom_call_target="tpu_custom_call" | custom-call | flops 891289600 | bytes 9437184 | tf_op jit(solution)/shard_map/pallas_call | solution.py:433
  79.8 0.9 collective-permute-start.21
  80.7 1.2 collective-permute-start.20
  81.9 1.4 %collective-permute-start.19 = (bf16[100,16,128]{2,1,0:T(8,128)(2,1)}, bf16[100,16,128]{2,1,0:T(8,128)(2,1)S(1)}, u32[]{:S(2)}, u32[]{:S(2)}) collective-permute-start(bf16[100,16,128]{2,1,0:T(8,128)(2,1)} %shard_map.62.refs_0_), channel_id=1, source_target_pairs={{0,16},{16,0},{32,48},{48,32},{64,80},{80,64},{96,112},{112,96},{1... | collective-permute-start | bytes 1228808 | tf_op jit(solution)/shard_map/ppermute | solution.py:34
  83.3 7.0 %collective-permute-done.21.refs_3_ = bf16[100,16,128]{2,1,0:T(8,128)(2,1)S(1)} collective-permute-done((bf16[100,16,128]{2,1,0:T(8,128)(2,1)}, bf16[100,16,128]{2,1,0:T(8,128)(2,1)S(1)}, u32[]{:S(2)}, u32[]{:S(2)}) %collective-permute-start.21) | collective-permute-done | bytes 409632 | tf_op jit(solution)/shard_map/ppermute | solution.py:34
  90.4 2.3 %collective-permute-done.20.refs_2_ = bf16[100,16,128]{2,1,0:T(8,128)(2,1)S(1)} collective-permute-done((bf16[100,16,128]{2,1,0:T(8,128)(2,1)}, bf16[100,16,128]{2,1,0:T(8,128)(2,1)S(1)}, u32[]{:S(2)}, u32[]{:S(2)}) %collective-permute-start.20) | collective-permute-done | bytes 409632 | tf_op jit(solution)/shard_map/ppermute | solution.py:34
  92.8 1.7 %collective-permute-start.26 = (bf16[100,16,128]{2,1,0:T(8,128)(2,1)S(1)}, bf16[100,16,128]{2,1,0:T(8,128)(2,1)S(1)}, u32[]{:S(2)}, u32[]{:S(2)}) collective-permute-start(bf16[100,16,128]{2,1,0:T(8,128)(2,1)S(1)} %pad_maximum_fusion.5), channel_id=1, source_target_pairs={{0,16},{16,0},{32,48},{48,32},{64,80},{80,64},{96,112},{112,96},{1... | collective-permute-start | bytes 1228808 | tf_op jit(solution)/shard_map/ppermute | solution.py:34
  94.5 0.8 collective-permute-start.24
  95.3 1.3 collective-permute-start.22
  96.6 1.9 %collective-permute-start.25 = (bf16[50,16,128]{2,1,0:T(8,128)(2,1)S(1)}, bf16[50,16,128]{2,1,0:T(8,128)(2,1)S(1)}, u32[]{:S(2)}, u32[]{:S(2)}) collective-permute-start(bf16[50,16,128]{2,1,0:T(8,128)(2,1)S(1)} %get-tuple-element.13), channel_id=1, source_target_pairs={{0,96},{16,112},{32,0},{48,16},{64,32},{80,48},{96,64},{112,80},{1... | collective-permute-start | bytes 614408 | tf_op jit(solution)/shard_map/ppermute | solution.py:34
  98.5 0.1 collective-permute-start.23
  98.7 4.0 %collective-permute-done.24.refs_6_ = bf16[50,16,128]{2,1,0:T(8,128)(2,1)S(1)} collective-permute-done((bf16[50,16,128]{2,1,0:T(8,128)(2,1)S(1)}, bf16[50,16,128]{2,1,0:T(8,128)(2,1)S(1)}, u32[]{:S(2)}, u32[]{:S(2)}) %collective-permute-start.24) | collective-permute-done | bytes 204832 | tf_op jit(solution)/shard_map/ppermute | solution.py:34
  102.6 1.8 %collective-permute-start.28 = (bf16[50,16,128]{2,1,0:T(8,128)(2,1)S(1)}, bf16[50,16,128]{2,1,0:T(8,128)(2,1)S(1)}, u32[]{:S(2)}, u32[]{:S(2)}) collective-permute-start(bf16[50,16,128]{2,1,0:T(8,128)(2,1)S(1)} %collective-permute-done.24.refs_6_), channel_id=1, source_target_pairs={{0,96},{16,112},{32,0},{48,16},{64,32},{80,48},{96,64},{112,80},{1... | collective-permute-start | bytes 614408 | tf_op jit(solution)/shard_map/ppermute | solution.py:34
  104.4 0.0 collective-permute-done.22.refs_4_
  104.5 0.2 collective-permute-start.27
  104.7 1.5 %collective-permute-done.25.refs_7_ = bf16[50,16,128]{2,1,0:T(8,128)(2,1)S(1)} collective-permute-done((bf16[50,16,128]{2,1,0:T(8,128)(2,1)S(1)}, bf16[50,16,128]{2,1,0:T(8,128)(2,1)S(1)}, u32[]{:S(2)}, u32[]{:S(2)}) %collective-permute-start.25) | collective-permute-done | bytes 204832 | tf_op jit(solution)/shard_map/ppermute | solution.py:34
  106.2 2.4 %collective-permute-done.23.refs_5_ = bf16[50,16,128]{2,1,0:T(8,128)(2,1)S(1)} collective-permute-done((bf16[50,16,128]{2,1,0:T(8,128)(2,1)S(1)}, bf16[50,16,128]{2,1,0:T(8,128)(2,1)S(1)}, u32[]{:S(2)}, u32[]{:S(2)}) %collective-permute-start.23) | collective-permute-done | bytes 204832 | tf_op jit(solution)/shard_map/ppermute | solution.py:34
  108.6 2.8 %collective-permute-done.27.refs_9_ = bf16[50,16,128]{2,1,0:T(8,128)(2,1)S(1)} collective-permute-done((bf16[50,16,128]{2,1,0:T(8,128)(2,1)S(1)}, bf16[50,16,128]{2,1,0:T(8,128)(2,1)S(1)}, u32[]{:S(2)}, u32[]{:S(2)}) %collective-permute-start.27) | collective-permute-done | bytes 204832 | tf_op jit(solution)/shard_map/ppermute | solution.py:34
  111.5 0.6 copy-done.23
  112.1 8.2 %shard_map.64 = bf16[64,16,512]{2,1,0:T(8,128)(2,1)} custom-call(s32[2]{0:T(128)} %pad_add_fusion.place, s32[128,128]{1,0:T(8,128)} %get-tuple-element.9.lists.all_lists, s32[128,128]{1,0:T(8,128)} %get-tuple-element.11.step_slots, bf16[100,16,128]{2,1,0:T(8,128)(2,1)} %shard_map.62.refs_0_, bf16[100,16,128]{2,1,0:T(8,128)(2,1)} %copy-done.11, ...), custom_call_target="tpu_custom_call" | custom-call | flops 1101004800 | bytes 9437184 | tf_op jit(solution)/shard_map/pallas_call | solution.py:451
  120.3 3.6 %all-to-all-start.1 = ((bf16[64,16,512]{2,1,0:T(8,128)(2,1)}), bf16[64,16,512]{2,1,0:T(8,128)(2,1)S(1)}, u32[]{:S(2)}, u32[]{:S(2)}) async-start(bf16[64,16,512]{2,1,0:T(8,128)(2,1)} %shard_map.64), calls=%async_computation.1 | async-start | bytes 2097152 | tf_op jit(solution)/shard_map/all_to_all | solution.py:470
  123.9 6.8 %shard_map.63 = bf16[8,8,16,512]{3,2,1,0:T(8,128)(2,1)} custom-call(s32[2]{0:T(128)} %pad_add_fusion.place, s32[128,128]{1,0:T(8,128)} %get-tuple-element.9.lists.all_lists, bf16[100,16,128]{2,1,0:T(8,128)(2,1)} %shard_map.62.refs_0_, bf16[100,16,128]{2,1,0:T(8,128)(2,1)} %copy-done.11, bf16[100,16,128]{2,1,0:T(8,128)(2,1)} %copy-done.10, ...), custom_call_target="tpu_custom_call" | custom-call | bytes 4194304 | tf_op jit(solution)/shard_map/pallas_call | solution.py:471
  130.7 6.1 %all-to-all-done.1 = bf16[64,16,512]{2,1,0:T(8,128)(2,1)S(1)} async-done(((bf16[64,16,512]{2,1,0:T(8,128)(2,1)}), bf16[64,16,512]{2,1,0:T(8,128)(2,1)S(1)}, u32[]{:S(2)}, u32[]{:S(2)}) %all-to-all-start.1) | async-done | bytes 1048608 | tf_op jit(solution)/shard_map/all_to_all | solution.py:470
  136.9 1.1 copy.6
  (77 shorter events, 0.3 us)
Async XLA Ops:
  28.0 9.2 %collective-permute-start.2 = (bf16[72,16,128]{2,1,0:T(8,128)(2,1)}, bf16[72,16,128]{2,1,0:T(8,128)(2,1)S(1)}, u32[]{:S(2)}, u32[]{:S(2)}) collective-permute-start(bf16[72,16,128]{2,1,0:T(8,128)(2,1)} %get-tuple-element.8.refs_0_.refs_8_.refs_11_), channel_id=1, source_target_pairs={{0,12},{1,13},{2,14},{3,15},{4,0},{5,1},{6,2},{7,3},{8,4},{9,5},{1... | collective-permute-start | bytes 884744 | tf_op jit(solution)/shard_map/ppermute | solution.py:44
  32.1 8.4 %collective-permute-start.1 = (bf16[72,16,128]{2,1,0:T(8,128)(2,1)}, bf16[72,16,128]{2,1,0:T(8,128)(2,1)S(1)}, u32[]{:S(2)}, u32[]{:S(2)}) collective-permute-start(bf16[72,16,128]{2,1,0:T(8,128)(2,1)} %get-tuple-element.8.refs_0_.refs_8_.refs_11_), channel_id=1, source_target_pairs={{0,4},{1,5},{2,6},{3,7},{4,8},{5,9},{6,10},{7,11},{8,12},{9,13},{1... | collective-permute-start | bytes 884744 | tf_op jit(solution)/shard_map/ppermute | solution.py:44
  32.2 10.7 %collective-permute-start = (bf16[72,16,128]{2,1,0:T(8,128)(2,1)}, bf16[72,16,128]{2,1,0:T(8,128)(2,1)S(1)}, u32[]{:S(2)}, u32[]{:S(2)}) collective-permute-start(bf16[72,16,128]{2,1,0:T(8,128)(2,1)} %get-tuple-element.8.refs_0_.refs_8_.refs_11_), channel_id=1, source_target_pairs={{0,2},{1,3},{2,0},{3,1},{4,6},{5,7},{6,4},{7,5},{8,10},{9,11},{10,... | collective-permute-start | bytes 884744 | tf_op jit(solution)/shard_map/ppermute | solution.py:44
  35.1 11.0 %collective-permute-start.14 = (bf16[72,16,128]{2,1,0:T(8,128)(2,1)}, bf16[72,16,128]{2,1,0:T(8,128)(2,1)S(1)}, u32[]{:S(2)}, u32[]{:S(2)}) collective-permute-start(bf16[72,16,128]{2,1,0:T(8,128)(2,1)} %get-tuple-element.8.refs_0_.refs_8_.refs_11_), channel_id=1, source_target_pairs={{0,96},{16,112},{32,0},{48,16},{64,32},{80,48},{96,64},{112,80},{1... | collective-permute-start | bytes 884744 | tf_op jit(solution)/shard_map/ppermute | solution.py:34
  36.2 9.9 %collective-permute-start.13 = (bf16[72,16,128]{2,1,0:T(8,128)(2,1)}, bf16[72,16,128]{2,1,0:T(8,128)(2,1)S(1)}, u32[]{:S(2)}, u32[]{:S(2)}) collective-permute-start(bf16[72,16,128]{2,1,0:T(8,128)(2,1)} %get-tuple-element.8.refs_0_.refs_8_.refs_11_), channel_id=1, source_target_pairs={{0,32},{16,48},{32,64},{48,80},{64,96},{80,112},{96,0},{112,16},{1... | collective-permute-start | bytes 884744 | tf_op jit(solution)/shard_map/ppermute | solution.py:34
  37.2 11.4 %copy-start.2 = (bf16[72,16,128]{2,1,0:T(8,128)(2,1)}, bf16[72,16,128]{2,1,0:T(8,128)(2,1)S(1)}, u32[]{:S(2)}) copy-start(bf16[72,16,128]{2,1,0:T(8,128)(2,1)S(1)} %collective-permute-done.2.refs_3_.refs_11_.refs_14_) | copy-start | bytes 884740
  37.2 9.5 %collective-permute-start.12 = (bf16[72,16,128]{2,1,0:T(8,128)(2,1)}, bf16[72,16,128]{2,1,0:T(8,128)(2,1)S(1)}, u32[]{:S(2)}, u32[]{:S(2)}) collective-permute-start(bf16[72,16,128]{2,1,0:T(8,128)(2,1)} %get-tuple-element.8.refs_0_.refs_8_.refs_11_), channel_id=1, source_target_pairs={{0,16},{16,0},{32,48},{48,32},{64,80},{80,64},{96,112},{112,96},{1... | collective-permute-start | bytes 884744 | tf_op jit(solution)/shard_map/ppermute | solution.py:34
  40.5 8.1 %copy-start.3 = (bf16[72,16,128]{2,1,0:T(8,128)(2,1)}, bf16[72,16,128]{2,1,0:T(8,128)(2,1)S(1)}, u32[]{:S(2)}) copy-start(bf16[72,16,128]{2,1,0:T(8,128)(2,1)S(1)} %collective-permute-done.1.refs_2_.refs_10_.refs_13_) | copy-start | bytes 884740
  42.8 5.8 %copy-start.1 = (bf16[72,16,128]{2,1,0:T(8,128)(2,1)}, bf16[72,16,128]{2,1,0:T(8,128)(2,1)S(1)}, u32[]{:S(2)}) copy-start(bf16[72,16,128]{2,1,0:T(8,128)(2,1)S(1)} %collective-permute-done.refs_1_.refs_9_.refs_12_) | copy-start | bytes 884740
  42.9 9.0 %collective-permute-start.4 = (bf16[108,16,128]{2,1,0:T(8,128)(2,1)S(1)}, bf16[108,16,128]{2,1,0:T(8,128)(2,1)S(1)}, u32[]{:S(2)}, u32[]{:S(2)}) collective-permute-start(bf16[108,16,128]{2,1,0:T(8,128)(2,1)S(1)} %get-tuple-element.20), channel_id=1, source_target_pairs={{0,12},{1,13},{2,14},{3,15},{4,0},{5,1},{6,2},{7,3},{8,4},{9,5},{1... | collective-permute-start | bytes 1327112 | tf_op jit(solution)/shard_map/ppermute | solution.py:44
  46.1 9.6 %collective-permute-start.3 = (bf16[108,16,128]{2,1,0:T(8,128)(2,1)S(1)}, bf16[108,16,128]{2,1,0:T(8,128)(2,1)S(1)}, u32[]{:S(2)}, u32[]{:S(2)}) collective-permute-start(bf16[108,16,128]{2,1,0:T(8,128)(2,1)S(1)} %get-tuple-element.21), channel_id=1, source_target_pairs={{0,4},{1,5},{2,6},{3,7},{4,8},{5,9},{6,10},{7,11},{8,12},{9,13},{1... | collective-permute-start | bytes 1327112 | tf_op jit(solution)/shard_map/ppermute | solution.py:44
  46.1 1.3 copy-start.26
  46.1 1.3 copy-start.27
  46.7 0.7 copy-start.17
  47.4 14.7 %copy-start.6 = (bf16[72,16,128]{2,1,0:T(8,128)(2,1)S(1)}, bf16[72,16,128]{2,1,0:T(8,128)(2,1)}, u32[]{:S(2)}) copy-start(bf16[72,16,128]{2,1,0:T(8,128)(2,1)} %get-tuple-element.8.refs_0_.refs_8_.refs_11_) | copy-start | bytes 884740
  47.4 9.3 %collective-permute-start.16 = (bf16[108,16,128]{2,1,0:T(8,128)(2,1)S(1)}, bf16[108,16,128]{2,1,0:T(8,128)(2,1)S(1)}, u32[]{:S(2)}, u32[]{:S(2)}) collective-permute-start(bf16[108,16,128]{2,1,0:T(8,128)(2,1)S(1)} %get-tuple-element.18), channel_id=1, source_target_pairs={{0,96},{16,112},{32,0},{48,16},{64,32},{80,48},{96,64},{112,80},{1... | collective-permute-start | bytes 1327112 | tf_op jit(solution)/shard_map/ppermute | solution.py:34
  49.6 17.9 %collective-permute-start.8 = (bf16[216,16,128]{2,1,0:T(8,128)(2,1)}, bf16[216,16,128]{2,1,0:T(8,128)(2,1)S(1)}, u32[]{:S(2)}, u32[]{:S(2)}) collective-permute-start(bf16[216,16,128]{2,1,0:T(8,128)(2,1)} %pad_maximum_fusion), channel_id=1, source_target_pairs={{0,1},{1,0},{2,3},{3,2},{4,5},{5,4},{6,7},{7,6},{8,9},{9,8},{10,11... | collective-permute-start | bytes 2654216 | tf_op jit(solution)/shard_map/ppermute | solution.py:44
  49.6 13.8 %collective-permute-start.15 = (bf16[108,16,128]{2,1,0:T(8,128)(2,1)S(1)}, bf16[108,16,128]{2,1,0:T(8,128)(2,1)S(1)}, u32[]{:S(2)}, u32[]{:S(2)}) collective-permute-start(bf16[108,16,128]{2,1,0:T(8,128)(2,1)S(1)} %get-tuple-element.19), channel_id=1, source_target_pairs={{0,32},{16,48},{32,64},{48,80},{64,96},{80,112},{96,0},{112,16},{1... | collective-permute-start | bytes 1327112 | tf_op jit(solution)/shard_map/ppermute | solution.py:34
  51.9 15.6 %copy-start.4 = (bf16[108,16,128]{2,1,0:T(8,128)(2,1)}, bf16[108,16,128]{2,1,0:T(8,128)(2,1)S(1)}, u32[]{:S(2)}) copy-start(bf16[108,16,128]{2,1,0:T(8,128)(2,1)S(1)} %collective-permute-done.4.refs_5_.refs_13_.refs_16_) | copy-start | bytes 1327108
  51.9 6.4 %collective-permute-start.6 = (bf16[36,16,128]{2,1,0:T(8,128)(2,1)S(1)}, bf16[36,16,128]{2,1,0:T(8,128)(2,1)S(1)}, u32[]{:S(2)}, u32[]{:S(2)}) collective-permute-start(bf16[36,16,128]{2,1,0:T(8,128)(2,1)S(1)} %slice.59), channel_id=1, source_target_pairs={{0,12},{1,13},{2,14},{3,15},{4,0},{5,1},{6,2},{7,3},{8,4},{9,5},{1... | collective-permute-start | bytes 442376 | tf_op jit(solution)/shard_map/ppermute | solution.py:44
  55.7 11.9 %copy-start.5 = (bf16[108,16,128]{2,1,0:T(8,128)(2,1)}, bf16[108,16,128]{2,1,0:T(8,128)(2,1)S(1)}, u32[]{:S(2)}) copy-start(bf16[108,16,128]{2,1,0:T(8,128)(2,1)S(1)} %collective-permute-done.3.refs_4_.refs_12_.refs_15_) | copy-start | bytes 1327108
  55.7 6.4 %collective-permute-start.5 = (bf16[36,16,128]{2,1,0:T(8,128)(2,1)S(1)}, bf16[36,16,128]{2,1,0:T(8,128)(2,1)S(1)}, u32[]{:S(2)}, u32[]{:S(2)}) collective-permute-start(bf16[36,16,128]{2,1,0:T(8,128)(2,1)S(1)} %slice.58), channel_id=1, source_target_pairs={{0,4},{1,5},{2,6},{3,7},{4,8},{5,9},{6,10},{7,11},{8,12},{9,13},{1... | collective-permute-start | bytes 442376 | tf_op jit(solution)/shard_map/ppermute | solution.py:44
  56.7 9.1 %copy-start.24 = (bf16[108,16,128]{2,1,0:T(8,128)(2,1)}, bf16[108,16,128]{2,1,0:T(8,128)(2,1)S(1)}, u32[]{:S(2)}) copy-start(bf16[108,16,128]{2,1,0:T(8,128)(2,1)S(1)} %collective-permute-done.16.refs_5_) | copy-start | bytes 1327108
  56.7 9.1 %collective-permute-start.10 = (bf16[108,16,128]{2,1,0:T(8,128)(2,1)S(1)}, bf16[108,16,128]{2,1,0:T(8,128)(2,1)S(1)}, u32[]{:S(2)}, u32[]{:S(2)}) collective-permute-start(bf16[108,16,128]{2,1,0:T(8,128)(2,1)S(1)} %collective-permute-done.4.refs_5_.refs_13_.refs_16_), channel_id=1, source_target_pairs={{0,1},{1,0},{2,3},{3,2},{4,5},{5,4},{6,7},{7,6},{8,9},{9,8},{10,11... | collective-permute-start | bytes 1327112 | tf_op jit(solution)/shard_map/ppermute | solution.py:44
  58.4 9.2 %copy-start.14 = (bf16[36,16,128]{2,1,0:T(8,128)(2,1)}, bf16[36,16,128]{2,1,0:T(8,128)(2,1)S(1)}, u32[]{:S(2)}) copy-start(bf16[36,16,128]{2,1,0:T(8,128)(2,1)S(1)} %collective-permute-done.6.refs_7_.refs_15_.refs_18_) | copy-start | bytes 442372
  58.4 9.1 %collective-permute-start.9 = (bf16[108,16,128]{2,1,0:T(8,128)(2,1)S(1)}, bf16[108,16,128]{2,1,0:T(8,128)(2,1)S(1)}, u32[]{:S(2)}, u32[]{:S(2)}) collective-permute-start(bf16[108,16,128]{2,1,0:T(8,128)(2,1)S(1)} %collective-permute-done.3.refs_4_.refs_12_.refs_15_), channel_id=1, source_target_pairs={{0,1},{1,0},{2,3},{3,2},{4,5},{5,4},{6,7},{7,6},{8,9},{9,8},{10,11... | collective-permute-start | bytes 1327112 | tf_op jit(solution)/shard_map/ppermute | solution.py:44
  62.1 5.4 %copy-start.15 = (bf16[36,16,128]{2,1,0:T(8,128)(2,1)}, bf16[36,16,128]{2,1,0:T(8,128)(2,1)S(1)}, u32[]{:S(2)}) copy-start(bf16[36,16,128]{2,1,0:T(8,128)(2,1)S(1)} %collective-permute-done.5.refs_6_.refs_14_.refs_17_) | copy-start | bytes 442372
  62.1 2.7 %collective-permute-start.7 = (bf16[72,16,128]{2,1,0:T(8,128)(2,1)S(1)}, bf16[72,16,128]{2,1,0:T(8,128)(2,1)S(1)}, u32[]{:S(2)}, u32[]{:S(2)}) collective-permute-start(bf16[72,16,128]{2,1,0:T(8,128)(2,1)S(1)} %copy-done.6), channel_id=1, source_target_pairs={{0,1},{1,0},{2,3},{3,2},{4,5},{5,4},{6,7},{7,6},{8,9},{9,8},{10,11... | collective-permute-start | bytes 884744 | tf_op jit(solution)/shard_map/ppermute | solution.py:44
  63.4 3.5 %copy-start.25 = (bf16[108,16,128]{2,1,0:T(8,128)(2,1)}, bf16[108,16,128]{2,1,0:T(8,128)(2,1)S(1)}, u32[]{:S(2)}) copy-start(bf16[108,16,128]{2,1,0:T(8,128)(2,1)S(1)} %collective-permute-done.15.refs_4_) | copy-start | bytes 1327108
  63.4 4.1 %collective-permute-start.11 = (bf16[72,16,128]{2,1,0:T(8,128)(2,1)}, bf16[72,16,128]{2,1,0:T(8,128)(2,1)S(1)}, u32[]{:S(2)}, u32[]{:S(2)}) collective-permute-start(bf16[72,16,128]{2,1,0:T(8,128)(2,1)} %pad_maximum_fusion.6), channel_id=1, source_target_pairs={{0,1},{1,0},{2,3},{3,2},{4,5},{5,4},{6,7},{7,6},{8,9},{9,8},{10,11... | collective-permute-start | bytes 884744 | tf_op jit(solution)/shard_map/ppermute | solution.py:44
  64.8 2.8 %copy-start.12 = (bf16[72,16,128]{2,1,0:T(8,128)(2,1)}, bf16[72,16,128]{2,1,0:T(8,128)(2,1)S(1)}, u32[]{:S(2)}) copy-start(bf16[72,16,128]{2,1,0:T(8,128)(2,1)S(1)} %collective-permute-done.7.refs_8_.refs_16_.refs_19_) | copy-start | bytes 884740
  64.8 6.7 %collective-permute-start.18 = (bf16[36,16,128]{2,1,0:T(8,128)(2,1)}, bf16[36,16,128]{2,1,0:T(8,128)(2,1)}, u32[]{:S(2)}, u32[]{:S(2)}) collective-permute-start(bf16[36,16,128]{2,1,0:T(8,128)(2,1)} %slice.63), channel_id=1, source_target_pairs={{0,96},{16,112},{32,0},{48,16},{64,32},{80,48},{96,64},{112,80},{1... | collective-permute-start | bytes 442376 | tf_op jit(solution)/shard_map/ppermute | solution.py:34
  65.8 1.8 %copy-start.7 = (bf16[108,16,128]{2,1,0:T(8,128)(2,1)}, bf16[108,16,128]{2,1,0:T(8,128)(2,1)S(1)}, u32[]{:S(2)}) copy-start(bf16[108,16,128]{2,1,0:T(8,128)(2,1)S(1)} %collective-permute-done.10.refs_11_.refs_19_.refs_22_) | copy-start | bytes 1327108
  65.8 7.1 %collective-permute-start.17 = (bf16[36,16,128]{2,1,0:T(8,128)(2,1)}, bf16[36,16,128]{2,1,0:T(8,128)(2,1)}, u32[]{:S(2)}, u32[]{:S(2)}) collective-permute-start(bf16[36,16,128]{2,1,0:T(8,128)(2,1)} %slice.62), channel_id=1, source_target_pairs={{0,32},{16,48},{32,64},{48,80},{64,96},{80,112},{96,0},{112,16},{1... | collective-permute-start | bytes 442376 | tf_op jit(solution)/shard_map/ppermute | solution.py:34
  67.5 0.7 copy-start.13
  67.5 0.9 copy-start.8
  67.5 1.1 copy-start
  79.8 10.6 %collective-permute-start.21 = (bf16[100,16,128]{2,1,0:T(8,128)(2,1)}, bf16[100,16,128]{2,1,0:T(8,128)(2,1)S(1)}, u32[]{:S(2)}, u32[]{:S(2)}) collective-permute-start(bf16[100,16,128]{2,1,0:T(8,128)(2,1)} %shard_map.62.refs_0_), channel_id=1, source_target_pairs={{0,96},{16,112},{32,0},{48,16},{64,32},{80,48},{96,64},{112,80},{1... | collective-permute-start | bytes 1228808 | tf_op jit(solution)/shard_map/ppermute | solution.py:34
  80.7 12.0 %collective-permute-start.20 = (bf16[100,16,128]{2,1,0:T(8,128)(2,1)}, bf16[100,16,128]{2,1,0:T(8,128)(2,1)S(1)}, u32[]{:S(2)}, u32[]{:S(2)}) collective-permute-start(bf16[100,16,128]{2,1,0:T(8,128)(2,1)} %shard_map.62.refs_0_), channel_id=1, source_target_pairs={{0,32},{16,48},{32,64},{48,80},{64,96},{80,112},{96,0},{112,16},{1... | collective-permute-start | bytes 1228808 | tf_op jit(solution)/shard_map/ppermute | solution.py:34
  81.9 12.6 %collective-permute-start.19 = (bf16[100,16,128]{2,1,0:T(8,128)(2,1)}, bf16[100,16,128]{2,1,0:T(8,128)(2,1)S(1)}, u32[]{:S(2)}, u32[]{:S(2)}) collective-permute-start(bf16[100,16,128]{2,1,0:T(8,128)(2,1)} %shard_map.62.refs_0_), channel_id=1, source_target_pairs={{0,16},{16,0},{32,48},{48,32},{64,80},{80,64},{96,112},{112,96},{1... | collective-permute-start | bytes 1228808 | tf_op jit(solution)/shard_map/ppermute | solution.py:34
  90.3 2.4 %copy-start.9 = (bf16[100,16,128]{2,1,0:T(8,128)(2,1)}, bf16[100,16,128]{2,1,0:T(8,128)(2,1)S(1)}, u32[]{:S(2)}) copy-start(bf16[100,16,128]{2,1,0:T(8,128)(2,1)S(1)} %collective-permute-done.21.refs_3_) | copy-start | bytes 1228804
  92.7 1.8 %copy-start.10 = (bf16[100,16,128]{2,1,0:T(8,128)(2,1)}, bf16[100,16,128]{2,1,0:T(8,128)(2,1)S(1)}, u32[]{:S(2)}) copy-start(bf16[100,16,128]{2,1,0:T(8,128)(2,1)S(1)} %collective-permute-done.20.refs_2_) | copy-start | bytes 1228804
  92.8 15.8 %collective-permute-start.26 = (bf16[100,16,128]{2,1,0:T(8,128)(2,1)S(1)}, bf16[100,16,128]{2,1,0:T(8,128)(2,1)S(1)}, u32[]{:S(2)}, u32[]{:S(2)}) collective-permute-start(bf16[100,16,128]{2,1,0:T(8,128)(2,1)S(1)} %pad_maximum_fusion.5), channel_id=1, source_target_pairs={{0,16},{16,0},{32,48},{48,32},{64,80},{80,64},{96,112},{112,96},{1... | collective-permute-start | bytes 1228808 | tf_op jit(solution)/shard_map/ppermute | solution.py:34
  94.5 16.9 %copy-start.11 = (bf16[100,16,128]{2,1,0:T(8,128)(2,1)}, bf16[100,16,128]{2,1,0:T(8,128)(2,1)S(1)}, u32[]{:S(2)}) copy-start(bf16[100,16,128]{2,1,0:T(8,128)(2,1)S(1)} %collective-permute-done.19.refs_1_) | copy-start | bytes 1228804
  94.5 8.1 %collective-permute-start.24 = (bf16[50,16,128]{2,1,0:T(8,128)(2,1)S(1)}, bf16[50,16,128]{2,1,0:T(8,128)(2,1)S(1)}, u32[]{:S(2)}, u32[]{:S(2)}) collective-permute-start(bf16[50,16,128]{2,1,0:T(8,128)(2,1)S(1)} %get-tuple-element.16), channel_id=1, source_target_pairs={{0,96},{16,112},{32,0},{48,16},{64,32},{80,48},{96,64},{112,80},{1... | collective-permute-start | bytes 614408 | tf_op jit(solution)/shard_map/ppermute | solution.py:34
  95.3 9.2 %collective-permute-start.22 = (bf16[50,16,128]{2,1,0:T(8,128)(2,1)S(1)}, bf16[50,16,128]{2,1,0:T(8,128)(2,1)S(1)}, u32[]{:S(2)}, u32[]{:S(2)}) collective-permute-start(bf16[50,16,128]{2,1,0:T(8,128)(2,1)S(1)} %get-tuple-element.17), channel_id=1, source_target_pairs={{0,32},{16,48},{32,64},{48,80},{64,96},{80,112},{96,0},{112,16},{1... | collective-permute-start | bytes 614408 | tf_op jit(solution)/shard_map/ppermute | solution.py:34
  96.6 9.6 %collective-permute-start.25 = (bf16[50,16,128]{2,1,0:T(8,128)(2,1)S(1)}, bf16[50,16,128]{2,1,0:T(8,128)(2,1)S(1)}, u32[]{:S(2)}, u32[]{:S(2)}) collective-permute-start(bf16[50,16,128]{2,1,0:T(8,128)(2,1)S(1)} %get-tuple-element.13), channel_id=1, source_target_pairs={{0,96},{16,112},{32,0},{48,16},{64,32},{80,48},{96,64},{112,80},{1... | collective-permute-start | bytes 614408 | tf_op jit(solution)/shard_map/ppermute | solution.py:34
  98.5 10.1 %collective-permute-start.23 = (bf16[50,16,128]{2,1,0:T(8,128)(2,1)S(1)}, bf16[50,16,128]{2,1,0:T(8,128)(2,1)S(1)}, u32[]{:S(2)}, u32[]{:S(2)}) collective-permute-start(bf16[50,16,128]{2,1,0:T(8,128)(2,1)S(1)} %get-tuple-element.15), channel_id=1, source_target_pairs={{0,32},{16,48},{32,64},{48,80},{64,96},{80,112},{96,0},{112,16},{1... | collective-permute-start | bytes 614408 | tf_op jit(solution)/shard_map/ppermute | solution.py:34
  102.6 8.8 %copy-start.18 = (bf16[50,16,128]{2,1,0:T(8,128)(2,1)}, bf16[50,16,128]{2,1,0:T(8,128)(2,1)S(1)}, u32[]{:S(2)}) copy-start(bf16[50,16,128]{2,1,0:T(8,128)(2,1)S(1)} %collective-permute-done.24.refs_6_) | copy-start | bytes 614404
  102.6 6.0 %collective-permute-start.28 = (bf16[50,16,128]{2,1,0:T(8,128)(2,1)S(1)}, bf16[50,16,128]{2,1,0:T(8,128)(2,1)S(1)}, u32[]{:S(2)}, u32[]{:S(2)}) collective-permute-start(bf16[50,16,128]{2,1,0:T(8,128)(2,1)S(1)} %collective-permute-done.24.refs_6_), channel_id=1, source_target_pairs={{0,96},{16,112},{32,0},{48,16},{64,32},{80,48},{96,64},{112,80},{1... | collective-permute-start | bytes 614408 | tf_op jit(solution)/shard_map/ppermute | solution.py:34
  104.5 7.0 %copy-start.19 = (bf16[50,16,128]{2,1,0:T(8,128)(2,1)}, bf16[50,16,128]{2,1,0:T(8,128)(2,1)S(1)}, u32[]{:S(2)}) copy-start(bf16[50,16,128]{2,1,0:T(8,128)(2,1)S(1)} %collective-permute-done.22.refs_4_) | copy-start | bytes 614404
  104.5 7.0 %collective-permute-start.27 = (bf16[50,16,128]{2,1,0:T(8,128)(2,1)S(1)}, bf16[50,16,128]{2,1,0:T(8,128)(2,1)S(1)}, u32[]{:S(2)}, u32[]{:S(2)}) collective-permute-start(bf16[50,16,128]{2,1,0:T(8,128)(2,1)S(1)} %collective-permute-done.22.refs_4_), channel_id=1, source_target_pairs={{0,32},{16,48},{32,64},{48,80},{64,96},{80,112},{96,0},{112,16},{1... | collective-permute-start | bytes 614408 | tf_op jit(solution)/shard_map/ppermute | solution.py:34
  106.2 5.3 %copy-start.20 = (bf16[50,16,128]{2,1,0:T(8,128)(2,1)}, bf16[50,16,128]{2,1,0:T(8,128)(2,1)S(1)}, u32[]{:S(2)}) copy-start(bf16[50,16,128]{2,1,0:T(8,128)(2,1)S(1)} %collective-permute-done.25.refs_7_) | copy-start | bytes 614404
  108.6 2.9 %copy-start.21 = (bf16[50,16,128]{2,1,0:T(8,128)(2,1)}, bf16[50,16,128]{2,1,0:T(8,128)(2,1)S(1)}, u32[]{:S(2)}) copy-start(bf16[50,16,128]{2,1,0:T(8,128)(2,1)S(1)} %collective-permute-done.23.refs_5_) | copy-start | bytes 614404
  108.6 2.9 %copy-start.16 = (bf16[100,16,128]{2,1,0:T(8,128)(2,1)}, bf16[100,16,128]{2,1,0:T(8,128)(2,1)S(1)}, u32[]{:S(2)}) copy-start(bf16[100,16,128]{2,1,0:T(8,128)(2,1)S(1)} %collective-permute-done.26.refs_8_) | copy-start | bytes 1228804
  108.6 2.9 %copy-start.22 = (bf16[50,16,128]{2,1,0:T(8,128)(2,1)}, bf16[50,16,128]{2,1,0:T(8,128)(2,1)S(1)}, u32[]{:S(2)}) copy-start(bf16[50,16,128]{2,1,0:T(8,128)(2,1)S(1)} %collective-permute-done.28.refs_10_) | copy-start | bytes 614404
  111.4 0.7 copy-start.23
  120.3 16.6 %all-to-all-start.1 = ((bf16[64,16,512]{2,1,0:T(8,128)(2,1)}), bf16[64,16,512]{2,1,0:T(8,128)(2,1)S(1)}, u32[]{:S(2)}, u32[]{:S(2)}) async-start(bf16[64,16,512]{2,1,0:T(8,128)(2,1)} %shard_map.64), calls=%async_computation.1 | async-start | bytes 2097152 | tf_op jit(solution)/shard_map/all_to_all | solution.py:470
